TPU v7x, 256 devices: a whole 4x4x8 slice. The times are simulated.
256 devices in a mesh: dp: 8 (over z), expert: 32 (over x, y, core).
Axes of the slice: x: 4, y: 4, z: 8, core: 2. Of those that a mesh axis runs over, the one named last changes fastest.
Arguments:
- queries: bfloat16 [256, 2560], replicated, may hold values from -8 to 8
- patch_keys: bfloat16 [131072, 2560], P(('dp', 'expert')), may hold values from -160 to 160
- patch_values: bfloat16 [131072, 2560], P(('dp', 'expert')), may hold values from -6 to 6
- norm_gain: float32 [2560], replicated, may hold values from 0.25 to 1.75
- gate_weight: bfloat16 [32, 2560, 832], P('expert', 'dp'), may hold values from -0.125 to 0.125
- up_weight: bfloat16 [32, 2560, 832], P('expert', 'dp'), may hold values from -0.125 to 0.125
- down_weight: bfloat16 [32, 832, 2560], P('expert', None, 'dp'), may hold values from -0.21875 to 0.21875
- expert_ids: int32 [32768, 6], P(('dp', 'expert')), may hold values from 0 to 31, all different within a row; in each aligned block of 128 rows (0 to 127, 128 to 255, ...) at most 28 rows name the same one
- combine_weights: float32 [32768, 6], P(('dp', 'expert')), may hold values from 0.1 to 1
- latent_grad: bfloat16 [32768, 2560], P(('dp', 'expert')), may hold values from -6 to 6
Outputs:
- layer_out: bfloat16 [32768, 2560], P(('dp', 'expert'))
- query_grad: float32 [256, 2560], replicated
Inputs may be any that keep to these rules, and one draw needn't show every extreme that they name: `expert_ids`: in the 128 rows of one device no expert is named more than 28 times, a bound that some block reaches.
All inputs are finite; a program needn't handle non-finite values.
Results may differ from a plain program's by a relative error of at most 0.024.
The roundings to bfloat16 on the way count: a program that leaves them out, or rounds other values in their place, can miss the bound.
Values may be sent and summed in bfloat16 or wider, within the bound.
No kernel may reach another device: no remote copies, remote signals or barrier semaphores. Data moves between devices by JAX's collectives and lax.ppermute only.
A program may use at most 128 MiB of HBM per device.

v0:
```python
import math

import jax
import jax.numpy as jnp
from jax import lax
from jax.sharding import PartitionSpec as P

HEADS = 20
HEAD_DIM = 128
TOP = 6


EPSILON = 1e-06


def swapped(value, axis, bit):
    mask = 2**bit
    pairs = [(source, source ^ mask) for source in range(lax.axis_size(axis))]
    return lax.ppermute(value, axis, pairs)


def per_device(
    queries,
    patch_keys,
    patch_values,
    norm_gain,
    gate_weight,
    up_weight,
    down_weight,
    expert_ids,
    combine_weights,
    latent_grad,
):
    score_scale = 1.0 / math.sqrt(HEAD_DIM)
    query_count = queries.shape[0]
    model_width = queries.shape[1]
    own_rows = latent_grad.shape[0]
    parity = lax.axis_index("expert") % 2
    head_queries = queries.reshape(query_count, HEADS, HEAD_DIM)
    local_keys = patch_keys.reshape(-1, HEADS, HEAD_DIM)
    local_values = patch_values.reshape(-1, HEADS, HEAD_DIM)
    cotangent = latent_grad.reshape(own_rows, HEADS, HEAD_DIM)
    full_weights = (
        lax.all_gather(gate_weight, "dp", axis=1, tiled=True),
        lax.all_gather(up_weight, "dp", axis=1, tiled=True),
        lax.all_gather(down_weight, "dp", axis=2, tiled=True),
    )
    gate_full, up_full, down_full = full_weights
    far_keys, far_values = swapped((patch_keys, patch_values), "expert", 0)
    keys_all = jnp.concatenate([local_keys, far_keys.reshape(-1, HEADS, HEAD_DIM)], axis=0)
    values_all = jnp.concatenate([local_values, far_values.reshape(-1, HEADS, HEAD_DIM)], axis=0)
    mine_queries = lax.dynamic_slice_in_dim(head_queries, parity * own_rows, own_rows, 0)
    scores = (
        jnp.einsum("qhd,khd->hqk", mine_queries, keys_all, preferred_element_type=jnp.float32)
        * score_scale
    )
    peak = jnp.max(scores, axis=2, keepdims=True)
    exponent = jnp.exp(scores - peak)
    softmax_weights = exponent / jnp.sum(exponent, axis=2, keepdims=True)
    attended = jnp.einsum(
        "hqk,khd->qhd",
        softmax_weights.astype(jnp.bfloat16),
        values_all,
        preferred_element_type=jnp.float32,
    )
    latent_heads = attended.astype(jnp.bfloat16)
    value_dot = jnp.einsum(
        "qhd,khd->hqk", cotangent, values_all, preferred_element_type=jnp.float32
    )
    inner_dot = jnp.einsum(
        "qhd,qhd->hq", cotangent, latent_heads, preferred_element_type=jnp.float32
    )
    score_grad = (softmax_weights * (value_dot - inner_dot[:, :, None]) * score_scale).astype(
        jnp.bfloat16
    )
    query_part = jnp.einsum(
        "hqk,khd->qhd", score_grad, keys_all, preferred_element_type=jnp.float32
    )
    empty_grad = jnp.zeros((query_count, HEADS, HEAD_DIM), jnp.float32)
    local_grad = lax.dynamic_update_slice_in_dim(empty_grad, query_part, parity * own_rows, 0)
    query_grad = lax.psum(local_grad.reshape(query_count, model_width), ("dp", "expert"))
    latents = latent_heads.reshape(own_rows, model_width)
    latents_wide = latents.astype(jnp.float32)
    factor = lax.rsqrt(jnp.mean(latents_wide * latents_wide, axis=1, keepdims=True) + EPSILON)
    normed = (latents_wide * factor * norm_gain).astype(jnp.bfloat16)
    expert_count = lax.axis_size("expert")
    capacity = max(2, own_rows * TOP * 7 // (expert_count * 6))
    flat_ids = expert_ids.reshape(-1)
    onehot = (flat_ids[:, None] == jnp.arange(expert_count, dtype=jnp.int32)[None, :]).astype(
        jnp.int32
    )
    slot_index = jnp.sum(
        (jnp.cumsum(onehot, axis=0, dtype=jnp.int32) - 1) * onehot, axis=1, dtype=jnp.int32
    )
    position = flat_ids * capacity + slot_index
    source_rows = jnp.arange(own_rows * TOP, dtype=jnp.int32) // TOP
    send_buffer = (
        jnp.zeros((expert_count * capacity, model_width), jnp.bfloat16)
        .at[position]
        .set(normed[source_rows])
    )
    send_buffer = send_buffer.reshape(expert_count, capacity, model_width)
    block = lax.all_to_all(send_buffer, "expert", split_axis=0, concat_axis=0, tiled=True)
    flat_rows = block.reshape(-1, model_width)
    gate_act = jnp.dot(flat_rows, gate_full[0], preferred_element_type=jnp.float32)
    up_act = jnp.dot(flat_rows, up_full[0], preferred_element_type=jnp.float32)
    hidden = (jax.nn.silu(gate_act) * up_act).astype(jnp.bfloat16)
    result = jnp.dot(hidden, down_full[0], preferred_element_type=jnp.float32).astype(jnp.bfloat16)
    came_back = lax.all_to_all(
        result.reshape(block.shape), "expert", split_axis=0, concat_axis=0, tiled=True
    )
    picked = came_back.reshape(expert_count * capacity, model_width)[position].reshape(
        own_rows, TOP, model_width
    )
    mixture = jnp.sum(combine_weights[:, :, None] * picked.astype(jnp.float32), axis=1)
    layer_out = (latents_wide + mixture).astype(jnp.bfloat16)
    return (layer_out, query_grad)


def solution(mesh):
    return jax.shard_map(
        per_device,
        mesh=mesh,
        in_specs=(
            P(),
            P(("dp", "expert"), None),
            P(("dp", "expert"), None),
            P(),
            P("expert", "dp", None),
            P("expert", "dp", None),
            P("expert", None, "dp"),
            P(("dp", "expert"), None),
            P(("dp", "expert"), None),
            P(("dp", "expert"), None),
        ),
        out_specs=(P(("dp", "expert"), None), P()),
        check_vma=False,
    )
```

profile of v0, /device:TPU:1, one launch (start us, length us, event | category | flops | bytes accessed | tf_op | source)
XLA Modules:
  0.0 580.4 jit_solution(3175552100791840105)
XLA Ops:
  9.5 4.4 copy.23
  13.9 3.2 collective-permute-start.1
  17.2 4.4 copy.19
  22.0 3.2 copy.25
  25.3 3.3 copy.21
  31.1 4.4 copy.26
  35.5 7.4 %fusion.22 = f32[20,128,1024]{2,1,0:T(8,128)} fusion(bf16[512,20,128]{2,0,1:T(8,128)(2,1)} %copy.26, bf16[512,20,128]{2,0,1:T(8,128)(2,1)S(1)} %copy.25, bf16[256,20,128]{0,2,1:T(8,128)(2,1)} %bitcast.66, s32[]{:T(128)S(6)} %select_n.45), kind=kOutput, calls=%fused_computation.29 | convolution fusion | flops 681574400 | bytes 16384004 | tf_op jit(solution)/shard_map/qhd,khd->hqk/dot_general | solution.py:54
  42.9 4.5 copy.20
  47.4 14.0 %fusion.59 = (f32[20,128]{1,0:T(8,128)S(1)}, f32[20,128,1024]{2,1,0:T(8,128)}) fusion(f32[20,128,1024]{2,1,0:T(8,128)} %fusion.22), kind=kOutput, calls=%fused_computation.71 | output fusion | flops 10486783 | bytes 20981760 | tf_op jit(solution)/shard_map/sub | solution.py:58
  61.4 13.7 %bitcast_convert_fusion = (f32[128,20,128]{0,2,1:T(8,128)}, bf16[20,128,128]{2,1,0:T(8,128)(2,1)S(1)}) fusion(f32[20,128]{1,0:T(8,128)S(1)} %get-tuple-element.4, f32[20,128,1024]{2,1,0:T(8,128)} %fusion.22, bf16[512,20,128]{0,2,1:T(8,128)(2,1)} %bitcast.69, bf16[512,20,128]{0,2,1:T(8,128)(2,1)S(1)} %bitcast.68), kind=kOutput, calls=%fused_computation.40 | convolution fusion | flops 695340544 | bytes 17704960 | tf_op jit(solution)/shard_map/hqk,khd->qhd/dot_general | solution.py:60
  77.3 37.6 %scatter_custom_fusion = bf16[896,2560]{1,0:T(8,128)(2,1)} fusion(s32[768]{0:T(1024)S(1)} %fusion.46, bf16[128,2560]{1,0:T(8,128)(2,1)S(1)} %multiply_convert_fusion.1, s32[1024]{0:T(1024)S(1)} %pad_clamp_fusion.1, bf16[]{:T(256)} %constant.52.clone.1), kind=kCustom, calls=%fused_computation.27 | custom fusion | bytes 4587522 | tf_op jit(solution)/shard_map/scatter | solution.py:100
  114.9 7.2 %reshape.153 = bf16[32,28,2560]{2,1,0:T(8,128)(2,1)} reshape(bf16[896,2560]{1,0:T(8,128)(2,1)} %scatter_custom_fusion) | data formatting | bytes 9175040 | tf_op jit(solution)/shard_map/reshape | solution.py:102
  122.1 67.7 %all_to_all.10 = bf16[32,28,2560]{2,1,0:T(8,128)(2,1)} all-to-all(bf16[32,28,2560]{2,1,0:T(8,128)(2,1)} %reshape.153), channel_id=1, replica_groups=mesh['dp'=8,'expert'=32] {'expert'}, dimensions={0} | all-to-all | bytes 9175040 | tf_op jit(solution)/shard_map/all_to_all | solution.py:103
  189.9 7.2 %reshape.154 = bf16[896,2560]{1,0:T(8,128)(2,1)} reshape(bf16[32,28,2560]{2,1,0:T(8,128)(2,1)} %all_to_all.10) | data formatting | bytes 9175040 | tf_op jit(solution)/shard_map/reshape | solution.py:104
  197.1 9.9 %fusion.14 = f32[896,832]{0,1:T(8,128)} fusion(bf16[896,2560]{1,0:T(8,128)(2,1)} %reshape.154, bf16[1,2560,832]{2,1,0:T(8,128)(2,1)} %all-gather.6.cloned.1.call-done), kind=kOutput, calls=%fused_computation.22 | convolution fusion | flops 3816816640 | bytes 11829248 | tf_op jit(solution)/shard_map/dot_general | solution.py:106
  207.0 17.9 %convolution_convert_fusion = bf16[896,2560]{1,0:T(8,128)(2,1)} fusion(bf16[1,832,2560]{1,2,0:T(8,128)(2,1)} %all-gather.8.cloned.1.call-done, f32[896,832]{0,1:T(8,128)} %fusion.14, bf16[896,2560]{1,0:T(8,128)(2,1)} %reshape.154, bf16[1,2560,832]{2,1,0:T(8,128)(2,1)} %all-gather.4.cloned.1.call-done), kind=kOutput, calls=%fused_computation.11 | convolution fusion | flops 7640399872 | bytes 20676608 | tf_op jit(solution)/shard_map/dot_general | solution.py:108
  224.9 7.2 %reshape.155 = bf16[32,28,2560]{2,1,0:T(8,128)(2,1)} reshape(bf16[896,2560]{1,0:T(8,128)(2,1)} %convolution_convert_fusion) | data formatting | bytes 9175040 | tf_op jit(solution)/shard_map/reshape | solution.py:110
  232.1 4.8 all-to-all-start.1
  239.3 10.0 %fusion.29 = f32[256,20,128]{0,2,1:T(8,128)} fusion(f32[256,20,128]{0,2,1:T(8,128)} %broadcast_in_dim.5, s32[]{:T(128)S(6)} %select_n.45, f32[20,128]{1,0:T(8,128)S(1)} %fusion.35, bf16[128,20,128]{0,2,1:T(8,128)(2,1)S(1)} %bitcast.72, f32[20,128,1024]{2,1,0:T(8,128)} %get-tuple-element.5, f32[20,128]{1,0:T(8,128)S(1)} %get-tuple-element.4, ...), kind=kOutput, calls=%fused_computation.33 | convolution fusion | flops 1376256000 | bytes 22958084 | tf_op jit(solution)/shard_map/hqk,khd->qhd/dot_general | solution.py:76
  249.5 285.1 %all-reduce.2.cloned.1.call-done = f32[256,2560]{0,1:T(8,128)} async-done(((f32[256,2560]{0,1:T(8,128)}), f32[256,2560]{0,1:T(8,128)}) %all-reduce.2.cloned.1.call-update) | async-done | bytes 2621456 | tf_op jit(solution)/shard_map/psum | solution.py:81
  537.8 7.2 %reshape.156 = bf16[896,2560]{1,0:T(8,128)(2,1)} reshape(bf16[32,28,2560]{2,1,0:T(8,128)(2,1)} %all-to-all-done.1) | data formatting | bytes 9175040 | tf_op jit(solution)/shard_map/reshape | solution.py:112
  545.0 11.2 %gather_fusion = bf16[768,2560]{1,0:T(8,128)(2,1)} fusion(bf16[896,2560]{1,0:T(8,128)(2,1)} %reshape.156, s32[1024]{0:T(1024)S(1)} %pad_clamp_fusion), kind=kCustom, calls=%fused_computation.1 | custom fusion | bytes 7867392 | tf_op jit(solution)/shard_map/gather | solution.py:112
  556.3 7.7 %reshape.160 = f32[128,6,2560]{2,1,0:T(8,128)} reshape(bf16[768,2560]{1,0:T(8,128)(2,1)} %gather_fusion) | data formatting | bytes 11796480 | tf_op jit(solution)/shard_map/convert_element_type | solution.py:115
  564.0 7.9 %multiply_reduce_fusion = f32[128,2560]{1,0:T(8,128)S(1)} fusion(f32[128,6,2560]{2,1,0:T(8,128)} %reshape.160, f32[128,6]{1,0:T(8,128)S(1)} %copy.27), kind=kLoop, calls=%fused_computation.7 | loop fusion | flops 3604480 | bytes 9178112 | tf_op jit(solution)/shard_map/reduce_sum | solution.py:115
  (52 shorter events, 13.3 us)
Async XLA Ops:
  8.0 189.1 %all-gather.6.cloned.1.call-start = ((), (), s32[]{:S(2)}) async-start(), calls=%async_computation.3 | async-start | bytes 5160960 | tf_op jit(solution)/shard_map/all_gather | solution.py:45
  8.7 198.2 %all-gather.4.cloned.1.call-start = ((), (), s32[]{:S(2)}) async-start(), calls=%async_computation.2 | async-start | bytes 5160960 | tf_op jit(solution)/shard_map/all_gather | solution.py:44
  9.5 12.1 %copy-start.3 = (s32[128,6]{0,1:T(8,128)S(1)}, s32[128,6]{0,1:T(8,128)}, u32[]{:S(2)}) copy-start(s32[128,6]{0,1:T(8,128)} %param.17) | copy-start | bytes 9220
  9.5 197.5 %all-gather.8.cloned.1.call-start = ((), (), s32[]{:S(2)}) async-start(), calls=%async_computation.4 | async-start | bytes 5160960 | tf_op jit(solution)/shard_map/all_gather | solution.py:46
  13.9 17.2 %collective-permute-start.1 = (bf16[512,2560]{0,1:T(8,128)(2,1)}, bf16[512,2560]{0,1:T(8,128)(2,1)}, u32[]{:S(2)}, u32[]{:S(2)}) collective-permute-start(bf16[512,2560]{0,1:T(8,128)(2,1)} %copy.23), channel_id=1, source_target_pairs={{0,1},{1,0},{2,3},{3,2},{4,5},{5,4},{6,7},{7,6},{8,9},{9,8},{10,11... | collective-permute-start | bytes 7864328 | tf_op jit(solution)/shard_map/ppermute | solution.py:19
  17.2 25.7 %collective-permute-start = (bf16[512,2560]{1,0:T(8,128)(2,1)}, bf16[512,2560]{1,0:T(8,128)(2,1)}, u32[]{:S(2)}, u32[]{:S(2)}) collective-permute-start(bf16[512,2560]{1,0:T(8,128)(2,1)} %param.12), channel_id=1, source_target_pairs={{0,1},{1,0},{2,3},{3,2},{4,5},{5,4},{6,7},{7,6},{8,9},{9,8},{10,11... | collective-permute-start | bytes 7864328 | tf_op jit(solution)/shard_map/ppermute | solution.py:19
  25.2 17.7 %copy-start = (bf16[512,20,128]{2,0,1:T(8,128)(2,1)}, bf16[512,20,128]{2,0,1:T(8,128)(2,1)S(1)}, u32[]{:S(2)}) copy-start(bf16[512,20,128]{2,0,1:T(8,128)(2,1)S(1)} %copy.25) | copy-start | bytes 7864324
  47.4 14.0 %copy-start.1 = (bf16[512,2560]{0,1:T(8,128)(2,1)S(1)}, bf16[512,2560]{0,1:T(8,128)(2,1)}, u32[]{:S(2)}) copy-start(bf16[512,2560]{0,1:T(8,128)(2,1)} %copy.19) | copy-start | bytes 7864324
  61.4 15.8 %copy-start.4 = (f32[2560]{0:T(1024)S(1)}, f32[2560]{0:T(1024)}, u32[]{:S(2)}) copy-start(f32[2560]{0:T(1024)} %param.13) | copy-start | bytes 30724
  232.1 4.9 copy-start.2
  232.1 305.8 %all-to-all-start.1 = ((bf16[32,28,2560]{2,1,0:T(8,128)(2,1)}), bf16[32,28,2560]{2,1,0:T(8,128)(2,1)}, u32[]{:S(2)}, u32[]{:S(2)}) async-start(bf16[32,28,2560]{2,1,0:T(8,128)(2,1)} %reshape.155), calls=%async_computation.1 | async-start | bytes 10485760 | tf_op jit(solution)/shard_map/all_to_all | solution.py:109
  236.9 297.7 %all-reduce.2.cloned.1.call-start = ((), (), s32[]{:S(2)}) async-start(), calls=%async_computation.5 | async-start | bytes 5242880 | tf_op jit(solution)/shard_map/psum | solution.py:81
  239.3 10.1 %copy-start.5 = (f32[128,6]{0,1:T(8,128)S(1)}, f32[128,6]{0,1:T(8,128)}, u32[]{:S(2)}) copy-start(f32[128,6]{0,1:T(8,128)} %param.18) | copy-start | bytes 9220
Sparse Core Ops, SparseCore 0:
  10.6 62.2 all-gather.5
  74.7 57.0 all-gather.3
  133.7 57.0 all-gather.7
Sparse Core Ops, SparseCore 1:
  249.4 285.1 all-reduce.1
where the time goes:
time: 591 us; the launch traced here: 580 us
  waiting for transfers between devices  287 us (49%)
  local copies, waits for them, and re-layouts  118 us (20%)
  blocking collectives  67.7 us (11%)
  matrix products  59 us (10%)
  other arithmetic  25.6 us (4%)
  between operations  15.8 us (3%)
  starting transfers between devices  8.2 us (1%)
    psum x1, waiting for transfers between devices, per_device(): lax.psum(local_grad.reshape(query_count, model_width), ('dp', 'expert'))  285 us
    all_to_all x1, blocking collectives, per_device(): lax.all_to_all(send_buffer, 'expert', split_axis=0, concat_axis=0, tiled=...  67.7 us
    scatter x1, local copies, waits for them, and re-layouts, per_device(): send_buffer = jnp.zeros((expert_count * capacity, model_width), jnp.bfloa...  37.6 us
    dot_general x1, matrix products, per_device(): jnp.dot(hidden, down_full[0], preferred_element_type=jnp.float32)  17.9 us
    unnamed x19, local copies, waits for them, and re-layouts  15.9 us
    sub x1, other arithmetic, per_device(): exponent = jnp.exp(scores - peak)  14 us
    dot_general x1, matrix products, per_device(): jnp.einsum('hqk,khd->qhd', softmax_weights.astype(jnp.bfloat16), values_a...  13.7 us
  transfers between devices with their start and end apart: 7, of which 1 were waited for; matrix products, arithmetic and copies ran while one was open for 24% of the time, Pallas kernels for 0%

commit v1 on v0

v1 whole, which is shorter than its diff:
```python
import functools
import math

import jax
import jax.numpy as jnp
from jax import lax
from jax.experimental import pallas as pl
from jax.experimental.pallas import tpu as pltpu
from jax.sharding import PartitionSpec as P

HEADS = 20
HEAD_DIM = 128
WIDTH = HEADS * HEAD_DIM
ROWS = 128
PATCHES = 512
TOP = 6
EXPERTS = 32
HID = 832
CAPACITY = 28
N_DP = 8
SHARD = WIDTH // N_DP
PARTS = 4
PART = WIDTH // PARTS
BLOCK = PARTS * CAPACITY
GROUP = 4
GROUP_ROWS = GROUP * BLOCK
GROUP_SLOTS = GROUP * CAPACITY
GROUPS = EXPERTS // GROUP
SLOTS = EXPERTS * CAPACITY
EPSILON = 1e-06
SCALE = 1.0 / math.sqrt(HEAD_DIM)
HEADS_PER_STEP = 2
VMEM_LIMIT = 56 * 1024 * 1024

F32 = jnp.float32
BF16 = jnp.bfloat16


def dot(a, b):
    return jnp.dot(a, b, preferred_element_type=F32)


def dot_t(a, b):
    return lax.dot_general(a, b, (((1,), (1,)), ((), ())), preferred_element_type=F32)


def iota(shape, axis):
    return lax.broadcasted_iota(jnp.int32, shape, axis)


def over_28(value):
    return (value * 1171) >> 15


def over_112(value):
    return (value * 1171) >> 17


def head_weights(queries, near_keys, far_keys):
    near = dot_t(queries, near_keys) * SCALE
    far = dot_t(queries, far_keys) * SCALE
    peak = jnp.maximum(
        jnp.max(near, axis=1, keepdims=True), jnp.max(far, axis=1, keepdims=True)
    )
    near = jnp.exp(near - peak)
    far = jnp.exp(far - peak)
    total = jnp.sum(near, axis=1, keepdims=True) + jnp.sum(far, axis=1, keepdims=True)
    inverse = 1.0 / total
    return near * inverse, far * inverse


def forward_kernel(parity, queries, near_keys, far_keys, near_values, far_values, latents):
    for head in range(HEADS_PER_STEP):
        at = slice(head * HEAD_DIM, (head + 1) * HEAD_DIM)
        near, far = head_weights(queries[:, at], near_keys[:, at], far_keys[:, at])
        attended = dot(near.astype(BF16), near_values[:, at]) + dot(
            far.astype(BF16), far_values[:, at]
        )
        latents[:, at] = attended.astype(BF16)


def backward_kernel(
    parity, queries, near_keys, far_keys, near_values, far_values, latents, cotangent, grad
):
    for head in range(HEADS_PER_STEP):
        at = slice(head * HEAD_DIM, (head + 1) * HEAD_DIM)
        near, far = head_weights(queries[:, at], near_keys[:, at], far_keys[:, at])
        given = cotangent[:, at]
        inner = jnp.sum(
            given.astype(F32) * latents[:, at].astype(F32), axis=1, keepdims=True
        )
        near = near * (dot_t(given, near_values[:, at]) - inner) * SCALE
        far = far * (dot_t(given, far_values[:, at]) - inner) * SCALE
        grad[:, at] = dot(near.astype(BF16), near_keys[:, at]) + dot(
            far.astype(BF16), far_keys[:, at]
        )


def attention(kernel, out_type, flops, parity, queries, keys, far_keys, values, far_values, *more):
    wide = HEADS_PER_STEP * HEAD_DIM
    own = pl.BlockSpec((ROWS, wide), lambda i, parity: (0, i))
    patches = pl.BlockSpec((PATCHES, wide), lambda i, parity: (0, i))
    asked = pl.BlockSpec((ROWS, wide), lambda i, parity: (parity[0], i))
    return pl.pallas_call(
        kernel,
        out_shape=jax.ShapeDtypeStruct((ROWS, WIDTH), out_type),
        grid_spec=pltpu.PrefetchScalarGridSpec(
            num_scalar_prefetch=1,
            grid=(HEADS // HEADS_PER_STEP,),
            in_specs=[asked, patches, patches, patches, patches] + [own] * len(more),
            out_specs=own,
        ),
        compiler_params=pltpu.CompilerParams(vmem_limit_bytes=VMEM_LIMIT),
        cost_estimate=pl.CostEstimate(
            flops=flops, bytes_accessed=13_000_000, transcendentals=2_621_440
        ),
    )(parity, queries, keys, far_keys, values, far_values, *more)


def slot_table(ids):
    named = jnp.zeros((ROWS, EXPERTS), F32)
    for choice in range(TOP):
        named = named + (ids[:, choice : choice + 1] == iota((ROWS, EXPERTS), 1)).astype(F32)
    earlier = (iota((ROWS, ROWS), 0) > iota((ROWS, ROWS), 1)).astype(BF16)
    before = dot(earlier, named.astype(BF16))
    return jnp.where(named > 0, before, -1.0)


def dispatch_kernel(latents, gain, ids, out, stacked):
    wide = latents[...].astype(F32)
    factor = lax.rsqrt(jnp.mean(wide * wide, axis=1, keepdims=True) + EPSILON)
    normed = (wide * factor * gain[...]).astype(BF16)
    for part in range(PARTS):
        stacked[part * ROWS : (part + 1) * ROWS, :] = normed[:, part * PART : (part + 1) * PART]
    slots = slot_table(ids).astype(BF16)
    row = iota((GROUP_ROWS, 1), 0)
    expert_of = over_112(row)
    slot_of = row - over_28(row) * CAPACITY
    part_of = over_28(row) - expert_of * PARTS
    lane_part = iota((GROUP_ROWS, PARTS * ROWS), 1) >> 7
    right_part = lane_part == part_of

    def group(g, carry):
        pick = (iota((GROUP_ROWS, EXPERTS), 1) == expert_of + g * GROUP).astype(BF16)
        place = dot_t(pick, slots)
        match = jnp.concatenate([place] * PARTS, axis=1) == slot_of.astype(F32)
        chosen = jnp.where(match & right_part, 1.0, 0.0).astype(BF16)
        at = pl.multiple_of(g * GROUP_ROWS, GROUP_ROWS)
        out[pl.ds(at, GROUP_ROWS), :] = dot(chosen, stacked[...]).astype(BF16)
        return carry

    lax.fori_loop(0, GROUPS, group, 0)


def dispatch(latents, gain, ids):
    return pl.pallas_call(
        dispatch_kernel,
        out_shape=jax.ShapeDtypeStruct((EXPERTS * BLOCK, PART), BF16),
        scratch_shapes=[pltpu.VMEM((PARTS * ROWS, PART), BF16)],
        compiler_params=pltpu.CompilerParams(vmem_limit_bytes=VMEM_LIMIT),
        cost_estimate=pl.CostEstimate(
            flops=2_400_000_000, bytes_accessed=6_000_000, transcendentals=0
        ),
    )(latents, gain, ids)


def spread_rows():
    row = iota((GROUP_ROWS, GROUP_ROWS), 0)
    part = over_112(row)
    block = over_28(row) - part * GROUP
    slot = row - over_28(row) * CAPACITY
    target = block * BLOCK + part * CAPACITY + slot
    return (iota((GROUP_ROWS, GROUP_ROWS), 1) == target).astype(BF16)


def gathered_rows():
    row = iota((GROUP_ROWS, GROUP_ROWS), 0)
    block = over_112(row)
    part = over_28(row) - block * PARTS
    slot = row - over_28(row) * CAPACITY
    target = part * GROUP_SLOTS + block * CAPACITY + slot
    return (iota((GROUP_ROWS, GROUP_ROWS), 1) == target).astype(BF16)


def open_blocks(blocks, rows):
    order = spread_rows()

    def group(g, carry):
        at = pl.multiple_of(g * GROUP_ROWS, GROUP_ROWS)
        found = dot(order, blocks[pl.ds(at, GROUP_ROWS), :]).astype(BF16)
        to = pl.multiple_of(g * GROUP_SLOTS, GROUP_SLOTS)
        for part in range(PARTS):
            rows[pl.ds(to, GROUP_SLOTS), part * PART : (part + 1) * PART] = found[
                part * GROUP_SLOTS : (part + 1) * GROUP_SLOTS, :
            ]
        return carry

    lax.fori_loop(0, GROUPS, group, 0)


HALF = SLOTS // 2


def hidden_kernel(
    place, received, own, f1, f2, f3, b1, b2, b3, gate4, up4, hidden, gate_full, up_full, rows, sems
):
    copies = []

    def bring(source, target, shard):
        at = pl.multiple_of(lax.rem(shard + N_DP, N_DP) * SHARD, SHARD)
        copy = pltpu.make_async_copy(
            source, target.at[pl.ds(at, SHARD), :], sems.at[len(copies)]
        )
        copy.start()
        copies.append(copy)

    z = place[0]
    for source, shard in (
        (own, z), (f1, z - 1), (b1, z + 1), (f2, z - 2), (b2, z + 2), (f3, z - 3), (b3, z + 3),
    ):
        bring(source.at[pl.ds(0, SHARD), :], gate_full, shard)
        bring(source.at[pl.ds(SHARD, SHARD), :], up_full, shard)
    bring(gate4, gate_full, z + 4)
    bring(up4, up_full, z + 4)
    open_blocks(received, rows)
    for copy in copies:
        copy.wait()

    def half(h, carry):
        at = pl.multiple_of(h * HALF, HALF)
        taken = rows[pl.ds(at, HALF), :]
        gate = dot(taken, gate_full[...])
        up = dot(taken, up_full[...])
        hidden[pl.ds(at, HALF), :] = (gate / (1.0 + jnp.exp(-gate)) * up).astype(BF16)
        return carry

    lax.fori_loop(0, 2, half, 0)


def hidden_units(place, received, own, forth, back, gate4, up4):
    smem = pl.BlockSpec(memory_space=pltpu.SMEM)
    vmem = pl.BlockSpec(memory_space=pltpu.VMEM)
    hbm = pl.BlockSpec(memory_space=pl.ANY)
    return pl.pallas_call(
        hidden_kernel,
        out_shape=jax.ShapeDtypeStruct((SLOTS, HID), BF16),
        in_specs=[smem, vmem] + [hbm] * 9,
        out_specs=vmem,
        scratch_shapes=[
            pltpu.VMEM((WIDTH, HID), BF16),
            pltpu.VMEM((WIDTH, HID), BF16),
            pltpu.VMEM((SLOTS, WIDTH), BF16),
            pltpu.SemaphoreType.DMA((16,)),
        ],
        compiler_params=pltpu.CompilerParams(vmem_limit_bytes=VMEM_LIMIT),
        cost_estimate=pl.CostEstimate(
            flops=9_700_000_000, bytes_accessed=15_000_000, transcendentals=745_472
        ),
    )(place, received, own, *forth, *back, gate4, up4)


def result_kernel(place, hidden, own, f1, f2, f3, b1, b2, b3, low4, high4, out, full, rows, sems):
    copies = []

    def bring(source, shard, offset, count):
        at = pl.multiple_of(lax.rem(shard + N_DP, N_DP) * SHARD + offset, 32)
        copy = pltpu.make_async_copy(source, full.at[pl.ds(at, count), :], sems.at[len(copies)])
        copy.start()
        copies.append(copy)

    z = place[0]
    for source, shard in (
        (own, z), (f1, z - 1), (b1, z + 1), (f2, z - 2), (b2, z + 2), (f3, z - 3), (b3, z + 3),
    ):
        bring(source, shard, 0, SHARD)
    bring(low4, z + 4, 0, SHARD // 2)
    bring(high4, z + 4, SHARD // 2, SHARD // 2)
    for copy in copies:
        copy.wait()

    def half(h, carry):
        at = pl.multiple_of(h * HALF, HALF)
        rows[pl.ds(at, HALF), :] = dot_t(hidden[pl.ds(at, HALF), :], full[...]).astype(BF16)
        return carry

    lax.fori_loop(0, 2, half, 0)
    order = gathered_rows()

    def group(g, carry):
        at = pl.multiple_of(g * GROUP_SLOTS, GROUP_SLOTS)
        taken = jnp.concatenate(
            [
                rows[pl.ds(at, GROUP_SLOTS), part * PART : (part + 1) * PART]
                for part in range(PARTS)
            ],
            axis=0,
        )
        to = pl.multiple_of(g * GROUP_ROWS, GROUP_ROWS)
        out[pl.ds(to, GROUP_ROWS), :] = dot(order, taken).astype(BF16)
        return carry

    lax.fori_loop(0, GROUPS, group, 0)


def results(place, hidden, own, forth, back, low4, high4):
    smem = pl.BlockSpec(memory_space=pltpu.SMEM)
    vmem = pl.BlockSpec(memory_space=pltpu.VMEM)
    hbm = pl.BlockSpec(memory_space=pl.ANY)
    return pl.pallas_call(
        result_kernel,
        out_shape=jax.ShapeDtypeStruct((EXPERTS * BLOCK, PART), BF16),
        in_specs=[smem, vmem] + [hbm] * 9,
        out_specs=vmem,
        scratch_shapes=[
            pltpu.VMEM((WIDTH, HID), BF16),
            pltpu.VMEM((SLOTS, WIDTH), BF16),
            pltpu.SemaphoreType.DMA((9,)),
        ],
        compiler_params=pltpu.CompilerParams(vmem_limit_bytes=VMEM_LIMIT),
        cost_estimate=pl.CostEstimate(
            flops=5_900_000_000, bytes_accessed=11_000_000, transcendentals=0
        ),
    )(place, hidden, own, *forth, *back, low4, high4)


def combine_kernel(returned, latents, ids, weights, out, rows):
    open_blocks(returned, rows)
    slots = slot_table(ids)
    shares = jnp.zeros((ROWS, EXPERTS), F32)
    for choice in range(TOP):
        named = ids[:, choice : choice + 1] == iota((ROWS, EXPERTS), 1)
        shares = shares + jnp.where(named, weights[:, choice : choice + 1], 0.0)
    high = shares.astype(BF16)
    rest = shares - high.astype(F32)
    middle = rest.astype(BF16)
    low = (rest - middle.astype(F32)).astype(BF16)
    row = iota((EXPERTS, SLOTS), 1)
    pick = (over_28(row) == iota((EXPERTS, SLOTS), 0)).astype(BF16)
    lane = iota((ROWS, SLOTS), 1)
    slot_of = (lane - over_28(lane) * CAPACITY).astype(F32)
    match = dot(slots.astype(BF16), pick) == slot_of
    terms = [
        jnp.where(match, dot(term, pick), 0.0).astype(BF16) for term in (high, middle, low)
    ]
    stacked = jnp.concatenate(terms, axis=0)
    for part in range(PARTS):
        at = slice(part * PART, (part + 1) * PART)
        found = dot(stacked, rows[:, at])
        mixed = found[:ROWS] + (found[ROWS : 2 * ROWS] + found[2 * ROWS :])
        out[:, at] = (latents[:, at].astype(F32) + mixed).astype(BF16)


def combine(returned, latents, ids, weights):
    return pl.pallas_call(
        combine_kernel,
        out_shape=jax.ShapeDtypeStruct((ROWS, WIDTH), BF16),
        scratch_shapes=[pltpu.VMEM((SLOTS, WIDTH), BF16)],
        compiler_params=pltpu.CompilerParams(vmem_limit_bytes=VMEM_LIMIT),
        cost_estimate=pl.CostEstimate(
            flops=4_000_000_000, bytes_accessed=6_000_000, transcendentals=0
        ),
    )(returned, latents, ids, weights)


SAME_CORE = [list(range(core, EXPERTS, 2)) for core in range(2)]


def other_core(value):
    return lax.ppermute(value, "expert", [(at, at ^ 1) for at in range(EXPERTS)])


def along(value, step):
    return lax.ppermute(value, "dp", [(at, (at + step) % N_DP) for at in range(N_DP)])


def ring(own):
    forth, back = [], []
    ahead = behind = own
    for _ in range(3):
        ahead, behind = along(ahead, 1), along(behind, -1)
        forth.append(ahead)
        back.append(behind)
    middle = own.shape[0] // 2
    return forth, back, along(ahead[:middle], 1), along(behind[middle:], -1)


def summed(part):
    pieces = lax.all_to_all(
        part.reshape(EXPERTS // 2, -1, WIDTH),
        "expert",
        split_axis=0,
        concat_axis=0,
        tiled=True,
        axis_index_groups=SAME_CORE,
    )
    total = jnp.sum(pieces, axis=0)
    for bit in (1, 2, 4):
        total = total + lax.ppermute(total, "dp", [(at, at ^ bit) for at in range(N_DP)])
    half = lax.all_gather(total, "expert", axis=0, tiled=True, axis_index_groups=SAME_CORE)
    return half, other_core(half)


def per_device(
    queries,
    patch_keys,
    patch_values,
    norm_gain,
    gate_weight,
    up_weight,
    down_weight,
    expert_ids,
    combine_weights,
    latent_grad,
):
    parity = lax.axis_index("expert") % 2
    which = parity.reshape(1).astype(jnp.int32)
    place = lax.axis_index("dp").reshape(1).astype(jnp.int32)
    far_keys, far_values = other_core(patch_keys), other_core(patch_values)
    gate_up = jnp.concatenate([gate_weight[0], up_weight[0]], axis=0)
    down = down_weight[0].T
    both = ring(gate_up)
    downs = ring(down)
    patches = (which, queries, patch_keys, far_keys, patch_values, far_values)
    latents = attention(forward_kernel, BF16, 1_342_177_280, *patches)
    sent = dispatch(latents, norm_gain.reshape(1, WIDTH), expert_ids)
    received = lax.all_to_all(
        sent.reshape(EXPERTS, BLOCK, PART), "expert", split_axis=0, concat_axis=0, tiled=True
    ).reshape(EXPERTS * BLOCK, PART)
    grad_part = attention(
        backward_kernel, F32, 2_684_354_560, *patches, latents, latent_grad
    )
    hidden = hidden_units(place, received, gate_up, *both)
    result = results(place, hidden, down, *downs)
    returned = lax.all_to_all(
        result.reshape(EXPERTS, BLOCK, PART), "expert", split_axis=0, concat_axis=0, tiled=True
    ).reshape(EXPERTS * BLOCK, PART)
    half, far_half = summed(grad_part)
    first = jnp.where(parity == 0, half, far_half)
    second = jnp.where(parity == 0, far_half, half)
    query_grad = jnp.concatenate([first, second], axis=0)
    layer_out = combine(returned, latents, expert_ids, combine_weights)
    return (layer_out, query_grad)


def solution(mesh):
    return jax.shard_map(
        per_device,
        mesh=mesh,
        in_specs=(
            P(),
            P(("dp", "expert"), None),
            P(("dp", "expert"), None),
            P(),
            P("expert", "dp", None),
            P("expert", "dp", None),
            P("expert", None, "dp"),
            P(("dp", "expert"), None),
            P(("dp", "expert"), None),
            P(("dp", "expert"), None),
        ),
        out_specs=(P(("dp", "expert"), None), P()),
        check_vma=False,
    )
```

time: 591 us -> 360 us (0.61); the launches traced: 580 us -> 356 us
  waiting for transfers between devices: 287 us -> 165 us
  local copies, waits for them, and re-layouts: 118 us -> 23.8 us
  Pallas kernels: 0 us -> 81 us
  blocking collectives: 67.7 us -> 0 us
  matrix products: 59 us -> 0 us
  starting transfers between devices: 8.2 us -> 65.1 us
  other arithmetic: 25.6 us -> 6.58 us
    psum x1 -> x0, waiting for transfers between devices: 285 us -> none  [per_device(): lax.psum(local_grad.reshape(query_count, model_width), ('dp', 'expert'))]
    ppermute x2 -> x22, waiting for transfers between devices: 0.01 us -> 112 us  [the longest x16 85.2 us: along(): lax.ppermute(value, 'dp', [(at, (at + step) % N_DP) for at in range(N_DP)])]
    pallas_call x0 -> x6, Pallas kernels: none -> 81 us  [the longest x2 27.4 us: attention(): pl.pallas_call(kernel, out_shape=jax.ShapeDtypeStruct((ROWS, WIDTH), out_...]
    all_to_all x1 -> x0, blocking collectives: 67.7 us -> none  [per_device(): lax.all_to_all(send_buffer, 'expert', split_axis=0, concat_axis=0, tiled=...]
    dot_general x5 -> x0, matrix products: 59 us -> none  [the longest x1 17.9 us: per_device(): jnp.dot(hidden, down_full[0], preferred_element_type=jnp.float32)]
    all_to_all x1 -> x3, waiting for transfers between devices: 0.01 us -> 49.7 us  [the longest x1 42 us: per_device(): lax.all_to_all(result.reshape(EXPERTS, BLOCK, PART), 'expert', split_axis...]
    scatter x1 -> x0, local copies, waits for them, and re-layouts: 37.6 us -> none  [per_device(): send_buffer = jnp.zeros((expert_count * capacity, model_width), jnp.bfloa...]
    ppermute x2 -> x22, starting transfers between devices: 3.24 us -> 39.9 us  [the longest x16 24.7 us: along(): lax.ppermute(value, 'dp', [(at, (at + step) % N_DP) for at in range(N_DP)])]
  transfers between devices with their start and end apart: 7 -> 26, of which waited for: 1 -> 12; matrix products, arithmetic and copies ran while one was open for 24% -> 8% of each run, Pallas kernels for 0% -> 12%
where the time goes in v1:
time: 360 us; the launch traced here: 356 us
  waiting for transfers between devices  165 us (46%)
  Pallas kernels  81 us (22%)
  starting transfers between devices  65.1 us (18%)
  local copies, waits for them, and re-layouts  23.8 us (7%)
  between operations  14.3 us (4%)
  other arithmetic  6.58 us (2%)
    ppermute x16, waiting for transfers between devices, along(): lax.ppermute(value, 'dp', [(at, (at + step) % N_DP) for at in range(N_DP)])  85.2 us
    all_to_all x1, waiting for transfers between devices, per_device(): lax.all_to_all(result.reshape(EXPERTS, BLOCK, PART), 'expert', split_axis...  42 us
    pallas_call x2, Pallas kernels, attention(): pl.pallas_call(kernel, out_shape=jax.ShapeDtypeStruct((ROWS, WIDTH), out_...  27.4 us
    ppermute x16, starting transfers between devices, along(): lax.ppermute(value, 'dp', [(at, (at + step) % N_DP) for at in range(N_DP)])  24.7 us
    pallas_call x1, Pallas kernels, hidden_units(): pl.pallas_call(hidden_kernel, out_shape=jax.ShapeDtypeStruct((SLOTS, HID)...  18 us
    ppermute x3, waiting for transfers between devices, summed(): lax.ppermute(total, 'dp', [(at, at ^ bit) for at in range(N_DP)])  16.4 us
    pallas_call x1, Pallas kernels, results(): pl.pallas_call(result_kernel, out_shape=jax.ShapeDtypeStruct((EXPERTS * B...  15.5 us
    ppermute x6, local copies, waits for them, and re-layouts, along(): lax.ppermute(value, 'dp', [(at, (at + step) % N_DP) for at in range(N_DP)])  12.6 us
  transfers between devices with their start and end apart: 26, of which 12 were waited for; matrix products, arithmetic and copies ran while one was open for 8% of the time, Pallas kernels for 12%

profile of v1, /device:TPU:1, one launch (start us, length us, event | category | flops | bytes accessed | tf_op | source)
XLA Modules:
  0.0 355.7 jit_solution(190884470355580407)
XLA Ops:
  7.2 3.3 collective-permute-start
  10.6 7.4 %collective-permute-done.far_keys = bf16[512,2560]{1,0:T(8,128)(2,1)S(1)} collective-permute-done((bf16[512,2560]{1,0:T(8,128)(2,1)}, bf16[512,2560]{1,0:T(8,128)(2,1)S(1)}, u32[]{:S(2)}, u32[]{:S(2)}) %collective-permute-start) | collective-permute-done | bytes 2621472 | tf_op jit(solution)/shard_map/ppermute | solution.py:369
  19.5 13.4 %shard_map.113.latents = bf16[128,2560]{1,0:T(8,128)(2,1)} custom-call(s32[1]{0:T(128)} %bitcast.1.parity, bf16[256,2560]{1,0:T(8,128)(2,1)} %queries.3, bf16[512,2560]{1,0:T(8,128)(2,1)} %near_keys.3, bf16[512,2560]{1,0:T(8,128)(2,1)} %copy-done, bf16[512,2560]{1,0:T(8,128)(2,1)} %near_values.3, bf16[512,2560]{1,0:T(8,128)(2,1)} %collective-permute-done.1.far_values), custom_call_target="tpu_custom_call" | custom-call | flops 1342177280 | bytes 13000000 | tf_op jit(solution)/shard_map/pallas_call | solution.py:104
  32.9 14.0 %shard_map.118 = f32[128,2560]{1,0:T(8,128)} custom-call(s32[1]{0:T(128)} %bitcast.1.parity, bf16[256,2560]{1,0:T(8,128)(2,1)} %queries.3, bf16[512,2560]{1,0:T(8,128)(2,1)} %near_keys.3, bf16[512,2560]{1,0:T(8,128)(2,1)} %copy-done, bf16[512,2560]{1,0:T(8,128)(2,1)} %near_values.3, bf16[512,2560]{1,0:T(8,128)(2,1)} %collective-permute-done.1.far_values, ...), custom_call_target="tpu_custom_call" | custom-call | flops 2684354560 | bytes 13000000 | tf_op jit(solution)/shard_map/pallas_call | solution.py:104
  46.9 5.2 %all-to-all-start.2 = ((f32[16,8,2560]{2,1,0:T(8,128)}), f32[16,8,2560]{2,1,0:T(8,128)S(1)}, u32[]{:S(2)}, u32[]{:S(2)}) async-start(f32[16,8,2560]{2,1,0:T(8,128)} %bitcast.12), calls=%async_computation.2 | async-start | bytes 2621440 | tf_op jit(solution)/shard_map/all_to_all | solution.py:388
  53.4 9.2 %shard_map.114 = bf16[3584,640]{1,0:T(8,128)(2,1)} custom-call(bf16[128,2560]{1,0:T(8,128)(2,1)} %shard_map.113.latents, f32[1,2560]{1,0:T(1,128)} %reshape.30.gain, s32[128,6]{1,0:T(8,128)} %copy.15.ids), custom_call_target="tpu_custom_call" | custom-call | flops 2400000000 | bytes 6000000 | tf_op jit(solution)/shard_map/pallas_call | solution.py:156
  62.6 7.7 %all-to-all-done.2 = f32[16,8,2560]{2,1,0:T(8,128)S(1)} async-done(((f32[16,8,2560]{2,1,0:T(8,128)}), f32[16,8,2560]{2,1,0:T(8,128)S(1)}, u32[]{:S(2)}, u32[]{:S(2)}) %all-to-all-start.2) | async-done | bytes 1310752 | tf_op jit(solution)/shard_map/all_to_all | solution.py:388
  70.3 8.0 %all-to-all-start = ((bf16[32,112,640]{2,1,0:T(8,128)(2,1)}), bf16[32,112,640]{2,1,0:T(8,128)(2,1)}, u32[]{:S(2)}, u32[]{:S(2)}) async-start(bf16[32,112,640]{2,1,0:T(8,128)(2,1)} %bitcast.13), calls=%async_computation | async-start | bytes 9175040 | tf_op jit(solution)/shard_map/all_to_all | solution.py:426
  83.0 3.9 %collective-permute-start.5 = (bf16[640,832]{0,1:T(8,128)(2,1)}, bf16[640,832]{0,1:T(8,128)(2,1)S(1)}, u32[]{:S(2)}, u32[]{:S(2)}) collective-permute-start(bf16[640,832]{0,1:T(8,128)(2,1)} %copy.16), channel_id=1, source_target_pairs={{0,224},{32,0},{64,32},{96,64},{128,96},{160,128},{192,160},{224,1... | collective-permute-start | bytes 3194888 | tf_op jit(solution)/shard_map/ppermute | solution.py:373
  86.9 23.8 %collective-permute-done.2 = bf16[640,832]{0,1:T(8,128)(2,1)S(1)} collective-permute-done((bf16[640,832]{0,1:T(8,128)(2,1)}, bf16[640,832]{0,1:T(8,128)(2,1)S(1)}, u32[]{:S(2)}, u32[]{:S(2)}) %collective-permute-start.2) | collective-permute-done | bytes 1064992 | tf_op jit(solution)/shard_map/ppermute | solution.py:373
  113.4 2.7 collective-permute-start.13
  116.1 20.1 %collective-permute-done.3 = bf16[640,832]{0,1:T(8,128)(2,1)S(1)} collective-permute-done((bf16[640,832]{0,1:T(8,128)(2,1)S(1)}, bf16[640,832]{0,1:T(8,128)(2,1)S(1)}, u32[]{:S(2)}, u32[]{:S(2)}) %collective-permute-start.3) | collective-permute-done | bytes 1064992 | tf_op jit(solution)/shard_map/ppermute | solution.py:373
  138.8 9.6 %collective-permute-done.10.f1 = bf16[320,832]{1,0:T(8,128)(2,1)S(1)} collective-permute-done((bf16[320,832]{1,0:T(8,128)(2,1)}, bf16[320,832]{1,0:T(8,128)(2,1)S(1)}, u32[]{:S(2)}, u32[]{:S(2)}) %collective-permute-start.10) | collective-permute-done | bytes 532512 | tf_op jit(solution)/shard_map/ppermute | solution.py:373
  151.9 31.7 %collective-permute-done.11.f2 = bf16[320,832]{1,0:T(8,128)(2,1)} collective-permute-done((bf16[320,832]{1,0:T(8,128)(2,1)S(1)}, bf16[320,832]{1,0:T(8,128)(2,1)}, u32[]{:S(2)}, u32[]{:S(2)}) %collective-permute-start.11) | collective-permute-done | bytes 532512 | tf_op jit(solution)/shard_map/ppermute | solution.py:373
  197.0 13.8 %collective-permute-done.18 = f32[8,2560]{1,0:T(8,128)S(1)} collective-permute-done((f32[8,2560]{1,0:T(8,128)}, f32[8,2560]{1,0:T(8,128)S(1)}, u32[]{:S(2)}, u32[]{:S(2)}) %collective-permute-start.18) | collective-permute-done | bytes 81952 | tf_op jit(solution)/shard_map/ppermute | solution.py:398
  216.9 3.1 collective-permute-start.20
  226.1 3.0 collective-permute-start.17
  233.9 18.0 %shard_map.115.hidden = bf16[896,832]{1,0:T(8,128)(2,1)} custom-call(s32[1]{0:T(128)} %bitcast.place, bf16[3584,640]{1,0:T(8,128)(2,1)} %bitcast.3.received, bf16[640,832]{1,0:T(8,128)(2,1)} %copy-done.1, bf16[640,832]{1,0:T(8,128)(2,1)} %copy.20.f1, bf16[640,832]{1,0:T(8,128)(2,1)} %copy.21.f2, bf16[640,832]{1,0:T(8,128)(2,1)} %copy.22.f3, ...), custom_call_target="tpu_custom_call" | custom-call | flops 9699999744 | bytes 15000000 | tf_op jit(solution)/shard_map/pallas_call | solution.py:244
  253.3 15.5 %shard_map.116 = bf16[3584,640]{1,0:T(8,128)(2,1)} custom-call(s32[1]{0:T(128)} %bitcast.place, bf16[896,832]{1,0:T(8,128)(2,1)} %shard_map.115.hidden, bf16[320,832]{1,0:T(8,128)(2,1)} %bitcast.19, bf16[320,832]{1,0:T(8,128)(2,1)} %copy-done.10, bf16[320,832]{1,0:T(8,128)(2,1)} %collective-permute-done.11.f2, bf16[320,832]{1,0:T(8,128)(2,1)} %collective-permute-done.12.f3, ...), custom_call_target="tpu_custom_call" | custom-call | flops 5900000256 | bytes 11000000 | tf_op jit(solution)/shard_map/pallas_call | solution.py:309
  268.8 11.9 %all-to-all-start.1 = ((bf16[32,112,640]{2,1,0:T(8,128)(2,1)}), bf16[32,112,640]{2,1,0:T(8,128)(2,1)}, u32[]{:S(2)}, u32[]{:S(2)}) async-start(bf16[32,112,640]{2,1,0:T(8,128)(2,1)} %bitcast.14), calls=%async_computation.1 | async-start | bytes 9175040 | tf_op jit(solution)/shard_map/all_to_all | solution.py:434
  280.7 2.8 all-gather.2.cloned.1.call-done
  283.5 6.3 %collective-permute-start.21 = (f32[128,2560]{1,0:T(8,128)}, f32[128,2560]{1,0:T(8,128)S(1)}, u32[]{:S(2)}, u32[]{:S(2)}) collective-permute-start(f32[128,2560]{1,0:T(8,128)} %all-gather.2.cloned.1.call-done), channel_id=1, source_target_pairs={{0,1},{1,0},{2,3},{3,2},{4,5},{5,4},{6,7},{7,6},{8,9},{9,8},{10,11... | collective-permute-start | bytes 3932168 | tf_op jit(solution)/shard_map/ppermute | solution.py:369
  295.9 42.0 %all-to-all-done.1 = bf16[32,112,640]{2,1,0:T(8,128)(2,1)} async-done(((bf16[32,112,640]{2,1,0:T(8,128)(2,1)}), bf16[32,112,640]{2,1,0:T(8,128)(2,1)}, u32[]{:S(2)}, u32[]{:S(2)}) %all-to-all-start.1) | async-done | bytes 4587552 | tf_op jit(solution)/shard_map/all_to_all | solution.py:434
  337.9 10.9 %shard_map.117 = bf16[128,2560]{1,0:T(8,128)(2,1)} custom-call(bf16[3584,640]{1,0:T(8,128)(2,1)} %bitcast.10.returned, bf16[128,2560]{1,0:T(8,128)(2,1)} %shard_map.113.latents, s32[128,6]{1,0:T(8,128)} %copy.15.ids, f32[128,6]{1,0:T(8,128)} %copy.27.weights), custom_call_target="tpu_custom_call" | custom-call | flops 4000000000 | bytes 6000000 | tf_op jit(solution)/shard_map/pallas_call | solution.py:354
  (84 shorter events, 54.0 us)
Async XLA Ops:
  7.2 10.8 %collective-permute-start = (bf16[512,2560]{1,0:T(8,128)(2,1)}, bf16[512,2560]{1,0:T(8,128)(2,1)S(1)}, u32[]{:S(2)}, u32[]{:S(2)}) collective-permute-start(bf16[512,2560]{1,0:T(8,128)(2,1)} %near_keys.3), channel_id=1, source_target_pairs={{0,1},{1,0},{2,3},{3,2},{4,5},{5,4},{6,7},{7,6},{8,9},{9,8},{10,11... | collective-permute-start | bytes 7864328 | tf_op jit(solution)/shard_map/ppermute | solution.py:369
  46.9 23.4 %all-to-all-start.2 = ((f32[16,8,2560]{2,1,0:T(8,128)}), f32[16,8,2560]{2,1,0:T(8,128)S(1)}, u32[]{:S(2)}, u32[]{:S(2)}) async-start(f32[16,8,2560]{2,1,0:T(8,128)} %bitcast.12), calls=%async_computation.2 | async-start | bytes 2621440 | tf_op jit(solution)/shard_map/all_to_all | solution.py:388
  70.3 163.5 %all-to-all-start = ((bf16[32,112,640]{2,1,0:T(8,128)(2,1)}), bf16[32,112,640]{2,1,0:T(8,128)(2,1)}, u32[]{:S(2)}, u32[]{:S(2)}) async-start(bf16[32,112,640]{2,1,0:T(8,128)(2,1)} %bitcast.13), calls=%async_computation | async-start | bytes 9175040 | tf_op jit(solution)/shard_map/all_to_all | solution.py:426
  78.4 205.1 %all-gather.2.cloned.1.call-start = ((), (), s32[]{:S(2)}) async-start(), calls=%async_computation.3 | async-start | bytes 1392640 | tf_op jit(solution)/shard_map/all_gather | solution.py:399
  81.3 29.4 %collective-permute-start.2 = (bf16[640,832]{0,1:T(8,128)(2,1)}, bf16[640,832]{0,1:T(8,128)(2,1)S(1)}, u32[]{:S(2)}, u32[]{:S(2)}) collective-permute-start(bf16[640,832]{0,1:T(8,128)(2,1)} %copy.16), channel_id=1, source_target_pairs={{0,32},{32,64},{64,96},{96,128},{128,160},{160,192},{192,224},{224... | collective-permute-start | bytes 3194888 | tf_op jit(solution)/shard_map/ppermute | solution.py:373
  83.0 27.8 %collective-permute-start.5 = (bf16[640,832]{0,1:T(8,128)(2,1)}, bf16[640,832]{0,1:T(8,128)(2,1)S(1)}, u32[]{:S(2)}, u32[]{:S(2)}) collective-permute-start(bf16[640,832]{0,1:T(8,128)(2,1)} %copy.16), channel_id=1, source_target_pairs={{0,224},{32,0},{64,32},{96,64},{128,96},{160,128},{192,160},{224,1... | collective-permute-start | bytes 3194888 | tf_op jit(solution)/shard_map/ppermute | solution.py:373
  110.7 25.4 %collective-permute-start.3 = (bf16[640,832]{0,1:T(8,128)(2,1)S(1)}, bf16[640,832]{0,1:T(8,128)(2,1)S(1)}, u32[]{:S(2)}, u32[]{:S(2)}) collective-permute-start(bf16[640,832]{0,1:T(8,128)(2,1)S(1)} %collective-permute-done.2), channel_id=1, source_target_pairs={{0,32},{32,64},{64,96},{96,128},{128,160},{160,192},{192,224},{224... | collective-permute-start | bytes 3194888 | tf_op jit(solution)/shard_map/ppermute | solution.py:373
  110.8 25.4 %collective-permute-start.6 = (bf16[640,832]{0,1:T(8,128)(2,1)S(1)}, bf16[640,832]{0,1:T(8,128)(2,1)}, u32[]{:S(2)}, u32[]{:S(2)}) collective-permute-start(bf16[640,832]{0,1:T(8,128)(2,1)S(1)} %collective-permute-done.5), channel_id=1, source_target_pairs={{0,224},{32,0},{64,32},{96,64},{128,96},{160,128},{192,160},{224,1... | collective-permute-start | bytes 3194888 | tf_op jit(solution)/shard_map/ppermute | solution.py:373
  113.4 35.0 %collective-permute-start.10 = (bf16[320,832]{1,0:T(8,128)(2,1)}, bf16[320,832]{1,0:T(8,128)(2,1)S(1)}, u32[]{:S(2)}, u32[]{:S(2)}) collective-permute-start(bf16[320,832]{1,0:T(8,128)(2,1)} %bitcast.17), channel_id=1, source_target_pairs={{0,32},{32,64},{64,96},{96,128},{128,160},{160,192},{192,224},{224... | collective-permute-start | bytes 1597448 | tf_op jit(solution)/shard_map/ppermute | solution.py:373
  113.4 35.8 %collective-permute-start.13 = (bf16[320,832]{1,0:T(8,128)(2,1)}, bf16[320,832]{1,0:T(8,128)(2,1)S(1)}, u32[]{:S(2)}, u32[]{:S(2)}) collective-permute-start(bf16[320,832]{1,0:T(8,128)(2,1)} %bitcast.18), channel_id=1, source_target_pairs={{0,224},{32,0},{64,32},{96,64},{128,96},{160,128},{192,160},{224,1... | collective-permute-start | bytes 1597448 | tf_op jit(solution)/shard_map/ppermute | solution.py:373
  136.2 50.2 %collective-permute-start.4 = (bf16[640,832]{0,1:T(8,128)(2,1)S(1)}, bf16[640,832]{0,1:T(8,128)(2,1)}, u32[]{:S(2)}, u32[]{:S(2)}) collective-permute-start(bf16[640,832]{0,1:T(8,128)(2,1)S(1)} %collective-permute-done.3), channel_id=1, source_target_pairs={{0,32},{32,64},{64,96},{96,128},{128,160},{160,192},{192,224},{224... | collective-permute-start | bytes 3194888 | tf_op jit(solution)/shard_map/ppermute | solution.py:373
  136.2 54.5 %collective-permute-start.7 = (bf16[640,832]{0,1:T(8,128)(2,1)}, bf16[640,832]{0,1:T(8,128)(2,1)}, u32[]{:S(2)}, u32[]{:S(2)}) collective-permute-start(bf16[640,832]{0,1:T(8,128)(2,1)} %collective-permute-done.6), channel_id=1, source_target_pairs={{0,224},{32,0},{64,32},{96,64},{128,96},{160,128},{192,160},{224,1... | collective-permute-start | bytes 3194888 | tf_op jit(solution)/shard_map/ppermute | solution.py:373
  149.3 34.4 %collective-permute-start.11 = (bf16[320,832]{1,0:T(8,128)(2,1)S(1)}, bf16[320,832]{1,0:T(8,128)(2,1)}, u32[]{:S(2)}, u32[]{:S(2)}) collective-permute-start(bf16[320,832]{1,0:T(8,128)(2,1)S(1)} %collective-permute-done.10.f1), channel_id=1, source_target_pairs={{0,32},{32,64},{64,96},{96,128},{128,160},{160,192},{192,224},{224... | collective-permute-start | bytes 1597448 | tf_op jit(solution)/shard_map/ppermute | solution.py:373
  149.3 34.4 %collective-permute-start.14 = (bf16[320,832]{1,0:T(8,128)(2,1)S(1)}, bf16[320,832]{1,0:T(8,128)(2,1)}, u32[]{:S(2)}, u32[]{:S(2)}) collective-permute-start(bf16[320,832]{1,0:T(8,128)(2,1)S(1)} %collective-permute-done.13.b1), channel_id=1, source_target_pairs={{0,224},{32,0},{64,32},{96,64},{128,96},{160,128},{192,160},{224,1... | collective-permute-start | bytes 1597448 | tf_op jit(solution)/shard_map/ppermute | solution.py:373
  183.7 40.4 %collective-permute-start.12 = (bf16[320,832]{1,0:T(8,128)(2,1)}, bf16[320,832]{1,0:T(8,128)(2,1)}, u32[]{:S(2)}, u32[]{:S(2)}) collective-permute-start(bf16[320,832]{1,0:T(8,128)(2,1)} %collective-permute-done.11.f2), channel_id=1, source_target_pairs={{0,32},{32,64},{64,96},{96,128},{128,160},{160,192},{192,224},{224... | collective-permute-start | bytes 1597448 | tf_op jit(solution)/shard_map/ppermute | solution.py:373
  183.7 41.5 %collective-permute-start.15 = (bf16[320,832]{1,0:T(8,128)(2,1)}, bf16[320,832]{1,0:T(8,128)(2,1)}, u32[]{:S(2)}, u32[]{:S(2)}) collective-permute-start(bf16[320,832]{1,0:T(8,128)(2,1)} %collective-permute-done.14.b2), channel_id=1, source_target_pairs={{0,224},{32,0},{64,32},{96,64},{128,96},{160,128},{192,160},{224,1... | collective-permute-start | bytes 1597448 | tf_op jit(solution)/shard_map/ppermute | solution.py:373
  190.7 43.2 %collective-permute-start.8 = (bf16[320,832]{1,0:T(8,128)(2,1)}, bf16[320,832]{1,0:T(8,128)(2,1)}, u32[]{:S(2)}, u32[]{:S(2)}) collective-permute-start(bf16[320,832]{1,0:T(8,128)(2,1)} %slice.16), channel_id=1, source_target_pairs={{0,32},{32,64},{64,96},{96,128},{128,160},{160,192},{192,224},{224... | collective-permute-start | bytes 1597448 | tf_op jit(solution)/shard_map/ppermute | solution.py:373
  193.7 40.2 %collective-permute-start.9 = (bf16[320,832]{1,0:T(8,128)(2,1)}, bf16[320,832]{1,0:T(8,128)(2,1)}, u32[]{:S(2)}, u32[]{:S(2)}) collective-permute-start(bf16[320,832]{1,0:T(8,128)(2,1)} %slice.17), channel_id=1, source_target_pairs={{0,224},{32,0},{64,32},{96,64},{128,96},{160,128},{192,160},{224,1... | collective-permute-start | bytes 1597448 | tf_op jit(solution)/shard_map/ppermute | solution.py:373
  197.0 13.8 %collective-permute-start.18 = (f32[8,2560]{1,0:T(8,128)}, f32[8,2560]{1,0:T(8,128)S(1)}, u32[]{:S(2)}, u32[]{:S(2)}) collective-permute-start(f32[8,2560]{1,0:T(8,128)} %reduce_sum.9), channel_id=1, source_target_pairs={{0,32},{32,0},{64,96},{96,64},{128,160},{160,128},{192,224},{224,1... | collective-permute-start | bytes 245768 | tf_op jit(solution)/shard_map/ppermute | solution.py:398
  216.9 16.3 %collective-permute-start.20 = (f32[8,2560]{1,0:T(8,128)S(1)}, f32[8,2560]{1,0:T(8,128)S(1)}, u32[]{:S(2)}, u32[]{:S(2)}) collective-permute-start(f32[8,2560]{1,0:T(8,128)S(1)} %add.15), channel_id=1, source_target_pairs={{0,128},{32,160},{64,192},{96,224},{128,0},{160,32},{192,64},{224,... | collective-permute-start | bytes 245768 | tf_op jit(solution)/shard_map/ppermute | solution.py:398
  225.0 26.8 %collective-permute-start.16 = (bf16[160,832]{1,0:T(8,128)(2,1)S(1)}, bf16[160,832]{1,0:T(8,128)(2,1)S(1)}, u32[]{:S(2)}, u32[]{:S(2)}) collective-permute-start(bf16[160,832]{1,0:T(8,128)(2,1)S(1)} %slice.18), channel_id=1, source_target_pairs={{0,32},{32,64},{64,96},{96,128},{128,160},{160,192},{192,224},{224... | collective-permute-start | bytes 798728 | tf_op jit(solution)/shard_map/ppermute | solution.py:373
  226.1 25.7 %collective-permute-start.17 = (bf16[160,832]{1,0:T(8,128)(2,1)S(1)}, bf16[160,832]{1,0:T(8,128)(2,1)S(1)}, u32[]{:S(2)}, u32[]{:S(2)}) collective-permute-start(bf16[160,832]{1,0:T(8,128)(2,1)S(1)} %slice.19), channel_id=1, source_target_pairs={{0,224},{32,0},{64,32},{96,64},{128,96},{160,128},{192,160},{224,1... | collective-permute-start | bytes 798728 | tf_op jit(solution)/shard_map/ppermute | solution.py:373
  268.8 69.1 %all-to-all-start.1 = ((bf16[32,112,640]{2,1,0:T(8,128)(2,1)}), bf16[32,112,640]{2,1,0:T(8,128)(2,1)}, u32[]{:S(2)}, u32[]{:S(2)}) async-start(bf16[32,112,640]{2,1,0:T(8,128)(2,1)} %bitcast.14), calls=%async_computation.1 | async-start | bytes 9175040 | tf_op jit(solution)/shard_map/all_to_all | solution.py:434
  283.5 9.2 %collective-permute-start.21 = (f32[128,2560]{1,0:T(8,128)}, f32[128,2560]{1,0:T(8,128)S(1)}, u32[]{:S(2)}, u32[]{:S(2)}) collective-permute-start(f32[128,2560]{1,0:T(8,128)} %all-gather.2.cloned.1.call-done), channel_id=1, source_target_pairs={{0,1},{1,0},{2,3},{3,2},{4,5},{5,4},{6,7},{7,6},{8,9},{9,8},{10,11... | collective-permute-start | bytes 3932168 | tf_op jit(solution)/shard_map/ppermute | solution.py:369
  (16 other events, 296.4 us)
Sparse Core Ops, SparseCore 0:
  234.0 49.4 all-gather.1

commit v2 on v0

v2 whole, which is shorter than its diff:
```python
import functools
import math

import jax
import jax.numpy as jnp
from jax import lax
from jax.experimental import pallas as pl
from jax.experimental.pallas import tpu as pltpu
from jax.sharding import PartitionSpec as P

HEADS = 20
HEAD_DIM = 128
WIDTH = HEADS * HEAD_DIM
ROWS = 128
PATCHES = 512
TOP = 6
EXPERTS = 32
HID = 832
CAPACITY = 28
N_DP = 8
SHARD = WIDTH // N_DP
HALVES = 2
BLOCK = HALVES * CAPACITY
GROUP = 8
GROUPS = EXPERTS // GROUP
GROUP_ROWS = GROUP * BLOCK
SMALL = 4
SMALL_ROWS = SMALL * BLOCK
SMALL_SLOTS = SMALL * CAPACITY
SLOTS = EXPERTS * CAPACITY
CHUNK = WIDTH // 2
SPLIT = (128, SHARD - 128)
EPSILON = 1e-06
SCALE = 1.0 / math.sqrt(HEAD_DIM)
HEADS_PER_STEP = 4
VMEM_LIMIT = 56 * 1024 * 1024

F32 = jnp.float32
BF16 = jnp.bfloat16


def dot(a, b):
    return jnp.dot(a, b, preferred_element_type=F32)


def dot_t(a, b):
    return lax.dot_general(a, b, (((1,), (1,)), ((), ())), preferred_element_type=F32)


def iota(shape, axis):
    return lax.broadcasted_iota(jnp.int32, shape, axis)


def over_28(value):
    return (value * 1171) >> 15


def over_56(value):
    return (value * 1171) >> 16


def head_weights(queries, near_keys, far_keys):
    near = dot_t(queries, near_keys) * SCALE
    far = dot_t(queries, far_keys) * SCALE
    peak = jnp.maximum(
        jnp.max(near, axis=1, keepdims=True), jnp.max(far, axis=1, keepdims=True)
    )
    near = jnp.exp(near - peak)
    far = jnp.exp(far - peak)
    total = jnp.sum(near, axis=1, keepdims=True) + jnp.sum(far, axis=1, keepdims=True)
    inverse = 1.0 / total
    return near * inverse, far * inverse


def attention_kernel(
    parity, queries, near_keys, far_keys, near_values, far_values, cotangent, latents, grad
):
    for head in range(HEADS_PER_STEP):
        at = slice(head * HEAD_DIM, (head + 1) * HEAD_DIM)
        near, far = head_weights(queries[:, at], near_keys[:, at], far_keys[:, at])
        attended = dot(near.astype(BF16), near_values[:, at]) + dot(
            far.astype(BF16), far_values[:, at]
        )
        rounded = attended.astype(BF16)
        latents[:, at] = rounded
        given = cotangent[:, at]
        inner = jnp.sum(given.astype(F32) * rounded.astype(F32), axis=1, keepdims=True)
        near = near * (dot_t(given, near_values[:, at]) - inner) * SCALE
        far = far * (dot_t(given, far_values[:, at]) - inner) * SCALE
        part = dot(near.astype(BF16), near_keys[:, at]) + dot(far.astype(BF16), far_keys[:, at])
        grad[:, at] = part.astype(BF16)


def attention(parity, queries, keys, far_keys, values, far_values, cotangent):
    wide = HEADS_PER_STEP * HEAD_DIM
    own = pl.BlockSpec((ROWS, wide), lambda i, parity: (0, i))
    patches = pl.BlockSpec((PATCHES, wide), lambda i, parity: (0, i))
    asked = pl.BlockSpec((ROWS, wide), lambda i, parity: (parity[0], i))
    return pl.pallas_call(
        attention_kernel,
        out_shape=(
            jax.ShapeDtypeStruct((ROWS, WIDTH), BF16),
            jax.ShapeDtypeStruct((ROWS, WIDTH), BF16),
        ),
        grid_spec=pltpu.PrefetchScalarGridSpec(
            num_scalar_prefetch=1,
            grid=(HEADS // HEADS_PER_STEP,),
            in_specs=[asked, patches, patches, patches, patches, own],
            out_specs=(own, own),
        ),
        compiler_params=pltpu.CompilerParams(vmem_limit_bytes=VMEM_LIMIT),
        cost_estimate=pl.CostEstimate(
            flops=2_684_354_560, bytes_accessed=13_000_000, transcendentals=2_621_440
        ),
    )(parity, queries, keys, far_keys, values, far_values, cotangent)


def slot_table(ids):
    named = jnp.zeros((ROWS, EXPERTS), F32)
    for choice in range(TOP):
        named = named + (ids[:, choice : choice + 1] == iota((ROWS, EXPERTS), 1)).astype(F32)
    earlier = (iota((ROWS, ROWS), 0) > iota((ROWS, ROWS), 1)).astype(BF16)
    before = dot(earlier, named.astype(BF16))
    return jnp.where(named > 0, before, -1.0)


def dispatch_kernel(latents, gain, ids, out, stacked, slots):
    at_group = pl.program_id(0)

    @pl.when(at_group == 0)
    def _():
        wide = latents[...].astype(F32)
        factor = lax.rsqrt(jnp.mean(wide * wide, axis=1, keepdims=True) + EPSILON)
        normed = (wide * factor * gain[...]).astype(BF16)
        stacked[:ROWS, :] = normed[:, :CHUNK]
        stacked[ROWS:, :] = normed[:, CHUNK:]
        slots[...] = slot_table(ids).astype(BF16)

    row = iota((GROUP_ROWS, 1), 0)
    expert_of = over_56(row)
    slot_of = row - over_28(row) * CAPACITY
    half_of = over_28(row) - expert_of * HALVES
    pick = (iota((GROUP_ROWS, EXPERTS), 1) == expert_of + at_group * GROUP).astype(BF16)
    match = dot_t(pick, slots[...]) == slot_of.astype(F32)
    chosen = jnp.concatenate(
        [jnp.where(match & (half_of == half), 1.0, 0.0) for half in range(HALVES)], axis=1
    )
    out[...] = dot(chosen.astype(BF16), stacked[...]).astype(BF16)


def dispatch(latents, gain, ids):
    return pl.pallas_call(
        dispatch_kernel,
        grid=(GROUPS,),
        in_specs=[
            pl.BlockSpec((ROWS, WIDTH), lambda i: (0, 0)),
            pl.BlockSpec((1, WIDTH), lambda i: (0, 0)),
            pl.BlockSpec((ROWS, TOP), lambda i: (0, 0)),
        ],
        out_specs=pl.BlockSpec((GROUP_ROWS, CHUNK), lambda i: (i, 0)),
        out_shape=jax.ShapeDtypeStruct((EXPERTS * BLOCK, CHUNK), BF16),
        scratch_shapes=[
            pltpu.VMEM((HALVES * ROWS, CHUNK), BF16),
            pltpu.VMEM((ROWS, EXPERTS), BF16),
        ],
        compiler_params=pltpu.CompilerParams(vmem_limit_bytes=VMEM_LIMIT),
        cost_estimate=pl.CostEstimate(
            flops=1_200_000_000, bytes_accessed=6_000_000, transcendentals=0
        ),
    )(latents, gain, ids)


def spread_rows():
    row = iota((SMALL_ROWS, SMALL_ROWS), 0)
    half = (row >= SMALL_SLOTS).astype(jnp.int32)
    slots = row - half * SMALL_SLOTS
    target = row - half * SMALL_SLOTS + over_28(slots) * CAPACITY + half * CAPACITY
    return (iota((SMALL_ROWS, SMALL_ROWS), 1) == target).astype(BF16)


def gathered_rows():
    row = iota((SMALL_ROWS, SMALL_ROWS), 0)
    block = over_56(row)
    half = over_28(row) - block * HALVES
    slot = row - over_28(row) * CAPACITY
    target = half * SMALL_SLOTS + block * CAPACITY + slot
    return (iota((SMALL_ROWS, SMALL_ROWS), 1) == target).astype(BF16)


HALF = SLOTS // 2
GATHER_ROWS = 2 * SHARD + SPLIT[0]


def whole_block(shape):
    return pl.BlockSpec(shape, lambda i: (0, 0))


def open_kernel(blocks, rows):
    order = spread_rows()
    for part in range(GROUP // SMALL):
        at, to = part * SMALL_ROWS, part * SMALL_SLOTS
        found = dot(order, blocks[at : at + SMALL_ROWS, :]).astype(BF16)
        rows[to : to + SMALL_SLOTS, :CHUNK] = found[:SMALL_SLOTS, :]
        rows[to : to + SMALL_SLOTS, CHUNK:] = found[SMALL_SLOTS:, :]


def opened(received):
    return pl.pallas_call(
        open_kernel,
        grid=(GROUPS,),
        in_specs=[pl.BlockSpec((GROUP_ROWS, CHUNK), lambda i: (i, 0))],
        out_specs=pl.BlockSpec((GROUP_ROWS // HALVES, WIDTH), lambda i: (i, 0)),
        out_shape=jax.ShapeDtypeStruct((SLOTS, WIDTH), BF16),
        compiler_params=pltpu.CompilerParams(vmem_limit_bytes=VMEM_LIMIT),
        cost_estimate=pl.CostEstimate(
            flops=1_000_000_000, bytes_accessed=9_000_000, transcendentals=0
        ),
    )(received)


def close_rows(order, rows, out):
    width = rows.shape[1] // 2
    for group in range(HALF // SMALL_SLOTS):
        taken = rows[group * SMALL_SLOTS : (group + 1) * SMALL_SLOTS, :]
        taken = jnp.concatenate([taken[:, :width], taken[:, width:]], axis=0)
        out[group * SMALL_ROWS : (group + 1) * SMALL_ROWS, :] = dot(order, taken).astype(BF16)


def expert_kernel(rows, gathered, hidden, out, taken, full, down, gates, outs, sems, out_sems):
    row_copies = [
        pltpu.make_async_copy(
            rows.at[pl.ds(half * HALF, HALF), :],
            taken.at[pl.ds(half * HALF, HALF), :],
            sems.at[half],
        )
        for half in range(2)
    ]
    gate_copies, up_copies, down_copies = [], [], []
    for shard in range(N_DP):
        for which, copies in enumerate((gate_copies, up_copies)):
            copies.append(
                pltpu.make_async_copy(
                    gathered.at[pl.ds(shard * GATHER_ROWS + which * SHARD, SHARD), :],
                    full.at[which, pl.ds(shard * SHARD, SHARD), :],
                    sems.at[2 + 3 * shard + which],
                )
            )
        down_copies.append(
            pltpu.make_async_copy(
                gathered.at[pl.ds(shard * GATHER_ROWS + 2 * SHARD, SPLIT[0]), :],
                down.at[pl.ds(shard * SPLIT[0], SPLIT[0]), :],
                sems.at[2 + 3 * shard + 2],
            )
        )
    for copy in [row_copies[0]] + gate_copies + [row_copies[1]] + up_copies + down_copies:
        copy.start()
    for copy in [row_copies[0]] + gate_copies:
        copy.wait()
    gates[:HALF, :] = dot(taken[:HALF, :], full[0])
    row_copies[1].wait()
    gates[HALF:, :] = dot(taken[HALF:, :], full[0])
    for copy in up_copies:
        copy.wait()
    for half in range(2):
        at = slice(half * HALF, (half + 1) * HALF)
        gate = gates[at, :]
        up = dot(taken[at, :], full[1])
        hidden[at, :] = (gate / (1.0 + jnp.exp(-gate)) * up).astype(BF16)
    for copy in down_copies:
        copy.wait()
    order = gathered_rows()
    out_copies = []
    for half in range(2):
        at = slice(half * HALF, (half + 1) * HALF)
        result = dot_t(hidden[at, :], down[...]).astype(BF16)
        close_rows(order, result, outs.at[half])
        copy = pltpu.make_async_copy(
            outs.at[half],
            out.at[pl.ds(half * HALF * HALVES, HALF * HALVES), :],
            out_sems.at[half],
        )
        copy.start()
        out_copies.append(copy)
    for copy in out_copies:
        copy.wait()


def experts(rows, gathered):
    columns = N_DP * SPLIT[0]
    hbm = pl.BlockSpec(memory_space=pl.ANY)
    return pl.pallas_call(
        expert_kernel,
        out_shape=(
            jax.ShapeDtypeStruct((SLOTS, HID), BF16),
            jax.ShapeDtypeStruct((EXPERTS * BLOCK, columns // 2), BF16),
        ),
        in_specs=[hbm, hbm],
        out_specs=(pl.BlockSpec(memory_space=pltpu.VMEM), hbm),
        scratch_shapes=[
            pltpu.VMEM((SLOTS, WIDTH), BF16),
            pltpu.VMEM((2, WIDTH, HID), BF16),
            pltpu.VMEM((columns, HID), BF16),
            pltpu.VMEM((SLOTS, HID), F32),
            pltpu.VMEM((2, HALF * HALVES, columns // 2), BF16),
            pltpu.SemaphoreType.DMA((2 + 3 * N_DP,)),
            pltpu.SemaphoreType.DMA((2,)),
        ],
        compiler_params=pltpu.CompilerParams(vmem_limit_bytes=VMEM_LIMIT),
        cost_estimate=pl.CostEstimate(
            flops=10_000_000_000, bytes_accessed=20_000_000, transcendentals=745_472
        ),
    )(rows, gathered)


def result_kernel(hidden, full, out):
    rows = dot_t(hidden[...], full[...]).astype(BF16)
    close_rows(gathered_rows(), rows, out)


def results(hidden, down):
    columns = down.shape[0]
    return pl.pallas_call(
        result_kernel,
        grid=(2,),
        out_shape=jax.ShapeDtypeStruct((EXPERTS * BLOCK, columns // 2), BF16),
        in_specs=[
            pl.BlockSpec((HALF, HID), lambda i: (i, 0)),
            whole_block((columns, HID)),
        ],
        out_specs=pl.BlockSpec((HALF * HALVES, columns // 2), lambda i: (i, 0)),
        compiler_params=pltpu.CompilerParams(vmem_limit_bytes=VMEM_LIMIT),
        cost_estimate=pl.CostEstimate(
            flops=3_000_000_000, bytes_accessed=8_000_000, transcendentals=0
        ),
    )(hidden, down)


TERMS = 2
SHARE_ROWS = TERMS * HALVES * ROWS


def share_kernel(ids, weights, out, slots, terms):
    at_group = pl.program_id(0)

    @pl.when(at_group == 0)
    def _():
        slots[...] = slot_table(ids).astype(BF16)
        shares = jnp.zeros((ROWS, EXPERTS), F32)
        for choice in range(TOP):
            named = ids[:, choice : choice + 1] == iota((ROWS, EXPERTS), 1)
            shares = shares + jnp.where(named, weights[:, choice : choice + 1], 0.0)
        high = shares.astype(BF16)
        terms[:ROWS, :] = high
        terms[ROWS:, :] = (shares - high.astype(F32)).astype(BF16)

    row = iota((EXPERTS, GROUP_ROWS), 1)
    pick = (over_56(row) + at_group * GROUP == iota((EXPERTS, GROUP_ROWS), 0)).astype(BF16)
    lane = iota((ROWS, GROUP_ROWS), 1)
    slot_of = lane - over_28(lane) * CAPACITY
    half_of = over_28(lane) - over_56(lane) * HALVES
    match = dot(slots[...], pick) == slot_of.astype(F32)
    shares = dot(terms[...], pick)
    for term in range(TERMS):
        for half in range(HALVES):
            at = (term * HALVES + half) * ROWS
            out[at : at + ROWS, :] = jnp.where(
                match & (half_of == half), shares[term * ROWS : (term + 1) * ROWS], 0.0
            ).astype(BF16)


def share_table(ids, weights):
    return pl.pallas_call(
        share_kernel,
        grid=(GROUPS,),
        in_specs=[whole_block((ROWS, TOP)), whole_block((ROWS, TOP))],
        out_specs=pl.BlockSpec((SHARE_ROWS, GROUP_ROWS), lambda i: (i, 0)),
        out_shape=jax.ShapeDtypeStruct((GROUPS * SHARE_ROWS, GROUP_ROWS), BF16),
        scratch_shapes=[
            pltpu.VMEM((ROWS, EXPERTS), BF16),
            pltpu.VMEM((TERMS * ROWS, EXPERTS), BF16),
        ],
        compiler_params=pltpu.CompilerParams(vmem_limit_bytes=VMEM_LIMIT),
        cost_estimate=pl.CostEstimate(
            flops=50_000_000, bytes_accessed=2_000_000, transcendentals=0
        ),
    )(ids, weights)


def mix_blocks(shares, returned, total):
    found = dot(shares[...], returned[...])
    step = HALVES * ROWS
    found = found[:step] + found[step:]

    @pl.when(pl.program_id(0) == 0)
    def _():
        total[...] = found

    @pl.when(pl.program_id(0) > 0)
    def _():
        total[...] += found


def mix_kernel(shares, returned, out, total):
    mix_blocks(shares, returned, total)

    @pl.when(pl.program_id(0) == GROUPS - 1)
    def _():
        width = returned.shape[1]
        out[:, :width] = total[:ROWS, :]
        out[:, width:] = total[ROWS:, :]


def last_kernel(shares, returned, first, latents, out, total):
    mix_blocks(shares, returned, total)

    @pl.when(pl.program_id(0) == GROUPS - 1)
    def _():
        pieces = []
        for shard in range(N_DP):
            half, at = shard // 4, shard % 4 * SPLIT[1]
            pieces.append(first[:, shard * SPLIT[0] : (shard + 1) * SPLIT[0]])
            pieces.append(total[half * ROWS : (half + 1) * ROWS, at : at + SPLIT[1]])
        whole = jnp.concatenate(pieces, axis=1)
        out[...] = (latents[...].astype(F32) + whole).astype(BF16)


def mixed(shares, returned, *last):
    width = returned.shape[1]
    specs = [
        pl.BlockSpec((SHARE_ROWS, GROUP_ROWS), lambda i: (i, 0)),
        pl.BlockSpec((GROUP_ROWS, width), lambda i: (i, 0)),
    ]
    out, kernel = jax.ShapeDtypeStruct((ROWS, 2 * width), F32), mix_kernel
    if last:
        specs += [whole_block(value.shape) for value in last]
        out, kernel = jax.ShapeDtypeStruct((ROWS, WIDTH), BF16), last_kernel
    return pl.pallas_call(
        kernel,
        grid=(GROUPS,),
        in_specs=specs,
        out_shape=out,
        out_specs=whole_block(out.shape),
        scratch_shapes=[pltpu.VMEM((HALVES * ROWS, width), F32)],
        compiler_params=pltpu.CompilerParams(vmem_limit_bytes=VMEM_LIMIT),
        cost_estimate=pl.CostEstimate(
            flops=1_200_000_000, bytes_accessed=4_000_000, transcendentals=0
        ),
    )(shares, returned, *last)


SAME_CORE = [list(range(core, EXPERTS, 2)) for core in range(2)]


def other_core(value):
    return lax.ppermute(value, "expert", [(at, at ^ 1) for at in range(EXPERTS)])


def between_chips(pieces):
    return lax.all_to_all(
        pieces,
        "expert",
        split_axis=0,
        concat_axis=0,
        tiled=True,
        axis_index_groups=SAME_CORE,
    )


def scattered(part):
    pieces = between_chips(part.reshape(EXPERTS // 2, -1, WIDTH))
    return jnp.sum(pieces.astype(F32), axis=0)


def exchange_sum(total, bit):
    return total + lax.ppermute(total, "dp", [(at, at ^ bit) for at in range(N_DP)])


def spread(total):
    pieces = jnp.broadcast_to(total.astype(BF16), (EXPERTS // 2,) + total.shape)
    return between_chips(pieces).reshape(-1, WIDTH)


def both_halves(half):
    far_half = other_core(half)
    low = lax.axis_index("expert") % 2 == 0
    whole = jnp.concatenate(
        [jnp.where(low, half, far_half), jnp.where(low, far_half, half)], axis=0
    )
    return whole.astype(F32)


def exchanged(blocks):
    rows, columns = blocks.shape
    return lax.all_to_all(
        blocks.reshape(EXPERTS, rows // EXPERTS, columns),
        "expert",
        split_axis=0,
        concat_axis=0,
        tiled=True,
    ).reshape(rows, columns)


def tied(*values):
    return lax.optimization_barrier(values)


def per_device(
    queries,
    patch_keys,
    patch_values,
    norm_gain,
    gate_weight,
    up_weight,
    down_weight,
    expert_ids,
    combine_weights,
    latent_grad,
):
    parity = lax.axis_index("expert") % 2
    which = parity.reshape(1).astype(jnp.int32)
    far_keys, far_values = other_core(patch_keys), other_core(patch_values)
    down = down_weight[0].T
    shard = jnp.concatenate([gate_weight[0], up_weight[0], down[: SPLIT[0]]], axis=0)
    gathered = lax.all_gather(shard, "dp", axis=0, tiled=True)
    patches = (which, queries, patch_keys, far_keys, patch_values, far_values)
    latents, grad_part = attention(*patches, latent_grad)
    latents, down = tied(latents, down)
    second_down = lax.all_gather(down[SPLIT[0] :], "dp", axis=0, tiled=True)
    total = scattered(grad_part)
    sent = dispatch(latents, norm_gain.reshape(1, WIDTH), expert_ids)
    sent, total, same_ids = tied(sent, total, expert_ids)
    received = exchanged(sent)
    shares = share_table(same_ids, combine_weights)
    total = exchange_sum(exchange_sum(exchange_sum(total, 1), 2), 4)
    received, total, shares = tied(received, total, shares)
    rows = opened(received)
    rows, total = tied(rows, total)
    half = spread(total)
    hidden, first = experts(rows, gathered)
    hidden, first, half = tied(hidden, first, half)
    first = exchanged(first)
    second = exchanged(results(hidden, second_down))
    first_mix = mixed(shares, first)
    layer_out = mixed(shares, second, first_mix, latents)
    query_grad = both_halves(half)
    return (layer_out, query_grad)


def solution(mesh):
    return jax.shard_map(
        per_device,
        mesh=mesh,
        in_specs=(
            P(),
            P(("dp", "expert"), None),
            P(("dp", "expert"), None),
            P(),
            P("expert", "dp", None),
            P("expert", "dp", None),
            P("expert", None, "dp"),
            P(("dp", "expert"), None),
            P(("dp", "expert"), None),
            P(("dp", "expert"), None),
        ),
        out_specs=(P(("dp", "expert"), None), P()),
        check_vma=False,
    )
```

time: 591 us -> 250 us (0.42); the launches traced: 580 us -> 250 us
  waiting for transfers between devices: 287 us -> 103 us
  local copies, waits for them, and re-layouts: 118 us -> 8.37 us
  Pallas kernels: 0 us -> 68.9 us
  blocking collectives: 67.7 us -> 0 us
  matrix products: 59 us -> 0 us
  starting transfers between devices: 8.2 us -> 49.8 us
  other arithmetic: 25.6 us -> 5.53 us
    psum x1 -> x0, waiting for transfers between devices: 285 us -> none  [per_device(): lax.psum(local_grad.reshape(query_count, model_width), ('dp', 'expert'))]
    pallas_call x0 -> x8, Pallas kernels: none -> 68.9 us  [the longest x1 18 us: experts(): pl.pallas_call(expert_kernel, out_shape=(jax.ShapeDtypeStruct((SLOTS, HID...]
    all_to_all x1 -> x0, blocking collectives: 67.7 us -> none  [per_device(): lax.all_to_all(send_buffer, 'expert', split_axis=0, concat_axis=0, tiled=...]
    all_to_all x1 -> x5, waiting for transfers between devices: 0.01 us -> 60 us  [the longest x3 55.5 us: exchanged(): lax.all_to_all(blocks.reshape(EXPERTS, rows // EXPERTS, columns), 'expert...]
    dot_general x5 -> x0, matrix products: 59 us -> none  [the longest x1 17.9 us: per_device(): jnp.dot(hidden, down_full[0], preferred_element_type=jnp.float32)]
    scatter x1 -> x0, local copies, waits for them, and re-layouts: 37.6 us -> none  [per_device(): send_buffer = jnp.zeros((expert_count * capacity, model_width), jnp.bfloa...]
    reshape x6 -> x1, local copies, waits for them, and re-layouts: 36.4 us -> 0.61 us  [per_device(): sent = dispatch(latents, norm_gain.reshape(1, WIDTH), expert_ids)]
    all_to_all x1 -> x5, starting transfers between devices: 4.8 us -> 34.8 us  [the longest x3 23.6 us: exchanged(): lax.all_to_all(blocks.reshape(EXPERTS, rows // EXPERTS, columns), 'expert...]
  transfers between devices with their start and end apart: 7 -> 13, of which waited for: 1 -> 11; matrix products, arithmetic and copies ran while one was open for 24% -> 3% of each run, Pallas kernels for 0% -> 25%
where the time goes in v2:
time: 250 us
  waiting for transfers between devices  103 us (41%)
  Pallas kernels  68.9 us (28%)
  starting transfers between devices  49.8 us (20%)
  between operations  14.2 us (6%)
  local copies, waits for them, and re-layouts  8.37 us (3%)
  other arithmetic  5.53 us (2%)
    all_to_all x3, waiting for transfers between devices, exchanged(): lax.all_to_all(blocks.reshape(EXPERTS, rows // EXPERTS, columns), 'expert...  55.5 us
    all_to_all x3, starting transfers between devices, exchanged(): lax.all_to_all(blocks.reshape(EXPERTS, rows // EXPERTS, columns), 'expert...  23.6 us
    pallas_call x1, Pallas kernels, experts(): pl.pallas_call(expert_kernel, out_shape=(jax.ShapeDtypeStruct((SLOTS, HID...  18 us
    pallas_call x1, Pallas kernels, attention(): pl.pallas_call(attention_kernel, out_shape=(jax.ShapeDtypeStruct((ROWS, W...  17.9 us
    all_gather x1, waiting for transfers between devices, per_device(): second_down = lax.all_gather(down[SPLIT[0]:], 'dp', axis=0, tiled=True)  17.3 us
    all_to_all x2, starting transfers between devices, between_chips(): lax.all_to_all(pieces, 'expert', split_axis=0, concat_axis=0, tiled=True,...  11.2 us
    ppermute x3, starting transfers between devices, exchange_sum(): lax.ppermute(total, 'dp', [(at, at ^ bit) for at in range(N_DP)])  11.1 us
    pallas_call x2, Pallas kernels, mixed(): pl.pallas_call(kernel, grid=(GROUPS,), in_specs=specs, out_shape=out, out...  10.6 us
  transfers between devices with their start and end apart: 13, of which 11 were waited for; matrix products, arithmetic and copies ran while one was open for 3% of the time, Pallas kernels for 25%

profile of v2, /device:TPU:1, one launch (start us, length us, event | category | flops | bytes accessed | tf_op | source)
XLA Modules:
  0.0 249.6 jit_solution(3704028471181317789)
XLA Ops:
  10.8 3.3 %collective-permute-start = (bf16[512,2560]{1,0:T(8,128)(2,1)S(1)}, bf16[512,2560]{1,0:T(8,128)(2,1)}, u32[]{:S(2)}, u32[]{:S(2)}) collective-permute-start(bf16[512,2560]{1,0:T(8,128)(2,1)S(1)} %copy-done.2), channel_id=1, source_target_pairs={{0,1},{1,0},{2,3},{3,2},{4,5},{5,4},{6,7},{7,6},{8,9},{9,8},{10,11... | collective-permute-start | bytes 7864328 | tf_op jit(solution)/shard_map/ppermute | solution.py:455
  14.2 7.3 %collective-permute-done.far_keys = bf16[512,2560]{1,0:T(8,128)(2,1)} collective-permute-done((bf16[512,2560]{1,0:T(8,128)(2,1)S(1)}, bf16[512,2560]{1,0:T(8,128)(2,1)}, u32[]{:S(2)}, u32[]{:S(2)}) %collective-permute-start) | collective-permute-done | bytes 2621472 | tf_op jit(solution)/shard_map/ppermute | solution.py:455
  22.8 17.9 %shard_map.113 = (bf16[128,2560]{1,0:T(8,128)(2,1)}, bf16[128,2560]{1,0:T(8,128)(2,1)}) custom-call(s32[1]{0:T(128)} %bitcast.parity, bf16[256,2560]{1,0:T(8,128)(2,1)} %queries.1, bf16[512,2560]{1,0:T(8,128)(2,1)} %near_keys.1, bf16[512,2560]{1,0:T(8,128)(2,1)} %collective-permute-done.far_keys, bf16[512,2560]{1,0:T(8,128)(2,1)} %near_values.1, ...), custom_call_target="tpu_custom_call" | custom-call | flops 2684354560 | bytes 13000000 | tf_op jit(solution)/shard_map/pallas_call | solution.py:99
  40.7 5.1 %all-to-all-start = ((bf16[16,8,2560]{2,1,0:T(8,128)(2,1)}), bf16[16,8,2560]{2,1,0:T(8,128)(2,1)S(1)}, u32[]{:S(2)}, u32[]{:S(2)}) async-start(bf16[16,8,2560]{2,1,0:T(8,128)(2,1)} %bitcast.21), calls=%async_computation | async-start | bytes 1310720 | tf_op jit(solution)/shard_map/all_to_all | solution.py:459
  47.1 5.6 %shard_map.114 = bf16[1792,1280]{1,0:T(8,128)(2,1)} custom-call(bf16[128,2560]{1,0:T(8,128)(2,1)} %get-tuple-element.20.latents, f32[1,2560]{1,0:T(1,128)} %reshape.35.gain, s32[128,6]{1,0:T(8,128)} %copy.12.ids), custom_call_target="tpu_custom_call" | custom-call | flops 1200000000 | bytes 6000000 | tf_op jit(solution)/shard_map/pallas_call | solution.py:152
  52.7 4.5 %all-to-all-done = bf16[16,8,2560]{2,1,0:T(8,128)(2,1)S(1)} async-done(((bf16[16,8,2560]{2,1,0:T(8,128)(2,1)}), bf16[16,8,2560]{2,1,0:T(8,128)(2,1)S(1)}, u32[]{:S(2)}, u32[]{:S(2)}) %all-to-all-start) | async-done | bytes 655392 | tf_op jit(solution)/shard_map/all_to_all | solution.py:459
  57.3 7.0 %all-to-all-start.1 = ((bf16[32,56,1280]{2,1,0:T(8,128)(2,1)}), bf16[32,56,1280]{2,1,0:T(8,128)(2,1)}, u32[]{:S(2)}, u32[]{:S(2)}) async-start(bf16[32,56,1280]{2,1,0:T(8,128)(2,1)} %bitcast.14), calls=%async_computation.1 | async-start | bytes 9175040 | tf_op jit(solution)/shard_map/all_to_all | solution.py:494
  66.8 4.6 %collective-permute-done.2 = f32[8,2560]{1,0:T(8,128)S(1)} collective-permute-done((f32[8,2560]{1,0:T(8,128)S(1)}, f32[8,2560]{1,0:T(8,128)S(1)}, u32[]{:S(2)}, u32[]{:S(2)}) %collective-permute-start.2) | collective-permute-done | bytes 81952 | tf_op jit(solution)/shard_map/ppermute | solution.py:475
  71.5 3.1 %collective-permute-start.3 = (f32[8,2560]{1,0:T(8,128)S(1)}, f32[8,2560]{1,0:T(8,128)S(1)}, u32[]{:S(2)}, u32[]{:S(2)}) collective-permute-start(f32[8,2560]{1,0:T(8,128)S(1)} %add.15), channel_id=1, source_target_pairs={{0,64},{32,96},{64,0},{96,32},{128,192},{160,224},{192,128},{224,1... | collective-permute-start | bytes 245768 | tf_op jit(solution)/shard_map/ppermute | solution.py:475
  74.5 5.9 %collective-permute-done.3 = f32[8,2560]{1,0:T(8,128)S(1)} collective-permute-done((f32[8,2560]{1,0:T(8,128)S(1)}, f32[8,2560]{1,0:T(8,128)S(1)}, u32[]{:S(2)}, u32[]{:S(2)}) %collective-permute-start.3) | collective-permute-done | bytes 81952 | tf_op jit(solution)/shard_map/ppermute | solution.py:475
  80.4 6.3 %collective-permute-start.4 = (f32[8,2560]{1,0:T(8,128)S(1)}, f32[8,2560]{1,0:T(8,128)S(1)}, u32[]{:S(2)}, u32[]{:S(2)}) collective-permute-start(f32[8,2560]{1,0:T(8,128)S(1)} %add.16), channel_id=1, source_target_pairs={{0,128},{32,160},{64,192},{96,224},{128,0},{160,32},{192,64},{224,... | collective-permute-start | bytes 245768 | tf_op jit(solution)/shard_map/ppermute | solution.py:475
  88.2 3.8 %shard_map.115.shares = bf16[2048,448]{1,0:T(8,128)(2,1)} custom-call(s32[128,6]{1,0:T(8,128)} %copy.13.ids, f32[128,6]{1,0:T(8,128)} %copy.14.weights), custom_call_target="tpu_custom_call" | custom-call | flops 50000000 | bytes 2000000 | tf_op jit(solution)/shard_map/pallas_call | solution.py:372
  92.1 29.2 %all-to-all-done.1 = bf16[32,56,1280]{2,1,0:T(8,128)(2,1)} async-done(((bf16[32,56,1280]{2,1,0:T(8,128)(2,1)}), bf16[32,56,1280]{2,1,0:T(8,128)(2,1)}, u32[]{:S(2)}, u32[]{:S(2)}) %all-to-all-start.1) | async-done | bytes 4587552 | tf_op jit(solution)/shard_map/all_to_all | solution.py:494
  121.3 5.8 %shard_map.116.rows = bf16[896,2560]{1,0:T(8,128)(2,1)} custom-call(bf16[1792,1280]{1,0:T(8,128)(2,1)} %bitcast.5.blocks), custom_call_target="tpu_custom_call" | custom-call | flops 1000000000 | bytes 9000000 | tf_op jit(solution)/shard_map/pallas_call | solution.py:208
  127.9 6.2 %all-to-all-start.2 = ((bf16[16,8,2560]{2,1,0:T(8,128)(2,1)}), bf16[16,8,2560]{2,1,0:T(8,128)(2,1)S(1)}, u32[]{:S(2)}, u32[]{:S(2)}) async-start(bf16[16,8,2560]{2,1,0:T(8,128)(2,1)} %broadcast_in_dim.3), calls=%async_computation.2 | async-start | bytes 1310720 | tf_op jit(solution)/shard_map/all_to_all | solution.py:459
  134.1 4.5 %all-gather.3.cloned.1.call-done.gathered = bf16[6144,832]{1,0:T(8,128)(2,1)} async-done(((bf16[768,832]{1,0:T(8,128)(2,1)}), bf16[6144,832]{1,0:T(8,128)(2,1)}) %all-gather.3.cloned.1.call-update) | async-done | bytes 10223632 | tf_op jit(solution)/shard_map/all_gather | solution.py:524
  138.6 18.0 %shard_map.117 = (bf16[896,832]{1,0:T(8,128)(2,1)}, bf16[1792,512]{1,0:T(8,128)(2,1)}) custom-call(bf16[896,2560]{1,0:T(8,128)(2,1)} %shard_map.116.rows, bf16[6144,832]{1,0:T(8,128)(2,1)} %all-gather.3.cloned.1.call-done.gathered), custom_call_target="tpu_custom_call" | custom-call | flops 10000000000 | bytes 20000000 | tf_op jit(solution)/shard_map/pallas_call | solution.py:291
  156.7 7.6 %all-to-all-start.4 = ((bf16[32,56,512]{2,1,0:T(8,128)(2,1)}), bf16[32,56,512]{2,1,0:T(8,128)(2,1)S(1)}, u32[]{:S(2)}, u32[]{:S(2)}) async-start(bf16[32,56,512]{2,1,0:T(8,128)(2,1)} %bitcast.20), calls=%async_computation.4 | async-start | bytes 3670016 | tf_op jit(solution)/shard_map/all_to_all | solution.py:494
  164.3 17.3 %all-gather.5.cloned.1.call-done.full = bf16[1536,832]{1,0:T(8,128)(2,1)} async-done(((bf16[192,832]{1,0:T(8,128)(2,1)}), bf16[1536,832]{1,0:T(8,128)(2,1)}) %all-gather.5.cloned.1.call-update) | async-done | bytes 2555920 | tf_op jit(solution)/shard_map/all_gather | solution.py:528
  181.6 7.1 %shard_map.118 = bf16[1792,768]{1,0:T(8,128)(2,1)} custom-call(bf16[896,832]{1,0:T(8,128)(2,1)} %get-tuple-element.32.hidden, bf16[1536,832]{1,0:T(8,128)(2,1)} %all-gather.5.cloned.1.call-done.full), custom_call_target="tpu_custom_call" | custom-call | flops 3000000000 | bytes 8000000 | tf_op jit(solution)/shard_map/pallas_call | solution.py:322
  191.0 9.0 %all-to-all-start.3 = ((bf16[32,56,768]{2,1,0:T(8,128)(2,1)}), bf16[32,56,768]{2,1,0:T(8,128)(2,1)S(1)}, u32[]{:S(2)}, u32[]{:S(2)}) async-start(bf16[32,56,768]{2,1,0:T(8,128)(2,1)} %bitcast.17), calls=%async_computation.3 | async-start | bytes 5505024 | tf_op jit(solution)/shard_map/all_to_all | solution.py:494
  205.3 4.7 %shard_map.119.first = f32[128,1024]{1,0:T(8,128)} custom-call(bf16[2048,448]{1,0:T(8,128)(2,1)} %shard_map.115.shares, bf16[1792,512]{1,0:T(8,128)(2,1)} %bitcast.16), custom_call_target="tpu_custom_call" | custom-call | flops 1200000000 | bytes 4000000 | tf_op jit(solution)/shard_map/pallas_call | solution.py:437
  210.0 25.3 %all-to-all-done.3 = bf16[32,56,768]{2,1,0:T(8,128)(2,1)S(1)} async-done(((bf16[32,56,768]{2,1,0:T(8,128)(2,1)}), bf16[32,56,768]{2,1,0:T(8,128)(2,1)S(1)}, u32[]{:S(2)}, u32[]{:S(2)}) %all-to-all-start.3) | async-done | bytes 2752544 | tf_op jit(solution)/shard_map/all_to_all | solution.py:494
  236.9 5.9 %shard_map.120 = bf16[128,2560]{1,0:T(8,128)(2,1)} custom-call(bf16[2048,448]{1,0:T(8,128)(2,1)} %shard_map.115.shares, bf16[1792,768]{1,0:T(8,128)(2,1)} %bitcast.15, f32[128,1024]{1,0:T(8,128)} %shard_map.119.first, bf16[128,2560]{1,0:T(8,128)(2,1)} %get-tuple-element.20.latents), custom_call_target="tpu_custom_call" | custom-call | flops 1200000000 | bytes 4000000 | tf_op jit(solution)/shard_map/pallas_call | solution.py:437
  (40 shorter events, 20.4 us)
Async XLA Ops:
  7.2 3.6 %copy-start.2 = (bf16[512,2560]{1,0:T(8,128)(2,1)S(1)}, bf16[512,2560]{1,0:T(8,128)(2,1)}, u32[]{:S(2)}) copy-start(bf16[512,2560]{1,0:T(8,128)(2,1)} %near_keys.1) | copy-start | bytes 7864324
  7.2 131.5 %all-gather.3.cloned.1.call-start = ((), (), s32[]{:S(2)}) async-start(), calls=%async_computation.5 | async-start | bytes 12386304 | tf_op jit(solution)/shard_map/all_gather | solution.py:524
  10.8 10.7 %collective-permute-start = (bf16[512,2560]{1,0:T(8,128)(2,1)S(1)}, bf16[512,2560]{1,0:T(8,128)(2,1)}, u32[]{:S(2)}, u32[]{:S(2)}) collective-permute-start(bf16[512,2560]{1,0:T(8,128)(2,1)S(1)} %copy-done.2), channel_id=1, source_target_pairs={{0,1},{1,0},{2,3},{3,2},{4,5},{5,4},{6,7},{7,6},{8,9},{9,8},{10,11... | collective-permute-start | bytes 7864328 | tf_op jit(solution)/shard_map/ppermute | solution.py:455
  14.1 8.6 %collective-permute-start.1 = (bf16[512,2560]{1,0:T(8,128)(2,1)}, bf16[512,2560]{1,0:T(8,128)(2,1)}, u32[]{:S(2)}, u32[]{:S(2)}) collective-permute-start(bf16[512,2560]{1,0:T(8,128)(2,1)} %near_values.1), channel_id=1, source_target_pairs={{0,1},{1,0},{2,3},{3,2},{4,5},{5,4},{6,7},{7,6},{8,9},{9,8},{10,11... | collective-permute-start | bytes 7864328 | tf_op jit(solution)/shard_map/ppermute | solution.py:455
  22.8 23.0 %copy-start.5 = (f32[2560]{0:T(1024)S(1)}, f32[2560]{0:T(1024)}, u32[]{:S(2)}) copy-start(f32[2560]{0:T(1024)} %param.13) | copy-start | bytes 30724
  22.8 23.6 %copy-start.4 = (s32[128,6]{0,1:T(8,128)S(1)}, s32[128,6]{0,1:T(8,128)}, u32[]{:S(2)}) copy-start(s32[128,6]{0,1:T(8,128)} %param.17) | copy-start | bytes 9220
  40.7 16.5 %all-to-all-start = ((bf16[16,8,2560]{2,1,0:T(8,128)(2,1)}), bf16[16,8,2560]{2,1,0:T(8,128)(2,1)S(1)}, u32[]{:S(2)}, u32[]{:S(2)}) async-start(bf16[16,8,2560]{2,1,0:T(8,128)(2,1)} %bitcast.21), calls=%async_computation | async-start | bytes 1310720 | tf_op jit(solution)/shard_map/all_to_all | solution.py:459
  57.2 7.1 %copy-start.3 = (bf16[1,832,320]{1,2,0:T(8,128)(2,1)S(1)}, bf16[1,832,320]{1,2,0:T(8,128)(2,1)}, u32[]{:S(2)}) copy-start(bf16[1,832,320]{1,2,0:T(8,128)(2,1)} %param.16) | copy-start | bytes 1597444
  57.3 29.5 %copy-start.6 = (f32[128,6]{0,1:T(8,128)S(1)}, f32[128,6]{0,1:T(8,128)}, u32[]{:S(2)}) copy-start(f32[128,6]{0,1:T(8,128)} %param.18) | copy-start | bytes 9220
  57.3 64.0 %all-to-all-start.1 = ((bf16[32,56,1280]{2,1,0:T(8,128)(2,1)}), bf16[32,56,1280]{2,1,0:T(8,128)(2,1)}, u32[]{:S(2)}, u32[]{:S(2)}) async-start(bf16[32,56,1280]{2,1,0:T(8,128)(2,1)} %bitcast.14), calls=%async_computation.1 | async-start | bytes 9175040 | tf_op jit(solution)/shard_map/all_to_all | solution.py:494
  64.3 117.3 %all-gather.5.cloned.1.call-start = ((), (), s32[]{:S(2)}) async-start(), calls=%async_computation.6 | async-start | bytes 3096576 | tf_op jit(solution)/shard_map/all_gather | solution.py:528
  65.1 6.3 %collective-permute-start.2 = (f32[8,2560]{1,0:T(8,128)S(1)}, f32[8,2560]{1,0:T(8,128)S(1)}, u32[]{:S(2)}, u32[]{:S(2)}) collective-permute-start(f32[8,2560]{1,0:T(8,128)S(1)} %convert_reduce_fusion), channel_id=1, source_target_pairs={{0,32},{32,0},{64,96},{96,64},{128,160},{160,128},{192,224},{224,1... | collective-permute-start | bytes 245768 | tf_op jit(solution)/shard_map/ppermute | solution.py:475
  71.5 9.0 %collective-permute-start.3 = (f32[8,2560]{1,0:T(8,128)S(1)}, f32[8,2560]{1,0:T(8,128)S(1)}, u32[]{:S(2)}, u32[]{:S(2)}) collective-permute-start(f32[8,2560]{1,0:T(8,128)S(1)} %add.15), channel_id=1, source_target_pairs={{0,64},{32,96},{64,0},{96,32},{128,192},{160,224},{192,128},{224,1... | collective-permute-start | bytes 245768 | tf_op jit(solution)/shard_map/ppermute | solution.py:475
  80.4 11.6 %collective-permute-start.4 = (f32[8,2560]{1,0:T(8,128)S(1)}, f32[8,2560]{1,0:T(8,128)S(1)}, u32[]{:S(2)}, u32[]{:S(2)}) collective-permute-start(f32[8,2560]{1,0:T(8,128)S(1)} %add.16), channel_id=1, source_target_pairs={{0,128},{32,160},{64,192},{96,224},{128,0},{160,32},{192,64},{224,... | collective-permute-start | bytes 245768 | tf_op jit(solution)/shard_map/ppermute | solution.py:475
  127.9 28.7 %all-to-all-start.2 = ((bf16[16,8,2560]{2,1,0:T(8,128)(2,1)}), bf16[16,8,2560]{2,1,0:T(8,128)(2,1)S(1)}, u32[]{:S(2)}, u32[]{:S(2)}) async-start(bf16[16,8,2560]{2,1,0:T(8,128)(2,1)} %broadcast_in_dim.3), calls=%async_computation.2 | async-start | bytes 1310720 | tf_op jit(solution)/shard_map/all_to_all | solution.py:459
  156.7 33.1 %all-to-all-start.4 = ((bf16[32,56,512]{2,1,0:T(8,128)(2,1)}), bf16[32,56,512]{2,1,0:T(8,128)(2,1)S(1)}, u32[]{:S(2)}, u32[]{:S(2)}) async-start(bf16[32,56,512]{2,1,0:T(8,128)(2,1)} %bitcast.20), calls=%async_computation.4 | async-start | bytes 3670016 | tf_op jit(solution)/shard_map/all_to_all | solution.py:494
  189.8 1.3 copy-start.1
  191.0 44.3 %all-to-all-start.3 = ((bf16[32,56,768]{2,1,0:T(8,128)(2,1)}), bf16[32,56,768]{2,1,0:T(8,128)(2,1)S(1)}, u32[]{:S(2)}, u32[]{:S(2)}) async-start(bf16[32,56,768]{2,1,0:T(8,128)(2,1)} %bitcast.17), calls=%async_computation.3 | async-start | bytes 5505024 | tf_op jit(solution)/shard_map/all_to_all | solution.py:494
  200.0 2.3 collective-permute-start.5
  235.3 1.5 copy-start
Sparse Core Ops, SparseCore 0:
  10.9 127.6 all-gather.2
  140.4 41.1 all-gather.4

commit v3 on v2

--- a/solution.py
+++ b/solution.py
@@ -30,6 +30,13 @@
 SLOTS = EXPERTS * CAPACITY
 CHUNK = WIDTH // 2
 SPLIT = (128, SHARD - 128)
+MAIN = 768
+REST = HID - MAIN
+FIRST_MAIN = 2 * SHARD + SPLIT[0]
+FIRST_REST = 64
+FIRST_ROWS = FIRST_MAIN + FIRST_REST
+SECOND_REST = 16
+SECOND_ROWS = SPLIT[1] + SECOND_REST
 EPSILON = 1e-06
 SCALE = 1.0 / math.sqrt(HEAD_DIM)
 HEADS_PER_STEP = 4
@@ -188,7 +195,6 @@
 
 
 HALF = SLOTS // 2
-GATHER_ROWS = 2 * SHARD + SPLIT[0]
 
 
 def whole_block(shape):
@@ -226,7 +232,54 @@
         out[group * SMALL_ROWS : (group + 1) * SMALL_ROWS, :] = dot(order, taken).astype(BF16)
 
 
-def expert_kernel(rows, gathered, hidden, out, taken, full, down, gates, outs, sems, out_sems):
+def side_by_side(left, right):
+    return jnp.concatenate([left.astype(F32), right.astype(F32)], axis=1).astype(BF16)
+
+
+def right_side(block):
+    return pltpu.roll(block.astype(F32), REST, 1)[:, :REST].astype(BF16)
+
+
+def pack_kernel(gate, up, down, first, second):
+    first[:SHARD, :] = gate[:, :MAIN]
+    first[SHARD : 2 * SHARD, :] = up[:, :MAIN]
+    first[2 * SHARD : FIRST_MAIN, :] = down[: SPLIT[0], :MAIN]
+    rest = side_by_side(gate[:, MAIN:], up[:, MAIN:])
+    for block in range(SHARD // FIRST_REST):
+        first[FIRST_MAIN:, block * 128 : (block + 1) * 128] = rest[
+            block * FIRST_REST : (block + 1) * FIRST_REST, :
+        ]
+    first[FIRST_MAIN:, MAIN - 128 :] = side_by_side(
+        down[:FIRST_REST, MAIN:], down[FIRST_REST : SPLIT[0], MAIN:]
+    )
+    second[: SPLIT[1], :] = down[SPLIT[0] :, :MAIN]
+    middle = SPLIT[0] + SPLIT[1] // 2
+    rest = side_by_side(down[SPLIT[0] : middle, MAIN:], down[middle:, MAIN:])
+    for block in range(MAIN // 128):
+        second[SPLIT[1] :, block * 128 : (block + 1) * 128] = rest[
+            block * SECOND_REST : (block + 1) * SECOND_REST, :
+        ]
+
+
+def packed(gate, up, down):
+    vmem = pl.BlockSpec(memory_space=pltpu.VMEM)
+    return pl.pallas_call(
+        pack_kernel,
+        out_shape=(
+            jax.ShapeDtypeStruct((FIRST_ROWS, MAIN), BF16),
+            jax.ShapeDtypeStruct((SECOND_ROWS, MAIN), BF16),
+        ),
+        in_specs=[vmem] * 3,
+        out_specs=(vmem, vmem),
+        compiler_params=pltpu.CompilerParams(vmem_limit_bytes=VMEM_LIMIT),
+        cost_estimate=pl.CostEstimate(flops=0, bytes_accessed=3_200_000, transcendentals=0),
+    )(gate, up, down)
+
+
+def expert_kernel(
+    rows, gathered, hidden, out,
+    taken, full, rests, blocks, down, down_rest, gates, outs, sems, out_sems,
+):
     row_copies = [
         pltpu.make_async_copy(
             rows.at[pl.ds(half * HALF, HALF), :],
@@ -235,45 +288,62 @@
         )
         for half in range(2)
     ]
-    gate_copies, up_copies, down_copies = [], [], []
+    gate_copies, up_copies, rest_copies = [], [], []
     for shard in range(N_DP):
+        start = shard * FIRST_ROWS
         for which, copies in enumerate((gate_copies, up_copies)):
             copies.append(
                 pltpu.make_async_copy(
-                    gathered.at[pl.ds(shard * GATHER_ROWS + which * SHARD, SHARD), :],
+                    gathered.at[pl.ds(start + which * SHARD, SHARD), :],
                     full.at[which, pl.ds(shard * SHARD, SHARD), :],
-                    sems.at[2 + 3 * shard + which],
+                    sems.at[2 + 4 * shard + which],
                 )
             )
-        down_copies.append(
+        rest_copies.append(
             pltpu.make_async_copy(
-                gathered.at[pl.ds(shard * GATHER_ROWS + 2 * SHARD, SPLIT[0]), :],
+                gathered.at[pl.ds(start + FIRST_MAIN, FIRST_REST), :],
+                blocks.at[shard],
+                sems.at[2 + 4 * shard + 2],
+            )
+        )
+        rest_copies.append(
+            pltpu.make_async_copy(
+                gathered.at[pl.ds(start + 2 * SHARD, SPLIT[0]), :],
                 down.at[pl.ds(shard * SPLIT[0], SPLIT[0]), :],
-                sems.at[2 + 3 * shard + 2],
+                sems.at[2 + 4 * shard + 3],
             )
         )
-    for copy in [row_copies[0]] + gate_copies + [row_copies[1]] + up_copies + down_copies:
+    for copy in [row_copies[0]] + gate_copies + [row_copies[1]] + up_copies + rest_copies:
         copy.start()
     for copy in [row_copies[0]] + gate_copies:
         copy.wait()
     gates[:HALF, :] = dot(taken[:HALF, :], full[0])
     row_copies[1].wait()
     gates[HALF:, :] = dot(taken[HALF:, :], full[0])
-    for copy in up_copies:
+    for copy in up_copies + rest_copies:
         copy.wait()
+    for shard in range(N_DP):
+        for block in range(SHARD // FIRST_REST):
+            at = shard * SHARD + block * FIRST_REST
+            rests[at : at + FIRST_REST, :] = blocks[shard, :, block * 128 : (block + 1) * 128]
+        last = blocks[shard, :, MAIN - 128 :]
+        at = shard * SPLIT[0]
+        down_rest[at : at + FIRST_REST, :] = last[:, :REST]
+        down_rest[at + FIRST_REST : at + SPLIT[0], :] = right_side(last)
     for half in range(2):
         at = slice(half * HALF, (half + 1) * HALF)
         gate = gates[at, :]
         up = dot(taken[at, :], full[1])
-        hidden[at, :] = (gate / (1.0 + jnp.exp(-gate)) * up).astype(BF16)
-    for copy in down_copies:
-        copy.wait()
+        hidden[at, :MAIN] = (gate / (1.0 + jnp.exp(-gate)) * up).astype(BF16)
+        both = dot(taken[at, :], rests[...])
+        gate, up = both[:, :REST], pltpu.roll(both, REST, 1)[:, :REST]
+        hidden[at, MAIN:] = (gate / (1.0 + jnp.exp(-gate)) * up).astype(BF16)
     order = gathered_rows()
     out_copies = []
     for half in range(2):
         at = slice(half * HALF, (half + 1) * HALF)
-        result = dot_t(hidden[at, :], down[...]).astype(BF16)
-        close_rows(order, result, outs.at[half])
+        result = dot_t(hidden[at, :MAIN], down[...]) + dot_t(hidden[at, MAIN:], down_rest[...])
+        close_rows(order, result.astype(BF16), outs.at[half])
         copy = pltpu.make_async_copy(
             outs.at[half],
             out.at[pl.ds(half * HALF * HALVES, HALF * HALVES), :],
@@ -287,7 +357,7 @@
 
 def experts(rows, gathered):
     columns = N_DP * SPLIT[0]
-    hbm = pl.BlockSpec(memory_space=pl.ANY)
+    hbm = pl.BlockSpec(memory_space=pltpu.HBM)
     return pl.pallas_call(
         expert_kernel,
         out_shape=(
@@ -298,11 +368,14 @@
         out_specs=(pl.BlockSpec(memory_space=pltpu.VMEM), hbm),
         scratch_shapes=[
             pltpu.VMEM((SLOTS, WIDTH), BF16),
-            pltpu.VMEM((2, WIDTH, HID), BF16),
-            pltpu.VMEM((columns, HID), BF16),
-            pltpu.VMEM((SLOTS, HID), F32),
+            pltpu.VMEM((2, WIDTH, MAIN), BF16),
+            pltpu.VMEM((WIDTH, 2 * REST), BF16),
+            pltpu.VMEM((N_DP, FIRST_REST, MAIN), BF16),
+            pltpu.VMEM((columns, MAIN), BF16),
+            pltpu.VMEM((columns, REST), BF16),
+            pltpu.VMEM((SLOTS, MAIN), F32),
             pltpu.VMEM((2, HALF * HALVES, columns // 2), BF16),
-            pltpu.SemaphoreType.DMA((2 + 3 * N_DP,)),
+            pltpu.SemaphoreType.DMA((2 + 4 * N_DP,)),
             pltpu.SemaphoreType.DMA((2,)),
         ],
         compiler_params=pltpu.CompilerParams(vmem_limit_bytes=VMEM_LIMIT),
@@ -312,27 +385,86 @@
     )(rows, gathered)
 
 
-def result_kernel(hidden, full, out):
-    rows = dot_t(hidden[...], full[...]).astype(BF16)
-    close_rows(gathered_rows(), rows, out)
-
-
-def results(hidden, down):
-    columns = down.shape[0]
+def result_kernel(hidden, gathered, out, units, full, rest, blocks, outs, sems, out_sems):
+    unit_copies = [
+        pltpu.make_async_copy(
+            hidden.at[pl.ds(half * HALF, HALF), :],
+            units.at[pl.ds(half * HALF, HALF), :],
+            sems.at[2 * N_DP + half],
+        )
+        for half in range(2)
+    ]
+    copies, rest_copies = [], []
+    for shard in range(N_DP):
+        start = shard * SECOND_ROWS
+        copies.append(
+            pltpu.make_async_copy(
+                gathered.at[pl.ds(start, SPLIT[1]), :],
+                full.at[pl.ds(shard * SPLIT[1], SPLIT[1]), :],
+                sems.at[2 * shard],
+            )
+        )
+        rest_copies.append(
+            pltpu.make_async_copy(
+                gathered.at[pl.ds(start + SPLIT[1], SECOND_REST), :],
+                blocks.at[shard],
+                sems.at[2 * shard + 1],
+            )
+        )
+    for copy in rest_copies + [unit_copies[0]] + copies + [unit_copies[1]]:
+        copy.start()
+    for copy in rest_copies:
+        copy.wait()
+    for shard in range(N_DP):
+        for block in range(MAIN // 128):
+            at = shard * SPLIT[1] + block * SECOND_REST
+            middle = at + SPLIT[1] // 2
+            both = blocks[shard, :, block * 128 : (block + 1) * 128]
+            rest[at : at + SECOND_REST, :] = both[:, :REST]
+            rest[middle : middle + SECOND_REST, :] = right_side(both)
+    for copy in [unit_copies[0]] + copies:
+        copy.wait()
+    order = gathered_rows()
+    out_copies = []
+    for half in range(2):
+        if half == 1:
+            unit_copies[1].wait()
+        at = slice(half * HALF, (half + 1) * HALF)
+        result = dot_t(units[at, :MAIN], full[...]) + dot_t(units[at, MAIN:], rest[...])
+        close_rows(order, result.astype(BF16), outs.at[half])
+        copy = pltpu.make_async_copy(
+            outs.at[half],
+            out.at[pl.ds(half * HALF * HALVES, HALF * HALVES), :],
+            out_sems.at[half],
+        )
+        copy.start()
+        out_copies.append(copy)
+    for copy in out_copies:
+        copy.wait()
+
+
+def results(hidden, gathered):
+    columns = N_DP * SPLIT[1]
+    hbm = pl.BlockSpec(memory_space=pltpu.HBM)
     return pl.pallas_call(
         result_kernel,
-        grid=(2,),
         out_shape=jax.ShapeDtypeStruct((EXPERTS * BLOCK, columns // 2), BF16),
-        in_specs=[
-            pl.BlockSpec((HALF, HID), lambda i: (i, 0)),
-            whole_block((columns, HID)),
+        in_specs=[hbm, hbm],
+        out_specs=hbm,
+        scratch_shapes=[
+            pltpu.VMEM((SLOTS, HID), BF16),
+            pltpu.VMEM((columns, MAIN), BF16),
+            pltpu.VMEM((columns, REST), BF16),
+            pltpu.VMEM((N_DP, SECOND_REST, MAIN), BF16),
+            pltpu.VMEM((2, HALF * HALVES, columns // 2), BF16),
+            pltpu.SemaphoreType.DMA((2 * N_DP + 2,)),
+            pltpu.SemaphoreType.DMA((2,)),
         ],
-        out_specs=pl.BlockSpec((HALF * HALVES, columns // 2), lambda i: (i, 0)),
         compiler_params=pltpu.CompilerParams(vmem_limit_bytes=VMEM_LIMIT),
         cost_estimate=pl.CostEstimate(
             flops=3_000_000_000, bytes_accessed=8_000_000, transcendentals=0
         ),
-    )(hidden, down)
+    )(hidden, gathered)
 
 
 TERMS = 2
@@ -386,62 +518,75 @@
     )(ids, weights)
 
 
-def mix_blocks(shares, returned, total):
-    found = dot(shares[...], returned[...])
+def mix_blocks(shares, returned, table, blocks, total, sems):
+    share_copies = [
+        pltpu.make_async_copy(
+            shares.at[pl.ds(g * SHARE_ROWS, SHARE_ROWS), :],
+            table.at[pl.ds(g * SHARE_ROWS, SHARE_ROWS), :],
+            sems.at[g],
+        )
+        for g in range(GROUPS)
+    ]
+    copies = [
+        pltpu.make_async_copy(
+            returned.at[pl.ds(g * GROUP_ROWS, GROUP_ROWS), :],
+            blocks.at[pl.ds(g * GROUP_ROWS, GROUP_ROWS), :],
+            sems.at[GROUPS + g],
+        )
+        for g in range(GROUPS)
+    ]
+    for g in range(GROUPS):
+        share_copies[g].start()
+        copies[g].start()
     step = HALVES * ROWS
-    found = found[:step] + found[step:]
-
-    @pl.when(pl.program_id(0) == 0)
-    def _():
-        total[...] = found
-
-    @pl.when(pl.program_id(0) > 0)
-    def _():
-        total[...] += found
-
-
-def mix_kernel(shares, returned, out, total):
-    mix_blocks(shares, returned, total)
-
-    @pl.when(pl.program_id(0) == GROUPS - 1)
-    def _():
-        width = returned.shape[1]
-        out[:, :width] = total[:ROWS, :]
-        out[:, width:] = total[ROWS:, :]
-
-
-def last_kernel(shares, returned, first, latents, out, total):
-    mix_blocks(shares, returned, total)
-
-    @pl.when(pl.program_id(0) == GROUPS - 1)
-    def _():
-        pieces = []
-        for shard in range(N_DP):
-            half, at = shard // 4, shard % 4 * SPLIT[1]
-            pieces.append(first[:, shard * SPLIT[0] : (shard + 1) * SPLIT[0]])
-            pieces.append(total[half * ROWS : (half + 1) * ROWS, at : at + SPLIT[1]])
-        whole = jnp.concatenate(pieces, axis=1)
-        out[...] = (latents[...].astype(F32) + whole).astype(BF16)
+    for g in range(GROUPS):
+        share_copies[g].wait()
+        copies[g].wait()
+        found = dot(
+            table[g * SHARE_ROWS : (g + 1) * SHARE_ROWS, :],
+            blocks[g * GROUP_ROWS : (g + 1) * GROUP_ROWS, :],
+        )
+        found = found[:step] + found[step:]
+        total[...] = found if g == 0 else total[...] + found
+
+
+def mix_kernel(shares, returned, out, table, blocks, total, sems):
+    mix_blocks(shares, returned, table, blocks, total, sems)
+    width = returned.shape[1]
+    out[:, :width] = total[:ROWS, :]
+    out[:, width:] = total[ROWS:, :]
+
+
+def last_kernel(shares, returned, first, latents, out, table, blocks, total, sems):
+    mix_blocks(shares, returned, table, blocks, total, sems)
+    pieces = []
+    for shard in range(N_DP):
+        half, at = shard // 4, shard % 4 * SPLIT[1]
+        pieces.append(first[:, shard * SPLIT[0] : (shard + 1) * SPLIT[0]])
+        pieces.append(total[half * ROWS : (half + 1) * ROWS, at : at + SPLIT[1]])
+    whole = jnp.concatenate(pieces, axis=1)
+    out[...] = (latents[...].astype(F32) + whole).astype(BF16)
 
 
 def mixed(shares, returned, *last):
     width = returned.shape[1]
-    specs = [
-        pl.BlockSpec((SHARE_ROWS, GROUP_ROWS), lambda i: (i, 0)),
-        pl.BlockSpec((GROUP_ROWS, width), lambda i: (i, 0)),
-    ]
+    hbm = pl.BlockSpec(memory_space=pl.ANY if last else pltpu.HBM)
+    vmem = pl.BlockSpec(memory_space=pltpu.VMEM)
     out, kernel = jax.ShapeDtypeStruct((ROWS, 2 * width), F32), mix_kernel
     if last:
-        specs += [whole_block(value.shape) for value in last]
         out, kernel = jax.ShapeDtypeStruct((ROWS, WIDTH), BF16), last_kernel
     return pl.pallas_call(
         kernel,
-        grid=(GROUPS,),
-        in_specs=specs,
+        in_specs=[hbm, hbm] + [vmem] * len(last),
         out_shape=out,
-        out_specs=whole_block(out.shape),
-        scratch_shapes=[pltpu.VMEM((HALVES * ROWS, width), F32)],
-        compiler_params=pltpu.CompilerParams(vmem_limit_bytes=VMEM_LIMIT),
+        out_specs=vmem,
+        scratch_shapes=[
+            pltpu.VMEM(shares.shape, BF16),
+            pltpu.VMEM(returned.shape, BF16),
+            pltpu.VMEM((HALVES * ROWS, width), F32),
+            pltpu.SemaphoreType.DMA((2 * GROUPS,)),
+        ],
+        compiler_params=pltpu.CompilerParams(vmem_limit_bytes=24 * 1024 * 1024),
         cost_estimate=pl.CostEstimate(
             flops=1_200_000_000, bytes_accessed=4_000_000, transcendentals=0
         ),
@@ -519,13 +664,12 @@
     parity = lax.axis_index("expert") % 2
     which = parity.reshape(1).astype(jnp.int32)
     far_keys, far_values = other_core(patch_keys), other_core(patch_values)
-    down = down_weight[0].T
-    shard = jnp.concatenate([gate_weight[0], up_weight[0], down[: SPLIT[0]]], axis=0)
+    shard, second_shard = packed(gate_weight[0], up_weight[0], down_weight[0].T)
     gathered = lax.all_gather(shard, "dp", axis=0, tiled=True)
     patches = (which, queries, patch_keys, far_keys, patch_values, far_values)
     latents, grad_part = attention(*patches, latent_grad)
-    latents, down = tied(latents, down)
-    second_down = lax.all_gather(down[SPLIT[0] :], "dp", axis=0, tiled=True)
+    latents, second_shard = tied(latents, second_shard)
+    second_gathered = lax.all_gather(second_shard, "dp", axis=0, tiled=True)
     total = scattered(grad_part)
     sent = dispatch(latents, norm_gain.reshape(1, WIDTH), expert_ids)
     sent, total, same_ids = tied(sent, total, expert_ids)
@@ -539,7 +683,7 @@
     hidden, first = experts(rows, gathered)
     hidden, first, half = tied(hidden, first, half)
     first = exchanged(first)
-    second = exchanged(results(hidden, second_down))
+    second = exchanged(results(hidden, second_gathered))
     first_mix = mixed(shares, first)
     layer_out = mixed(shares, second, first_mix, latents)
     query_grad = both_halves(half)

time: 250 us -> 239 us (0.956)
  other arithmetic: 5.53 us -> 2.02 us
  starting transfers between devices: 49.8 us -> 47.1 us
    all_to_all x3, waiting for transfers between devices: 55.5 us -> 62.3 us  [exchanged(): lax.all_to_all(blocks.reshape(EXPERTS, rows // EXPERTS, columns), 'expert...]
    all_gather x1, waiting for transfers between devices: 17.3 us -> 12.5 us  [per_device(): second_gathered = lax.all_gather(second_shard, 'dp', axis=0, tiled=True)]
    all_gather x1, waiting for transfers between devices: 4.51 us -> 0.02 us  [per_device(): gathered = lax.all_gather(shard, 'dp', axis=0, tiled=True)]
    all_to_all x3, starting transfers between devices: 23.6 us -> 20.6 us  [exchanged(): lax.all_to_all(blocks.reshape(EXPERTS, rows // EXPERTS, columns), 'expert...]
    pallas_call x3 -> x4, Pallas kernels: 17.8 us -> 17.3 us  [the longest x2 7.3 us: mixed(): pl.pallas_call(kernel, in_specs=[hbm, hbm] + [vmem] * len(last), out_shap...]
  transfers between devices with their start and end apart: 13 -> 13, of which waited for: 11 -> 10; matrix products, arithmetic and copies ran while one was open for 3% -> 2% of each run, Pallas kernels for 25% -> 25%
where the time goes in v3:
time: 239 us
  waiting for transfers between devices  101 us (42%)
  Pallas kernels  68.1 us (28%)
  starting transfers between devices  47.1 us (20%)
  between operations  14.2 us (6%)
  local copies, waits for them, and re-layouts  6.21 us (3%)
    all_to_all x3, waiting for transfers between devices, exchanged(): lax.all_to_all(blocks.reshape(EXPERTS, rows // EXPERTS, columns), 'expert...  62.3 us
    all_to_all x3, starting transfers between devices, exchanged(): lax.all_to_all(blocks.reshape(EXPERTS, rows // EXPERTS, columns), 'expert...  20.6 us
    pallas_call x1, Pallas kernels, attention(): pl.pallas_call(attention_kernel, out_shape=(jax.ShapeDtypeStruct((ROWS, W...  17.9 us
    pallas_call x1, Pallas kernels, experts(): pl.pallas_call(expert_kernel, out_shape=(jax.ShapeDtypeStruct((SLOTS, HID...  17.8 us
    all_gather x1, waiting for transfers between devices, per_device(): second_gathered = lax.all_gather(second_shard, 'dp', axis=0, tiled=True)  12.5 us
    all_to_all x2, starting transfers between devices, between_chips(): lax.all_to_all(pieces, 'expert', split_axis=0, concat_axis=0, tiled=True,...  11.2 us
    ppermute x3, starting transfers between devices, exchange_sum(): lax.ppermute(total, 'dp', [(at, at ^ bit) for at in range(N_DP)])  11.2 us
    ppermute x3, waiting for transfers between devices, exchange_sum(): lax.ppermute(total, 'dp', [(at, at ^ bit) for at in range(N_DP)])  10.5 us
  transfers between devices with their start and end apart: 13, of which 10 were waited for; matrix products, arithmetic and copies ran while one was open for 2% of the time, Pallas kernels for 25%

profile of v3, /device:TPU:1, one launch (start us, length us, event | category | flops | bytes accessed | tf_op | source)
XLA Modules:
  0.0 238.6 jit_solution(4433739317775141311)
XLA Ops:
  7.2 2.8 %shard_map.114 = (bf16[832,768]{1,0:T(8,128)(2,1)}, bf16[208,768]{1,0:T(8,128)(2,1)}) custom-call(bf16[320,832]{1,0:T(8,128)(2,1)} %bitcast.21, bf16[320,832]{1,0:T(8,128)(2,1)} %bitcast.22, bf16[320,832]{1,0:T(8,128)(2,1)} %bitcast.23), custom_call_target="tpu_custom_call" | custom-call | bytes 3200000 | tf_op jit(solution)/shard_map/pallas_call | solution.py:266
  10.1 3.3 %collective-permute-start = (bf16[512,2560]{1,0:T(8,128)(2,1)S(1)}, bf16[512,2560]{1,0:T(8,128)(2,1)}, u32[]{:S(2)}, u32[]{:S(2)}) collective-permute-start(bf16[512,2560]{1,0:T(8,128)(2,1)S(1)} %copy-done.4), channel_id=1, source_target_pairs={{0,1},{1,0},{2,3},{3,2},{4,5},{5,4},{6,7},{7,6},{8,9},{9,8},{10,11... | collective-permute-start | bytes 7864328 | tf_op jit(solution)/shard_map/ppermute | solution.py:600
  13.5 7.3 %collective-permute-done.far_keys = bf16[512,2560]{1,0:T(8,128)(2,1)} collective-permute-done((bf16[512,2560]{1,0:T(8,128)(2,1)S(1)}, bf16[512,2560]{1,0:T(8,128)(2,1)}, u32[]{:S(2)}, u32[]{:S(2)}) %collective-permute-start) | collective-permute-done | bytes 2621472 | tf_op jit(solution)/shard_map/ppermute | solution.py:600
  22.0 17.9 %shard_map.113 = (bf16[128,2560]{1,0:T(8,128)(2,1)}, bf16[128,2560]{1,0:T(8,128)(2,1)}) custom-call(s32[1]{0:T(128)} %bitcast.parity, bf16[256,2560]{1,0:T(8,128)(2,1)} %queries.1, bf16[512,2560]{1,0:T(8,128)(2,1)} %near_keys.1, bf16[512,2560]{1,0:T(8,128)(2,1)} %collective-permute-done.far_keys, bf16[512,2560]{1,0:T(8,128)(2,1)} %near_values.1, ...), custom_call_target="tpu_custom_call" | custom-call | flops 2684354560 | bytes 13000000 | tf_op jit(solution)/shard_map/pallas_call | solution.py:106
  39.9 5.0 %all-to-all-start = ((bf16[16,8,2560]{2,1,0:T(8,128)(2,1)}), bf16[16,8,2560]{2,1,0:T(8,128)(2,1)S(1)}, u32[]{:S(2)}, u32[]{:S(2)}) async-start(bf16[16,8,2560]{2,1,0:T(8,128)(2,1)} %bitcast.20), calls=%async_computation | async-start | bytes 1310720 | tf_op jit(solution)/shard_map/all_to_all | solution.py:604
  46.3 5.6 %shard_map.115 = bf16[1792,1280]{1,0:T(8,128)(2,1)} custom-call(bf16[128,2560]{1,0:T(8,128)(2,1)} %get-tuple-element.23.latents, f32[1,2560]{1,0:T(1,128)} %reshape.35.gain, s32[128,6]{1,0:T(8,128)} %copy.12.ids), custom_call_target="tpu_custom_call" | custom-call | flops 1200000000 | bytes 6000000 | tf_op jit(solution)/shard_map/pallas_call | solution.py:159
  51.9 4.6 %all-to-all-done = bf16[16,8,2560]{2,1,0:T(8,128)(2,1)S(1)} async-done(((bf16[16,8,2560]{2,1,0:T(8,128)(2,1)}), bf16[16,8,2560]{2,1,0:T(8,128)(2,1)S(1)}, u32[]{:S(2)}, u32[]{:S(2)}) %all-to-all-start) | async-done | bytes 655392 | tf_op jit(solution)/shard_map/all_to_all | solution.py:604
  56.5 6.8 %all-to-all-start.1 = ((bf16[32,56,1280]{2,1,0:T(8,128)(2,1)}), bf16[32,56,1280]{2,1,0:T(8,128)(2,1)}, u32[]{:S(2)}, u32[]{:S(2)}) async-start(bf16[32,56,1280]{2,1,0:T(8,128)(2,1)} %bitcast.15), calls=%async_computation.1 | async-start | bytes 9175040 | tf_op jit(solution)/shard_map/all_to_all | solution.py:639
  65.9 4.6 %collective-permute-done.2 = f32[8,2560]{1,0:T(8,128)S(1)} collective-permute-done((f32[8,2560]{1,0:T(8,128)S(1)}, f32[8,2560]{1,0:T(8,128)S(1)}, u32[]{:S(2)}, u32[]{:S(2)}) %collective-permute-start.2) | collective-permute-done | bytes 81952 | tf_op jit(solution)/shard_map/ppermute | solution.py:620
  70.5 3.1 %collective-permute-start.3 = (f32[8,2560]{1,0:T(8,128)S(1)}, f32[8,2560]{1,0:T(8,128)S(1)}, u32[]{:S(2)}, u32[]{:S(2)}) collective-permute-start(f32[8,2560]{1,0:T(8,128)S(1)} %add.15), channel_id=1, source_target_pairs={{0,64},{32,96},{64,0},{96,32},{128,192},{160,224},{192,128},{224,1... | collective-permute-start | bytes 245768 | tf_op jit(solution)/shard_map/ppermute | solution.py:620
  73.6 5.9 %collective-permute-done.3 = f32[8,2560]{1,0:T(8,128)S(1)} collective-permute-done((f32[8,2560]{1,0:T(8,128)S(1)}, f32[8,2560]{1,0:T(8,128)S(1)}, u32[]{:S(2)}, u32[]{:S(2)}) %collective-permute-start.3) | collective-permute-done | bytes 81952 | tf_op jit(solution)/shard_map/ppermute | solution.py:620
  79.5 6.4 %collective-permute-start.4 = (f32[8,2560]{1,0:T(8,128)S(1)}, f32[8,2560]{1,0:T(8,128)S(1)}, u32[]{:S(2)}, u32[]{:S(2)}) collective-permute-start(f32[8,2560]{1,0:T(8,128)S(1)} %add.16), channel_id=1, source_target_pairs={{0,128},{32,160},{64,192},{96,224},{128,0},{160,32},{192,64},{224,... | collective-permute-start | bytes 245768 | tf_op jit(solution)/shard_map/ppermute | solution.py:620
  87.3 3.8 %shard_map.116.shares = bf16[2048,448]{1,0:T(8,128)(2,1)} custom-call(s32[128,6]{1,0:T(8,128)} %copy.13.ids, f32[128,6]{1,0:T(8,128)} %copy.14.weights), custom_call_target="tpu_custom_call" | custom-call | flops 50000000 | bytes 2000000 | tf_op jit(solution)/shard_map/pallas_call | solution.py:504
  91.1 29.2 %all-to-all-done.1 = bf16[32,56,1280]{2,1,0:T(8,128)(2,1)} async-done(((bf16[32,56,1280]{2,1,0:T(8,128)(2,1)}), bf16[32,56,1280]{2,1,0:T(8,128)(2,1)}, u32[]{:S(2)}, u32[]{:S(2)}) %all-to-all-start.1) | async-done | bytes 4587552 | tf_op jit(solution)/shard_map/all_to_all | solution.py:639
  120.4 5.8 %shard_map.117.rows = bf16[896,2560]{1,0:T(8,128)(2,1)} custom-call(bf16[1792,1280]{1,0:T(8,128)(2,1)} %bitcast.7.blocks), custom_call_target="tpu_custom_call" | custom-call | flops 1000000000 | bytes 9000000 | tf_op jit(solution)/shard_map/pallas_call | solution.py:214
  127.0 6.2 %all-to-all-start.2 = ((bf16[16,8,2560]{2,1,0:T(8,128)(2,1)}), bf16[16,8,2560]{2,1,0:T(8,128)(2,1)S(1)}, u32[]{:S(2)}, u32[]{:S(2)}) async-start(bf16[16,8,2560]{2,1,0:T(8,128)(2,1)} %broadcast_in_dim.3), calls=%async_computation.2 | async-start | bytes 1310720 | tf_op jit(solution)/shard_map/all_to_all | solution.py:604
  133.3 17.8 %shard_map.118 = (bf16[896,832]{1,0:T(8,128)(2,1)}, bf16[1792,512]{1,0:T(8,128)(2,1)}) custom-call(bf16[896,2560]{1,0:T(8,128)(2,1)} %shard_map.117.rows, bf16[6656,768]{1,0:T(8,128)(2,1)} %all-gather.3.cloned.1.call-done.gathered), custom_call_target="tpu_custom_call" | custom-call | flops 10000000000 | bytes 20000000 | tf_op jit(solution)/shard_map/pallas_call | solution.py:361
  151.1 8.4 %all-to-all-start.4 = ((bf16[32,56,512]{2,1,0:T(8,128)(2,1)}), bf16[32,56,512]{2,1,0:T(8,128)(2,1)S(1)}, u32[]{:S(2)}, u32[]{:S(2)}) async-start(bf16[32,56,512]{2,1,0:T(8,128)(2,1)} %bitcast.19), calls=%async_computation.4 | async-start | bytes 3670016 | tf_op jit(solution)/shard_map/all_to_all | solution.py:639
  159.5 12.5 %all-gather.5.cloned.1.call-done.gathered = bf16[1664,768]{1,0:T(8,128)(2,1)} async-done(((bf16[208,768]{1,0:T(8,128)(2,1)}), bf16[1664,768]{1,0:T(8,128)(2,1)}) %all-gather.5.cloned.1.call-update) | async-done | bytes 2555920 | tf_op jit(solution)/shard_map/all_gather | solution.py:672
  172.0 7.2 %shard_map.119 = bf16[1792,768]{1,0:T(8,128)(2,1)} custom-call(bf16[896,832]{1,0:T(8,128)(2,1)} %get-tuple-element.36.hidden, bf16[1664,768]{1,0:T(8,128)(2,1)} %all-gather.5.cloned.1.call-done.gathered), custom_call_target="tpu_custom_call" | custom-call | flops 3000000000 | bytes 8000000 | tf_op jit(solution)/shard_map/pallas_call | solution.py:449
  179.2 5.8 %all-to-all-done.4 = bf16[32,56,512]{2,1,0:T(8,128)(2,1)S(1)} async-done(((bf16[32,56,512]{2,1,0:T(8,128)(2,1)}), bf16[32,56,512]{2,1,0:T(8,128)(2,1)S(1)}, u32[]{:S(2)}, u32[]{:S(2)}) %all-to-all-start.4) | async-done | bytes 1835040 | tf_op jit(solution)/shard_map/all_to_all | solution.py:639
  186.2 5.4 %all-to-all-start.3 = ((bf16[32,56,768]{2,1,0:T(8,128)(2,1)}), bf16[32,56,768]{2,1,0:T(8,128)(2,1)}, u32[]{:S(2)}, u32[]{:S(2)}) async-start(bf16[32,56,768]{2,1,0:T(8,128)(2,1)} %bitcast.16), calls=%async_computation.3 | async-start | bytes 5505024 | tf_op jit(solution)/shard_map/all_to_all | solution.py:639
  199.7 27.4 %all-to-all-done.3 = bf16[32,56,768]{2,1,0:T(8,128)(2,1)} async-done(((bf16[32,56,768]{2,1,0:T(8,128)(2,1)}), bf16[32,56,768]{2,1,0:T(8,128)(2,1)}, u32[]{:S(2)}, u32[]{:S(2)}) %all-to-all-start.3) | async-done | bytes 2752544 | tf_op jit(solution)/shard_map/all_to_all | solution.py:639
  227.1 4.6 %shard_map.121 = bf16[128,2560]{1,0:T(8,128)(2,1)} custom-call(bf16[2048,448]{1,0:T(8,128)(2,1)S(1)} %copy-done, bf16[1792,768]{1,0:T(8,128)(2,1)} %bitcast.10.returned, f32[128,1024]{1,0:T(8,128)S(1)} %shard_map.120.first, bf16[128,2560]{1,0:T(8,128)(2,1)S(1)} %copy-done.3), custom_call_target="tpu_custom_call" | custom-call | flops 1200000000 | bytes 4000000 | tf_op jit(solution)/shard_map/pallas_call | solution.py:578
  (40 shorter events, 17.0 us)
Async XLA Ops:
  7.2 2.9 %copy-start.4 = (bf16[512,2560]{1,0:T(8,128)(2,1)S(1)}, bf16[512,2560]{1,0:T(8,128)(2,1)}, u32[]{:S(2)}) copy-start(bf16[512,2560]{1,0:T(8,128)(2,1)} %near_keys.1) | copy-start | bytes 7864324
  7.2 126.1 %all-gather.3.cloned.1.call-start = ((), (), s32[]{:S(2)}) async-start(), calls=%async_computation.5 | async-start | bytes 11501568 | tf_op jit(solution)/shard_map/all_gather | solution.py:668
  10.1 10.7 %collective-permute-start = (bf16[512,2560]{1,0:T(8,128)(2,1)S(1)}, bf16[512,2560]{1,0:T(8,128)(2,1)}, u32[]{:S(2)}, u32[]{:S(2)}) collective-permute-start(bf16[512,2560]{1,0:T(8,128)(2,1)S(1)} %copy-done.4), channel_id=1, source_target_pairs={{0,1},{1,0},{2,3},{3,2},{4,5},{5,4},{6,7},{7,6},{8,9},{9,8},{10,11... | collective-permute-start | bytes 7864328 | tf_op jit(solution)/shard_map/ppermute | solution.py:600
  13.4 8.6 %collective-permute-start.1 = (bf16[512,2560]{1,0:T(8,128)(2,1)}, bf16[512,2560]{1,0:T(8,128)(2,1)}, u32[]{:S(2)}, u32[]{:S(2)}) collective-permute-start(bf16[512,2560]{1,0:T(8,128)(2,1)} %near_values.1), channel_id=1, source_target_pairs={{0,1},{1,0},{2,3},{3,2},{4,5},{5,4},{6,7},{7,6},{8,9},{9,8},{10,11... | collective-permute-start | bytes 7864328 | tf_op jit(solution)/shard_map/ppermute | solution.py:600
  22.0 22.9 %copy-start.6 = (f32[2560]{0:T(1024)S(1)}, f32[2560]{0:T(1024)}, u32[]{:S(2)}) copy-start(f32[2560]{0:T(1024)} %param.13) | copy-start | bytes 30724
  22.0 23.6 %copy-start.5 = (s32[128,6]{0,1:T(8,128)S(1)}, s32[128,6]{0,1:T(8,128)}, u32[]{:S(2)}) copy-start(s32[128,6]{0,1:T(8,128)} %param.17) | copy-start | bytes 9220
  39.9 16.5 %all-to-all-start = ((bf16[16,8,2560]{2,1,0:T(8,128)(2,1)}), bf16[16,8,2560]{2,1,0:T(8,128)(2,1)S(1)}, u32[]{:S(2)}, u32[]{:S(2)}) async-start(bf16[16,8,2560]{2,1,0:T(8,128)(2,1)} %bitcast.20), calls=%async_computation | async-start | bytes 1310720 | tf_op jit(solution)/shard_map/all_to_all | solution.py:604
  56.5 29.3 %copy-start.7 = (f32[128,6]{0,1:T(8,128)S(1)}, f32[128,6]{0,1:T(8,128)}, u32[]{:S(2)}) copy-start(f32[128,6]{0,1:T(8,128)} %param.18) | copy-start | bytes 9220
  56.5 63.8 %all-to-all-start.1 = ((bf16[32,56,1280]{2,1,0:T(8,128)(2,1)}), bf16[32,56,1280]{2,1,0:T(8,128)(2,1)}, u32[]{:S(2)}, u32[]{:S(2)}) async-start(bf16[32,56,1280]{2,1,0:T(8,128)(2,1)} %bitcast.15), calls=%async_computation.1 | async-start | bytes 9175040 | tf_op jit(solution)/shard_map/all_to_all | solution.py:639
  63.4 108.6 %all-gather.5.cloned.1.call-start = ((), (), s32[]{:S(2)}) async-start(), calls=%async_computation.6 | async-start | bytes 2875392 | tf_op jit(solution)/shard_map/all_gather | solution.py:672
  64.1 6.4 %collective-permute-start.2 = (f32[8,2560]{1,0:T(8,128)S(1)}, f32[8,2560]{1,0:T(8,128)S(1)}, u32[]{:S(2)}, u32[]{:S(2)}) collective-permute-start(f32[8,2560]{1,0:T(8,128)S(1)} %convert_reduce_fusion), channel_id=1, source_target_pairs={{0,32},{32,0},{64,96},{96,64},{128,160},{160,128},{192,224},{224,1... | collective-permute-start | bytes 245768 | tf_op jit(solution)/shard_map/ppermute | solution.py:620
  70.5 9.0 %collective-permute-start.3 = (f32[8,2560]{1,0:T(8,128)S(1)}, f32[8,2560]{1,0:T(8,128)S(1)}, u32[]{:S(2)}, u32[]{:S(2)}) collective-permute-start(f32[8,2560]{1,0:T(8,128)S(1)} %add.15), channel_id=1, source_target_pairs={{0,64},{32,96},{64,0},{96,32},{128,192},{160,224},{192,128},{224,1... | collective-permute-start | bytes 245768 | tf_op jit(solution)/shard_map/ppermute | solution.py:620
  79.5 11.6 %collective-permute-start.4 = (f32[8,2560]{1,0:T(8,128)S(1)}, f32[8,2560]{1,0:T(8,128)S(1)}, u32[]{:S(2)}, u32[]{:S(2)}) collective-permute-start(f32[8,2560]{1,0:T(8,128)S(1)} %add.16), channel_id=1, source_target_pairs={{0,128},{32,160},{64,192},{96,224},{128,0},{160,32},{192,64},{224,... | collective-permute-start | bytes 245768 | tf_op jit(solution)/shard_map/ppermute | solution.py:620
  127.0 24.1 %all-to-all-start.2 = ((bf16[16,8,2560]{2,1,0:T(8,128)(2,1)}), bf16[16,8,2560]{2,1,0:T(8,128)(2,1)S(1)}, u32[]{:S(2)}, u32[]{:S(2)}) async-start(bf16[16,8,2560]{2,1,0:T(8,128)(2,1)} %broadcast_in_dim.3), calls=%async_computation.2 | async-start | bytes 1310720 | tf_op jit(solution)/shard_map/all_to_all | solution.py:604
  151.1 33.9 %all-to-all-start.4 = ((bf16[32,56,512]{2,1,0:T(8,128)(2,1)}), bf16[32,56,512]{2,1,0:T(8,128)(2,1)S(1)}, u32[]{:S(2)}, u32[]{:S(2)}) async-start(bf16[32,56,512]{2,1,0:T(8,128)(2,1)} %bitcast.19), calls=%async_computation.4 | async-start | bytes 3670016 | tf_op jit(solution)/shard_map/all_to_all | solution.py:639
  185.0 1.2 copy-start.1
  186.2 40.8 %all-to-all-start.3 = ((bf16[32,56,768]{2,1,0:T(8,128)(2,1)}), bf16[32,56,768]{2,1,0:T(8,128)(2,1)}, u32[]{:S(2)}, u32[]{:S(2)}) async-start(bf16[32,56,768]{2,1,0:T(8,128)(2,1)} %bitcast.16), calls=%async_computation.3 | async-start | bytes 5505024 | tf_op jit(solution)/shard_map/all_to_all | solution.py:639
  191.6 2.2 collective-permute-start.5
  194.0 2.3 copy-start
  194.0 3.1 %copy-start.2 = (bf16[32,56,512]{2,1,0:T(8,128)(2,1)S(1)}, bf16[32,56,512]{2,1,0:T(8,128)(2,1)}, u32[]{:S(2)}) copy-start(bf16[32,56,512]{2,1,0:T(8,128)(2,1)} %copy-done.1) | copy-start | bytes 5505028
  195.8 31.3 %copy-start.3 = (bf16[128,2560]{1,0:T(8,128)(2,1)S(1)}, bf16[128,2560]{1,0:T(8,128)(2,1)}, u32[]{:S(2)}) copy-start(bf16[128,2560]{1,0:T(8,128)(2,1)} %get-tuple-element.23.latents) | copy-start | bytes 1966084
Sparse Core Ops, SparseCore 0:
  10.4 120.3 all-gather.2
  132.6 39.4 all-gather.4

commit v4 on v3

--- a/solution.py
+++ b/solution.py
@@ -177,23 +177,6 @@
     )(latents, gain, ids)
 
 
-def spread_rows():
-    row = iota((SMALL_ROWS, SMALL_ROWS), 0)
-    half = (row >= SMALL_SLOTS).astype(jnp.int32)
-    slots = row - half * SMALL_SLOTS
-    target = row - half * SMALL_SLOTS + over_28(slots) * CAPACITY + half * CAPACITY
-    return (iota((SMALL_ROWS, SMALL_ROWS), 1) == target).astype(BF16)
-
-
-def gathered_rows():
-    row = iota((SMALL_ROWS, SMALL_ROWS), 0)
-    block = over_56(row)
-    half = over_28(row) - block * HALVES
-    slot = row - over_28(row) * CAPACITY
-    target = half * SMALL_SLOTS + block * CAPACITY + slot
-    return (iota((SMALL_ROWS, SMALL_ROWS), 1) == target).astype(BF16)
-
-
 HALF = SLOTS // 2
 
 
@@ -202,12 +185,17 @@
 
 
 def open_kernel(blocks, rows):
-    order = spread_rows()
     for part in range(GROUP // SMALL):
         at, to = part * SMALL_ROWS, part * SMALL_SLOTS
-        found = dot(order, blocks[at : at + SMALL_ROWS, :]).astype(BF16)
-        rows[to : to + SMALL_SLOTS, :CHUNK] = found[:SMALL_SLOTS, :]
-        rows[to : to + SMALL_SLOTS, CHUNK:] = found[SMALL_SLOTS:, :]
+        taken = blocks[at : at + SMALL_ROWS, :].astype(F32)
+        for half in range(HALVES):
+            pieces = [
+                taken[block * BLOCK + half * CAPACITY : block * BLOCK + (half + 1) * CAPACITY, :]
+                for block in range(SMALL)
+            ]
+            rows[to : to + SMALL_SLOTS, half * CHUNK : (half + 1) * CHUNK] = jnp.concatenate(
+                pieces, axis=0
+            ).astype(BF16)
 
 
 def opened(received):
@@ -224,12 +212,15 @@
     )(received)
 
 
-def close_rows(order, rows, out):
+def close_rows(rows, out):
     width = rows.shape[1] // 2
-    for group in range(HALF // SMALL_SLOTS):
-        taken = rows[group * SMALL_SLOTS : (group + 1) * SMALL_SLOTS, :]
-        taken = jnp.concatenate([taken[:, :width], taken[:, width:]], axis=0)
-        out[group * SMALL_ROWS : (group + 1) * SMALL_ROWS, :] = dot(order, taken).astype(BF16)
+    for pair in range(HALF // CAPACITY // 2):
+        pieces = []
+        for block in (2 * pair, 2 * pair + 1):
+            taken = rows[block * CAPACITY : (block + 1) * CAPACITY, :]
+            pieces += [taken[:, :width], taken[:, width:]]
+        at = 2 * pair * BLOCK
+        out[at : at + 2 * BLOCK, :] = jnp.concatenate(pieces, axis=0).astype(BF16)
 
 
 def side_by_side(left, right):
@@ -240,37 +231,66 @@
     return pltpu.roll(block.astype(F32), REST, 1)[:, :REST].astype(BF16)
 
 
-def pack_kernel(gate, up, down, first, second):
-    first[:SHARD, :] = gate[:, :MAIN]
-    first[SHARD : 2 * SHARD, :] = up[:, :MAIN]
-    first[2 * SHARD : FIRST_MAIN, :] = down[: SPLIT[0], :MAIN]
-    rest = side_by_side(gate[:, MAIN:], up[:, MAIN:])
+def pack_kernel(
+    gate, up, down, first, second, gates, ups, downs, first_rest, second_rest, sems, out_sems
+):
+    loads = [
+        pltpu.make_async_copy(source, target, sems.at[index])
+        for index, (source, target) in enumerate(((gate, gates), (up, ups), (down, downs)))
+    ]
+    for load in loads:
+        load.start()
+    outs = []
+
+    def send(source, target):
+        outs.append(pltpu.make_async_copy(source, target, out_sems.at[len(outs)]))
+        outs[-1].start()
+
+    main = pl.ds(0, MAIN)
+    loads[0].wait()
+    send(gates.at[:, main], first.at[pl.ds(0, SHARD), :])
+    loads[1].wait()
+    send(ups.at[:, main], first.at[pl.ds(SHARD, SHARD), :])
+    loads[2].wait()
+    send(downs.at[pl.ds(0, SPLIT[0]), main], first.at[pl.ds(2 * SHARD, SPLIT[0]), :])
+    send(downs.at[pl.ds(SPLIT[0], SPLIT[1]), main], second.at[pl.ds(0, SPLIT[1]), :])
+    rest = side_by_side(gates[:, MAIN:], ups[:, MAIN:])
     for block in range(SHARD // FIRST_REST):
-        first[FIRST_MAIN:, block * 128 : (block + 1) * 128] = rest[
+        first_rest[:, block * 128 : (block + 1) * 128] = rest[
             block * FIRST_REST : (block + 1) * FIRST_REST, :
         ]
-    first[FIRST_MAIN:, MAIN - 128 :] = side_by_side(
-        down[:FIRST_REST, MAIN:], down[FIRST_REST : SPLIT[0], MAIN:]
+    first_rest[:, MAIN - 128 :] = side_by_side(
+        downs[:FIRST_REST, MAIN:], downs[FIRST_REST : SPLIT[0], MAIN:]
     )
-    second[: SPLIT[1], :] = down[SPLIT[0] :, :MAIN]
+    send(first_rest, first.at[pl.ds(FIRST_MAIN, FIRST_REST), :])
     middle = SPLIT[0] + SPLIT[1] // 2
-    rest = side_by_side(down[SPLIT[0] : middle, MAIN:], down[middle:, MAIN:])
+    rest = side_by_side(downs[SPLIT[0] : middle, MAIN:], downs[middle:, MAIN:])
     for block in range(MAIN // 128):
-        second[SPLIT[1] :, block * 128 : (block + 1) * 128] = rest[
+        second_rest[:, block * 128 : (block + 1) * 128] = rest[
             block * SECOND_REST : (block + 1) * SECOND_REST, :
         ]
+    send(second_rest, second.at[pl.ds(SPLIT[1], SECOND_REST), :])
+    for out in outs:
+        out.wait()
 
 
 def packed(gate, up, down):
-    vmem = pl.BlockSpec(memory_space=pltpu.VMEM)
+    hbm = pl.BlockSpec(memory_space=pltpu.HBM)
     return pl.pallas_call(
         pack_kernel,
         out_shape=(
             jax.ShapeDtypeStruct((FIRST_ROWS, MAIN), BF16),
             jax.ShapeDtypeStruct((SECOND_ROWS, MAIN), BF16),
         ),
-        in_specs=[vmem] * 3,
-        out_specs=(vmem, vmem),
+        in_specs=[hbm] * 3,
+        out_specs=(hbm, hbm),
+        scratch_shapes=[pltpu.VMEM((SHARD, HID), BF16)] * 3
+        + [
+            pltpu.VMEM((FIRST_REST, MAIN), BF16),
+            pltpu.VMEM((SECOND_REST, MAIN), BF16),
+            pltpu.SemaphoreType.DMA((3,)),
+            pltpu.SemaphoreType.DMA((6,)),
+        ],
         compiler_params=pltpu.CompilerParams(vmem_limit_bytes=VMEM_LIMIT),
         cost_estimate=pl.CostEstimate(flops=0, bytes_accessed=3_200_000, transcendentals=0),
     )(gate, up, down)
@@ -330,20 +350,17 @@
         at = shard * SPLIT[0]
         down_rest[at : at + FIRST_REST, :] = last[:, :REST]
         down_rest[at + FIRST_REST : at + SPLIT[0], :] = right_side(last)
-    for half in range(2):
-        at = slice(half * HALF, (half + 1) * HALF)
-        gate = gates[at, :]
-        up = dot(taken[at, :], full[1])
-        hidden[at, :MAIN] = (gate / (1.0 + jnp.exp(-gate)) * up).astype(BF16)
-        both = dot(taken[at, :], rests[...])
-        gate, up = both[:, :REST], pltpu.roll(both, REST, 1)[:, :REST]
-        hidden[at, MAIN:] = (gate / (1.0 + jnp.exp(-gate)) * up).astype(BF16)
-    order = gathered_rows()
+    gate = gates[...]
+    up = dot(taken[...], full[1])
+    hidden[:, :MAIN] = (gate / (1.0 + jnp.exp(-gate)) * up).astype(BF16)
+    both = dot(taken[...], rests[...])
+    gate, up = both[:, :REST], pltpu.roll(both, REST, 1)[:, :REST]
+    hidden[:, MAIN:] = (gate / (1.0 + jnp.exp(-gate)) * up).astype(BF16)
     out_copies = []
     for half in range(2):
         at = slice(half * HALF, (half + 1) * HALF)
         result = dot_t(hidden[at, :MAIN], down[...]) + dot_t(hidden[at, MAIN:], down_rest[...])
-        close_rows(order, result.astype(BF16), outs.at[half])
+        close_rows(result, outs.at[half])
         copy = pltpu.make_async_copy(
             outs.at[half],
             out.at[pl.ds(half * HALF * HALVES, HALF * HALVES), :],
@@ -424,14 +441,13 @@
             rest[middle : middle + SECOND_REST, :] = right_side(both)
     for copy in [unit_copies[0]] + copies:
         copy.wait()
-    order = gathered_rows()
     out_copies = []
     for half in range(2):
         if half == 1:
             unit_copies[1].wait()
         at = slice(half * HALF, (half + 1) * HALF)
         result = dot_t(units[at, :MAIN], full[...]) + dot_t(units[at, MAIN:], rest[...])
-        close_rows(order, result.astype(BF16), outs.at[half])
+        close_rows(result, outs.at[half])
         copy = pltpu.make_async_copy(
             outs.at[half],
             out.at[pl.ds(half * HALF * HALVES, HALF * HALVES), :],
@@ -460,7 +476,7 @@
             pltpu.SemaphoreType.DMA((2 * N_DP + 2,)),
             pltpu.SemaphoreType.DMA((2,)),
         ],
-        compiler_params=pltpu.CompilerParams(vmem_limit_bytes=VMEM_LIMIT),
+        compiler_params=pltpu.CompilerParams(vmem_limit_bytes=63 * 1024 * 1024),
         cost_estimate=pl.CostEstimate(
             flops=3_000_000_000, bytes_accessed=8_000_000, transcendentals=0
         ),
@@ -471,8 +487,10 @@
 SHARE_ROWS = TERMS * HALVES * ROWS
 
 
-def share_kernel(ids, weights, out, slots, terms):
+def share_kernel(ids, weights, total, out, repeated, slots, terms):
     at_group = pl.program_id(0)
+    for copy in range(EXPERTS // 2 // GROUPS):
+        repeated[copy] = total[...].astype(BF16)
 
     @pl.when(at_group == 0)
     def _():
@@ -500,25 +518,36 @@
             ).astype(BF16)
 
 
-def share_table(ids, weights):
+def share_table(ids, weights, total):
+    chips = EXPERTS // 2
     return pl.pallas_call(
         share_kernel,
         grid=(GROUPS,),
-        in_specs=[whole_block((ROWS, TOP)), whole_block((ROWS, TOP))],
-        out_specs=pl.BlockSpec((SHARE_ROWS, GROUP_ROWS), lambda i: (i, 0)),
-        out_shape=jax.ShapeDtypeStruct((GROUPS * SHARE_ROWS, GROUP_ROWS), BF16),
+        in_specs=[
+            whole_block((ROWS, TOP)),
+            whole_block((ROWS, TOP)),
+            whole_block(total.shape),
+        ],
+        out_specs=(
+            pl.BlockSpec((SHARE_ROWS, GROUP_ROWS), lambda i: (i, 0)),
+            pl.BlockSpec((chips // GROUPS,) + total.shape, lambda i: (i, 0, 0)),
+        ),
+        out_shape=(
+            jax.ShapeDtypeStruct((GROUPS * SHARE_ROWS, GROUP_ROWS), BF16),
+            jax.ShapeDtypeStruct((chips,) + total.shape, BF16),
+        ),
         scratch_shapes=[
             pltpu.VMEM((ROWS, EXPERTS), BF16),
             pltpu.VMEM((TERMS * ROWS, EXPERTS), BF16),
         ],
         compiler_params=pltpu.CompilerParams(vmem_limit_bytes=VMEM_LIMIT),
         cost_estimate=pl.CostEstimate(
-            flops=50_000_000, bytes_accessed=2_000_000, transcendentals=0
-        ),
-    )(ids, weights)
-
-
-def mix_blocks(shares, returned, table, blocks, total, sems):
+            flops=50_000_000, bytes_accessed=3_000_000, transcendentals=0
+        ),
+    )(ids, weights, total)
+
+
+def mix_blocks(shares, returned, table, blocks, total, sems, later=()):
     share_copies = [
         pltpu.make_async_copy(
             shares.at[pl.ds(g * SHARE_ROWS, SHARE_ROWS), :],
@@ -538,6 +567,8 @@
     for g in range(GROUPS):
         share_copies[g].start()
         copies[g].start()
+    for copy in later:
+        copy.start()
     step = HALVES * ROWS
     for g in range(GROUPS):
         share_copies[g].wait()
@@ -548,6 +579,8 @@
         )
         found = found[:step] + found[step:]
         total[...] = found if g == 0 else total[...] + found
+    for copy in later:
+        copy.wait()
 
 
 def mix_kernel(shares, returned, out, table, blocks, total, sems):
@@ -557,36 +590,44 @@
     out[:, width:] = total[ROWS:, :]
 
 
-def last_kernel(shares, returned, first, latents, out, table, blocks, total, sems):
-    mix_blocks(shares, returned, table, blocks, total, sems)
+def last_kernel(
+    shares, returned, first, latents, out, table, blocks, total, sems, others, own, last_sems
+):
+    copies = [
+        pltpu.make_async_copy(first, others, last_sems.at[0]),
+        pltpu.make_async_copy(latents, own, last_sems.at[1]),
+    ]
+    mix_blocks(shares, returned, table, blocks, total, sems, copies)
     pieces = []
     for shard in range(N_DP):
         half, at = shard // 4, shard % 4 * SPLIT[1]
-        pieces.append(first[:, shard * SPLIT[0] : (shard + 1) * SPLIT[0]])
+        pieces.append(others[:, shard * SPLIT[0] : (shard + 1) * SPLIT[0]])
         pieces.append(total[half * ROWS : (half + 1) * ROWS, at : at + SPLIT[1]])
     whole = jnp.concatenate(pieces, axis=1)
-    out[...] = (latents[...].astype(F32) + whole).astype(BF16)
+    out[...] = (own[...].astype(F32) + whole).astype(BF16)
 
 
 def mixed(shares, returned, *last):
     width = returned.shape[1]
-    hbm = pl.BlockSpec(memory_space=pl.ANY if last else pltpu.HBM)
-    vmem = pl.BlockSpec(memory_space=pltpu.VMEM)
+    hbm = pl.BlockSpec(memory_space=pltpu.HBM)
     out, kernel = jax.ShapeDtypeStruct((ROWS, 2 * width), F32), mix_kernel
+    scratch = [
+        pltpu.VMEM(shares.shape, BF16),
+        pltpu.VMEM(returned.shape, BF16),
+        pltpu.VMEM((HALVES * ROWS, width), F32),
+        pltpu.SemaphoreType.DMA((2 * GROUPS,)),
+    ]
     if last:
         out, kernel = jax.ShapeDtypeStruct((ROWS, WIDTH), BF16), last_kernel
+        scratch += [pltpu.VMEM(value.shape, value.dtype) for value in last]
+        scratch += [pltpu.SemaphoreType.DMA((2,))]
     return pl.pallas_call(
         kernel,
-        in_specs=[hbm, hbm] + [vmem] * len(last),
+        in_specs=[hbm] * (2 + len(last)),
         out_shape=out,
-        out_specs=vmem,
-        scratch_shapes=[
-            pltpu.VMEM(shares.shape, BF16),
-            pltpu.VMEM(returned.shape, BF16),
-            pltpu.VMEM((HALVES * ROWS, width), F32),
-            pltpu.SemaphoreType.DMA((2 * GROUPS,)),
-        ],
-        compiler_params=pltpu.CompilerParams(vmem_limit_bytes=24 * 1024 * 1024),
+        out_specs=pl.BlockSpec(memory_space=pltpu.VMEM),
+        scratch_shapes=scratch,
+        compiler_params=pltpu.CompilerParams(vmem_limit_bytes=63 * 1024 * 1024),
         cost_estimate=pl.CostEstimate(
             flops=1_200_000_000, bytes_accessed=4_000_000, transcendentals=0
         ),
@@ -618,11 +659,6 @@
 
 def exchange_sum(total, bit):
     return total + lax.ppermute(total, "dp", [(at, at ^ bit) for at in range(N_DP)])
-
-
-def spread(total):
-    pieces = jnp.broadcast_to(total.astype(BF16), (EXPERTS // 2,) + total.shape)
-    return between_chips(pieces).reshape(-1, WIDTH)
 
 
 def both_halves(half):
@@ -674,12 +710,12 @@
     sent = dispatch(latents, norm_gain.reshape(1, WIDTH), expert_ids)
     sent, total, same_ids = tied(sent, total, expert_ids)
     received = exchanged(sent)
-    shares = share_table(same_ids, combine_weights)
     total = exchange_sum(exchange_sum(exchange_sum(total, 1), 2), 4)
-    received, total, shares = tied(received, total, shares)
+    shares, repeated = share_table(same_ids, combine_weights, total)
+    received, repeated, shares = tied(received, repeated, shares)
     rows = opened(received)
-    rows, total = tied(rows, total)
-    half = spread(total)
+    rows, repeated = tied(rows, repeated)
+    half = between_chips(repeated).reshape(-1, WIDTH)
     hidden, first = experts(rows, gathered)
     hidden, first, half = tied(hidden, first, half)
     first = exchanged(first)

time: 239 us -> 237 us (level)
  local copies, waits for them, and re-layouts: 6.21 us -> 2.83 us
    all_to_all x3, waiting for transfers between devices: 62.3 us -> 56.9 us  [exchanged(): lax.all_to_all(blocks.reshape(EXPERTS, rows // EXPERTS, columns), 'expert...]
    ppermute x3, waiting for transfers between devices: 10.5 us -> 13.6 us  [exchange_sum(): lax.ppermute(total, 'dp', [(at, at ^ bit) for at in range(N_DP)])]
    all_gather x1, waiting for transfers between devices: 12.5 us -> 15.2 us  [per_device(): second_gathered = lax.all_gather(second_shard, 'dp', axis=0, tiled=True)]
    unnamed x18 -> x10, local copies, waits for them, and re-layouts: 3.98 us -> 1.49 us
  transfers between devices with their start and end apart: 13 -> 13, of which waited for: 10 -> 11; matrix products, arithmetic and copies ran while one was open for 2% -> 2% of each run, Pallas kernels for 25% -> 25%
where the time goes in v4:
time: 237 us; the launch traced here: 236 us
  waiting for transfers between devices  101 us (43%)
  Pallas kernels  67.2 us (28%)
  starting transfers between devices  48 us (20%)
  between operations  14.2 us (6%)
  local copies, waits for them, and re-layouts  2.83 us (1%)
  other arithmetic  2.64 us (1%)
    all_to_all x3, waiting for transfers between devices, exchanged(): lax.all_to_all(blocks.reshape(EXPERTS, rows // EXPERTS, columns), 'expert...  56.9 us
    all_to_all x3, starting transfers between devices, exchanged(): lax.all_to_all(blocks.reshape(EXPERTS, rows // EXPERTS, columns), 'expert...  21.5 us
    pallas_call x1, Pallas kernels, attention(): pl.pallas_call(attention_kernel, out_shape=(jax.ShapeDtypeStruct((ROWS, W...  17.9 us
    pallas_call x1, Pallas kernels, experts(): pl.pallas_call(expert_kernel, out_shape=(jax.ShapeDtypeStruct((SLOTS, HID...  17.4 us
    all_gather x1, waiting for transfers between devices, per_device(): second_gathered = lax.all_gather(second_shard, 'dp', axis=0, tiled=True)  15.2 us
    ppermute x3, waiting for transfers between devices, exchange_sum(): lax.ppermute(total, 'dp', [(at, at ^ bit) for at in range(N_DP)])  13.6 us
    ppermute x3, starting transfers between devices, exchange_sum(): lax.ppermute(total, 'dp', [(at, at ^ bit) for at in range(N_DP)])  11.2 us
    all_to_all x2, starting transfers between devices, between_chips(): lax.all_to_all(pieces, 'expert', split_axis=0, concat_axis=0, tiled=True,...  11.2 us
  transfers between devices with their start and end apart: 13, of which 11 were waited for; matrix products, arithmetic and copies ran while one was open for 2% of the time, Pallas kernels for 25%

profile of v4, /device:TPU:1, one launch (start us, length us, event | category | flops | bytes accessed | tf_op | source)
XLA Modules:
  0.0 236.1 jit_solution(7615093166904418040)
XLA Ops:
  9.7 3.3 %collective-permute-start = (bf16[512,2560]{1,0:T(8,128)(2,1)S(1)}, bf16[512,2560]{1,0:T(8,128)(2,1)}, u32[]{:S(2)}, u32[]{:S(2)}) collective-permute-start(bf16[512,2560]{1,0:T(8,128)(2,1)S(1)} %copy-done), channel_id=1, source_target_pairs={{0,1},{1,0},{2,3},{3,2},{4,5},{5,4},{6,7},{7,6},{8,9},{9,8},{10,11... | collective-permute-start | bytes 7864328 | tf_op jit(solution)/shard_map/ppermute | solution.py:641
  13.1 7.3 %collective-permute-done.far_keys = bf16[512,2560]{1,0:T(8,128)(2,1)} collective-permute-done((bf16[512,2560]{1,0:T(8,128)(2,1)S(1)}, bf16[512,2560]{1,0:T(8,128)(2,1)}, u32[]{:S(2)}, u32[]{:S(2)}) %collective-permute-start) | collective-permute-done | bytes 2621472 | tf_op jit(solution)/shard_map/ppermute | solution.py:641
  21.7 17.9 %shard_map.113 = (bf16[128,2560]{1,0:T(8,128)(2,1)}, bf16[128,2560]{1,0:T(8,128)(2,1)}) custom-call(s32[1]{0:T(128)} %bitcast.parity, bf16[256,2560]{1,0:T(8,128)(2,1)} %queries.1, bf16[512,2560]{1,0:T(8,128)(2,1)} %near_keys.1, bf16[512,2560]{1,0:T(8,128)(2,1)} %collective-permute-done.far_keys, bf16[512,2560]{1,0:T(8,128)(2,1)} %near_values.1, ...), custom_call_target="tpu_custom_call" | custom-call | flops 2684354560 | bytes 13000000 | tf_op jit(solution)/shard_map/pallas_call | solution.py:106
  39.6 5.0 %all-to-all-start = ((bf16[16,8,2560]{2,1,0:T(8,128)(2,1)}), bf16[16,8,2560]{2,1,0:T(8,128)(2,1)S(1)}, u32[]{:S(2)}, u32[]{:S(2)}) async-start(bf16[16,8,2560]{2,1,0:T(8,128)(2,1)} %bitcast.19), calls=%async_computation | async-start | bytes 1310720 | tf_op jit(solution)/shard_map/all_to_all | solution.py:645
  45.9 5.6 %shard_map.115 = bf16[1792,1280]{1,0:T(8,128)(2,1)} custom-call(bf16[128,2560]{1,0:T(8,128)(2,1)} %get-tuple-element.25.latents, f32[1,2560]{1,0:T(1,128)} %reshape.35.gain, s32[128,6]{1,0:T(8,128)} %copy.12.ids), custom_call_target="tpu_custom_call" | custom-call | flops 1200000000 | bytes 6000000 | tf_op jit(solution)/shard_map/pallas_call | solution.py:159
  51.5 4.5 %all-to-all-done = bf16[16,8,2560]{2,1,0:T(8,128)(2,1)S(1)} async-done(((bf16[16,8,2560]{2,1,0:T(8,128)(2,1)}), bf16[16,8,2560]{2,1,0:T(8,128)(2,1)S(1)}, u32[]{:S(2)}, u32[]{:S(2)}) %all-to-all-start) | async-done | bytes 655392 | tf_op jit(solution)/shard_map/all_to_all | solution.py:645
  56.2 6.8 %all-to-all-start.1 = ((bf16[32,56,1280]{2,1,0:T(8,128)(2,1)}), bf16[32,56,1280]{2,1,0:T(8,128)(2,1)}, u32[]{:S(2)}, u32[]{:S(2)}) async-start(bf16[32,56,1280]{2,1,0:T(8,128)(2,1)} %bitcast.14), calls=%async_computation.1 | async-start | bytes 9175040 | tf_op jit(solution)/shard_map/all_to_all | solution.py:675
  65.5 4.6 %collective-permute-done.2 = f32[8,2560]{1,0:T(8,128)S(1)} collective-permute-done((f32[8,2560]{1,0:T(8,128)S(1)}, f32[8,2560]{1,0:T(8,128)S(1)}, u32[]{:S(2)}, u32[]{:S(2)}) %collective-permute-start.2) | collective-permute-done | bytes 81952 | tf_op jit(solution)/shard_map/ppermute | solution.py:661
  73.2 5.9 %collective-permute-done.3 = f32[8,2560]{1,0:T(8,128)S(1)} collective-permute-done((f32[8,2560]{1,0:T(8,128)S(1)}, f32[8,2560]{1,0:T(8,128)S(1)}, u32[]{:S(2)}, u32[]{:S(2)}) %collective-permute-start.3) | collective-permute-done | bytes 81952 | tf_op jit(solution)/shard_map/ppermute | solution.py:661
  79.0 6.4 %collective-permute-start.4 = (f32[8,2560]{1,0:T(8,128)S(1)}, f32[8,2560]{1,0:T(8,128)S(1)}, u32[]{:S(2)}, u32[]{:S(2)}) collective-permute-start(f32[8,2560]{1,0:T(8,128)S(1)} %add.16), channel_id=1, source_target_pairs={{0,128},{32,160},{64,192},{96,224},{128,0},{160,32},{192,64},{224,... | collective-permute-start | bytes 245768 | tf_op jit(solution)/shard_map/ppermute | solution.py:661
  87.0 3.1 %collective-permute-done.4 = f32[8,2560]{1,0:T(8,128)S(1)} collective-permute-done((f32[8,2560]{1,0:T(8,128)S(1)}, f32[8,2560]{1,0:T(8,128)S(1)}, u32[]{:S(2)}, u32[]{:S(2)}) %collective-permute-start.4) | collective-permute-done | bytes 81952 | tf_op jit(solution)/shard_map/ppermute | solution.py:661
  90.7 3.9 %shard_map.116 = (bf16[2048,448]{1,0:T(8,128)(2,1)}, bf16[16,8,2560]{2,1,0:T(8,128)(2,1)}) custom-call(s32[128,6]{1,0:T(8,128)} %copy.13.ids, f32[128,6]{1,0:T(8,128)} %copy.14.weights, f32[8,2560]{1,0:T(8,128)} %add.17.total), custom_call_target="tpu_custom_call" | custom-call | flops 50000000 | bytes 3000000 | tf_op jit(solution)/shard_map/pallas_call | solution.py:523
  94.6 25.4 %all-to-all-done.1 = bf16[32,56,1280]{2,1,0:T(8,128)(2,1)} async-done(((bf16[32,56,1280]{2,1,0:T(8,128)(2,1)}), bf16[32,56,1280]{2,1,0:T(8,128)(2,1)}, u32[]{:S(2)}, u32[]{:S(2)}) %all-to-all-start.1) | async-done | bytes 4587552 | tf_op jit(solution)/shard_map/all_to_all | solution.py:675
  120.0 5.1 %shard_map.117.rows = bf16[896,2560]{1,0:T(8,128)(2,1)} custom-call(bf16[1792,1280]{1,0:T(8,128)(2,1)} %bitcast.7.blocks), custom_call_target="tpu_custom_call" | custom-call | flops 1000000000 | bytes 9000000 | tf_op jit(solution)/shard_map/pallas_call | solution.py:202
  125.1 6.2 %all-to-all-start.2 = ((bf16[16,8,2560]{2,1,0:T(8,128)(2,1)}), bf16[16,8,2560]{2,1,0:T(8,128)(2,1)S(1)}, u32[]{:S(2)}, u32[]{:S(2)}) async-start(bf16[16,8,2560]{2,1,0:T(8,128)(2,1)} %get-tuple-element.39), calls=%async_computation.2 | async-start | bytes 1310720 | tf_op jit(solution)/shard_map/all_to_all | solution.py:645
  131.3 17.4 %shard_map.118 = (bf16[896,832]{1,0:T(8,128)(2,1)}, bf16[1792,512]{1,0:T(8,128)(2,1)}) custom-call(bf16[896,2560]{1,0:T(8,128)(2,1)} %shard_map.117.rows, bf16[6656,768]{1,0:T(8,128)(2,1)} %all-gather.3.cloned.1.call-done.gathered), custom_call_target="tpu_custom_call" | custom-call | flops 10000000000 | bytes 20000000 | tf_op jit(solution)/shard_map/pallas_call | solution.py:378
  148.7 8.5 %all-to-all-start.4 = ((bf16[32,56,512]{2,1,0:T(8,128)(2,1)}), bf16[32,56,512]{2,1,0:T(8,128)(2,1)}, u32[]{:S(2)}, u32[]{:S(2)}) async-start(bf16[32,56,512]{2,1,0:T(8,128)(2,1)} %bitcast.18), calls=%async_computation.4 | async-start | bytes 3670016 | tf_op jit(solution)/shard_map/all_to_all | solution.py:675
  157.2 15.2 %all-gather.5.cloned.1.call-done.gathered = bf16[1664,768]{1,0:T(8,128)(2,1)} async-done(((bf16[208,768]{1,0:T(8,128)(2,1)}), bf16[1664,768]{1,0:T(8,128)(2,1)}) %all-gather.5.cloned.1.call-update) | async-done | bytes 2555920 | tf_op jit(solution)/shard_map/all_gather | solution.py:708
  172.4 6.4 %shard_map.119 = bf16[1792,768]{1,0:T(8,128)(2,1)} custom-call(bf16[896,832]{1,0:T(8,128)(2,1)} %get-tuple-element.40.hidden, bf16[1664,768]{1,0:T(8,128)(2,1)} %all-gather.5.cloned.1.call-done.gathered), custom_call_target="tpu_custom_call" | custom-call | flops 3000000000 | bytes 8000000 | tf_op jit(solution)/shard_map/pallas_call | solution.py:465
  178.9 3.9 %all-to-all-done.4 = bf16[32,56,512]{2,1,0:T(8,128)(2,1)} async-done(((bf16[32,56,512]{2,1,0:T(8,128)(2,1)}), bf16[32,56,512]{2,1,0:T(8,128)(2,1)}, u32[]{:S(2)}, u32[]{:S(2)}) %all-to-all-start.4) | async-done | bytes 1835040 | tf_op jit(solution)/shard_map/all_to_all | solution.py:675
  182.7 6.2 %all-to-all-start.3 = ((bf16[32,56,768]{2,1,0:T(8,128)(2,1)}), bf16[32,56,768]{2,1,0:T(8,128)(2,1)}, u32[]{:S(2)}, u32[]{:S(2)}) async-start(bf16[32,56,768]{2,1,0:T(8,128)(2,1)} %bitcast.15), calls=%async_computation.3 | async-start | bytes 5505024 | tf_op jit(solution)/shard_map/all_to_all | solution.py:675
  193.2 3.4 %shard_map.120.first = f32[128,1024]{1,0:T(8,128)} custom-call(bf16[2048,448]{1,0:T(8,128)(2,1)} %get-tuple-element.32.shares, bf16[1792,512]{1,0:T(8,128)(2,1)} %bitcast.12.returned), custom_call_target="tpu_custom_call" | custom-call | flops 1200000000 | bytes 4000000 | tf_op jit(solution)/shard_map/pallas_call | solution.py:624
  196.7 27.6 %all-to-all-done.3 = bf16[32,56,768]{2,1,0:T(8,128)(2,1)} async-done(((bf16[32,56,768]{2,1,0:T(8,128)(2,1)}), bf16[32,56,768]{2,1,0:T(8,128)(2,1)}, u32[]{:S(2)}, u32[]{:S(2)}) %all-to-all-start.3) | async-done | bytes 2752544 | tf_op jit(solution)/shard_map/all_to_all | solution.py:675
  224.3 5.0 %shard_map.121 = bf16[128,2560]{1,0:T(8,128)(2,1)} custom-call(bf16[2048,448]{1,0:T(8,128)(2,1)} %get-tuple-element.32.shares, bf16[1792,768]{1,0:T(8,128)(2,1)} %bitcast.10.returned, f32[128,1024]{1,0:T(8,128)} %shard_map.120.first, bf16[128,2560]{1,0:T(8,128)(2,1)} %get-tuple-element.25.latents), custom_call_target="tpu_custom_call" | custom-call | flops 1200000000 | bytes 4000000 | tf_op jit(solution)/shard_map/pallas_call | solution.py:624
  (31 shorter events, 17.2 us)
Async XLA Ops:
  7.2 2.5 %copy-start = (bf16[512,2560]{1,0:T(8,128)(2,1)S(1)}, bf16[512,2560]{1,0:T(8,128)(2,1)}, u32[]{:S(2)}) copy-start(bf16[512,2560]{1,0:T(8,128)(2,1)} %near_keys.1) | copy-start | bytes 7864324
  7.2 124.1 %all-gather.3.cloned.1.call-start = ((), (), s32[]{:S(2)}) async-start(), calls=%async_computation.5 | async-start | bytes 11501568 | tf_op jit(solution)/shard_map/all_gather | solution.py:704
  9.7 10.7 %collective-permute-start = (bf16[512,2560]{1,0:T(8,128)(2,1)S(1)}, bf16[512,2560]{1,0:T(8,128)(2,1)}, u32[]{:S(2)}, u32[]{:S(2)}) collective-permute-start(bf16[512,2560]{1,0:T(8,128)(2,1)S(1)} %copy-done), channel_id=1, source_target_pairs={{0,1},{1,0},{2,3},{3,2},{4,5},{5,4},{6,7},{7,6},{8,9},{9,8},{10,11... | collective-permute-start | bytes 7864328 | tf_op jit(solution)/shard_map/ppermute | solution.py:641
  13.0 8.6 %collective-permute-start.1 = (bf16[512,2560]{1,0:T(8,128)(2,1)}, bf16[512,2560]{1,0:T(8,128)(2,1)}, u32[]{:S(2)}, u32[]{:S(2)}) collective-permute-start(bf16[512,2560]{1,0:T(8,128)(2,1)} %near_values.1), channel_id=1, source_target_pairs={{0,1},{1,0},{2,3},{3,2},{4,5},{5,4},{6,7},{7,6},{8,9},{9,8},{10,11... | collective-permute-start | bytes 7864328 | tf_op jit(solution)/shard_map/ppermute | solution.py:641
  21.7 22.9 %copy-start.2 = (f32[2560]{0:T(1024)S(1)}, f32[2560]{0:T(1024)}, u32[]{:S(2)}) copy-start(f32[2560]{0:T(1024)} %param.13) | copy-start | bytes 30724
  21.7 23.5 %copy-start.1 = (s32[128,6]{0,1:T(8,128)S(1)}, s32[128,6]{0,1:T(8,128)}, u32[]{:S(2)}) copy-start(s32[128,6]{0,1:T(8,128)} %param.17) | copy-start | bytes 9220
  39.6 16.5 %all-to-all-start = ((bf16[16,8,2560]{2,1,0:T(8,128)(2,1)}), bf16[16,8,2560]{2,1,0:T(8,128)(2,1)S(1)}, u32[]{:S(2)}, u32[]{:S(2)}) async-start(bf16[16,8,2560]{2,1,0:T(8,128)(2,1)} %bitcast.19), calls=%async_computation | async-start | bytes 1310720 | tf_op jit(solution)/shard_map/all_to_all | solution.py:645
  56.1 29.3 %copy-start.3 = (f32[128,6]{0,1:T(8,128)S(1)}, f32[128,6]{0,1:T(8,128)}, u32[]{:S(2)}) copy-start(f32[128,6]{0,1:T(8,128)} %param.18) | copy-start | bytes 9220
  56.2 63.8 %all-to-all-start.1 = ((bf16[32,56,1280]{2,1,0:T(8,128)(2,1)}), bf16[32,56,1280]{2,1,0:T(8,128)(2,1)}, u32[]{:S(2)}, u32[]{:S(2)}) async-start(bf16[32,56,1280]{2,1,0:T(8,128)(2,1)} %bitcast.14), calls=%async_computation.1 | async-start | bytes 9175040 | tf_op jit(solution)/shard_map/all_to_all | solution.py:675
  63.0 109.4 %all-gather.5.cloned.1.call-start = ((), (), s32[]{:S(2)}) async-start(), calls=%async_computation.6 | async-start | bytes 2875392 | tf_op jit(solution)/shard_map/all_gather | solution.py:708
  63.8 6.4 %collective-permute-start.2 = (f32[8,2560]{1,0:T(8,128)S(1)}, f32[8,2560]{1,0:T(8,128)S(1)}, u32[]{:S(2)}, u32[]{:S(2)}) collective-permute-start(f32[8,2560]{1,0:T(8,128)S(1)} %convert_reduce_fusion), channel_id=1, source_target_pairs={{0,32},{32,0},{64,96},{96,64},{128,160},{160,128},{192,224},{224,1... | collective-permute-start | bytes 245768 | tf_op jit(solution)/shard_map/ppermute | solution.py:661
  70.1 8.9 %collective-permute-start.3 = (f32[8,2560]{1,0:T(8,128)S(1)}, f32[8,2560]{1,0:T(8,128)S(1)}, u32[]{:S(2)}, u32[]{:S(2)}) collective-permute-start(f32[8,2560]{1,0:T(8,128)S(1)} %add.15), channel_id=1, source_target_pairs={{0,64},{32,96},{64,0},{96,32},{128,192},{160,224},{192,128},{224,1... | collective-permute-start | bytes 245768 | tf_op jit(solution)/shard_map/ppermute | solution.py:661
  79.0 11.0 %collective-permute-start.4 = (f32[8,2560]{1,0:T(8,128)S(1)}, f32[8,2560]{1,0:T(8,128)S(1)}, u32[]{:S(2)}, u32[]{:S(2)}) collective-permute-start(f32[8,2560]{1,0:T(8,128)S(1)} %add.16), channel_id=1, source_target_pairs={{0,128},{32,160},{64,192},{96,224},{128,0},{160,32},{192,64},{224,... | collective-permute-start | bytes 245768 | tf_op jit(solution)/shard_map/ppermute | solution.py:661
  125.1 23.6 %all-to-all-start.2 = ((bf16[16,8,2560]{2,1,0:T(8,128)(2,1)}), bf16[16,8,2560]{2,1,0:T(8,128)(2,1)S(1)}, u32[]{:S(2)}, u32[]{:S(2)}) async-start(bf16[16,8,2560]{2,1,0:T(8,128)(2,1)} %get-tuple-element.39), calls=%async_computation.2 | async-start | bytes 1310720 | tf_op jit(solution)/shard_map/all_to_all | solution.py:645
  148.7 34.0 %all-to-all-start.4 = ((bf16[32,56,512]{2,1,0:T(8,128)(2,1)}), bf16[32,56,512]{2,1,0:T(8,128)(2,1)}, u32[]{:S(2)}, u32[]{:S(2)}) async-start(bf16[32,56,512]{2,1,0:T(8,128)(2,1)} %bitcast.18), calls=%async_computation.4 | async-start | bytes 3670016 | tf_op jit(solution)/shard_map/all_to_all | solution.py:675
  182.7 41.6 %all-to-all-start.3 = ((bf16[32,56,768]{2,1,0:T(8,128)(2,1)}), bf16[32,56,768]{2,1,0:T(8,128)(2,1)}, u32[]{:S(2)}, u32[]{:S(2)}) async-start(bf16[32,56,768]{2,1,0:T(8,128)(2,1)} %bitcast.15), calls=%async_computation.3 | async-start | bytes 5505024 | tf_op jit(solution)/shard_map/all_to_all | solution.py:675
  188.9 2.4 %collective-permute-start.5 = (bf16[128,2560]{1,0:T(8,128)(2,1)S(1)}, bf16[128,2560]{1,0:T(8,128)(2,1)S(1)}, u32[]{:S(2)}, u32[]{:S(2)}) collective-permute-start(bf16[128,2560]{1,0:T(8,128)(2,1)S(1)} %bitcast.16), channel_id=1, source_target_pairs={{0,1},{1,0},{2,3},{3,2},{4,5},{5,4},{6,7},{7,6},{8,9},{9,8},{10,11... | collective-permute-start | bytes 1966088 | tf_op jit(solution)/shard_map/ppermute | solution.py:641
Sparse Core Ops, SparseCore 0:
  10.4 120.3 all-gather.2
  132.6 39.8 all-gather.4

commit v5 on v4

--- a/solution.py
+++ b/solution.py
@@ -297,8 +297,8 @@
 
 
 def expert_kernel(
-    rows, gathered, hidden, out,
-    taken, full, rests, blocks, down, down_rest, gates, outs, sems, out_sems,
+    rows, gathered, units, out,
+    taken, full, rests, blocks, down, down_rest, gates, hidden, outs, sems, out_sems,
 ):
     row_copies = [
         pltpu.make_async_copy(
@@ -352,11 +352,12 @@
         down_rest[at + FIRST_REST : at + SPLIT[0], :] = right_side(last)
     gate = gates[...]
     up = dot(taken[...], full[1])
-    hidden[:, :MAIN] = (gate / (1.0 + jnp.exp(-gate)) * up).astype(BF16)
+    hidden[:, :MAIN] = (gate * (0.5 + 0.5 * jnp.tanh(0.5 * gate)) * up).astype(BF16)
     both = dot(taken[...], rests[...])
     gate, up = both[:, :REST], pltpu.roll(both, REST, 1)[:, :REST]
-    hidden[:, MAIN:] = (gate / (1.0 + jnp.exp(-gate)) * up).astype(BF16)
-    out_copies = []
+    hidden[:, MAIN:] = (gate * (0.5 + 0.5 * jnp.tanh(0.5 * gate)) * up).astype(BF16)
+    out_copies = [pltpu.make_async_copy(hidden, units, out_sems.at[2])]
+    out_copies[0].start()
     for half in range(2):
         at = slice(half * HALF, (half + 1) * HALF)
         result = dot_t(hidden[at, :MAIN], down[...]) + dot_t(hidden[at, MAIN:], down_rest[...])
@@ -382,7 +383,7 @@
             jax.ShapeDtypeStruct((EXPERTS * BLOCK, columns // 2), BF16),
         ),
         in_specs=[hbm, hbm],
-        out_specs=(pl.BlockSpec(memory_space=pltpu.VMEM), hbm),
+        out_specs=(hbm, hbm),
         scratch_shapes=[
             pltpu.VMEM((SLOTS, WIDTH), BF16),
             pltpu.VMEM((2, WIDTH, MAIN), BF16),
@@ -391,9 +392,10 @@
             pltpu.VMEM((columns, MAIN), BF16),
             pltpu.VMEM((columns, REST), BF16),
             pltpu.VMEM((SLOTS, MAIN), F32),
+            pltpu.VMEM((SLOTS, HID), BF16),
             pltpu.VMEM((2, HALF * HALVES, columns // 2), BF16),
             pltpu.SemaphoreType.DMA((2 + 4 * N_DP,)),
-            pltpu.SemaphoreType.DMA((2,)),
+            pltpu.SemaphoreType.DMA((3,)),
         ],
         compiler_params=pltpu.CompilerParams(vmem_limit_bytes=VMEM_LIMIT),
         cost_estimate=pl.CostEstimate(
@@ -484,7 +486,7 @@
 
 
 TERMS = 2
-SHARE_ROWS = TERMS * HALVES * ROWS
+SHARE_ROWS = TERMS * ROWS
 
 
 def share_kernel(ids, weights, total, out, repeated, slots, terms):
@@ -507,15 +509,11 @@
     pick = (over_56(row) + at_group * GROUP == iota((EXPERTS, GROUP_ROWS), 0)).astype(BF16)
     lane = iota((ROWS, GROUP_ROWS), 1)
     slot_of = lane - over_28(lane) * CAPACITY
-    half_of = over_28(lane) - over_56(lane) * HALVES
     match = dot(slots[...], pick) == slot_of.astype(F32)
     shares = dot(terms[...], pick)
     for term in range(TERMS):
-        for half in range(HALVES):
-            at = (term * HALVES + half) * ROWS
-            out[at : at + ROWS, :] = jnp.where(
-                match & (half_of == half), shares[term * ROWS : (term + 1) * ROWS], 0.0
-            ).astype(BF16)
+        at = slice(term * ROWS, (term + 1) * ROWS)
+        out[at, :] = jnp.where(match, shares[at], 0.0).astype(BF16)
 
 
 def share_table(ids, weights, total):
@@ -569,16 +567,20 @@
         copies[g].start()
     for copy in later:
         copy.start()
-    step = HALVES * ROWS
+    row = iota((1, GROUP_ROWS), 1)
+    half_of = over_28(row) - over_56(row) * HALVES
+    masks = [(half_of == half).astype(BF16) for half in range(HALVES)]
     for g in range(GROUPS):
         share_copies[g].wait()
         copies[g].wait()
-        found = dot(
-            table[g * SHARE_ROWS : (g + 1) * SHARE_ROWS, :],
-            blocks[g * GROUP_ROWS : (g + 1) * GROUP_ROWS, :],
-        )
-        found = found[:step] + found[step:]
-        total[...] = found if g == 0 else total[...] + found
+        counts = table[g * SHARE_ROWS : (g + 1) * SHARE_ROWS, :]
+        counts = jnp.concatenate([counts * mask for mask in masks], axis=0)
+        found = dot(counts, blocks[g * GROUP_ROWS : (g + 1) * GROUP_ROWS, :])
+        for half in range(HALVES):
+            at = half * SHARE_ROWS
+            part = found[at : at + ROWS] + found[at + ROWS : at + SHARE_ROWS]
+            at = slice(half * ROWS, (half + 1) * ROWS)
+            total[at, :] = part if g == 0 else total[at, :] + part
     for copy in later:
         copy.wait()
 

time: 237 us -> 237 us (level)
  no operation moved by 1% of the time
where the time goes in v5:
time: 237 us; the launch traced here: 236 us
  waiting for transfers between devices  102 us (43%)
  Pallas kernels  65.4 us (28%)
  starting transfers between devices  49.2 us (21%)
  between operations  14.2 us (6%)
  local copies, waits for them, and re-layouts  2.82 us (1%)
  other arithmetic  2.65 us (1%)
    all_to_all x3, waiting for transfers between devices, exchanged(): lax.all_to_all(blocks.reshape(EXPERTS, rows // EXPERTS, columns), 'expert...  56.2 us
    all_to_all x3, starting transfers between devices, exchanged(): lax.all_to_all(blocks.reshape(EXPERTS, rows // EXPERTS, columns), 'expert...  22.7 us
    pallas_call x1, Pallas kernels, attention(): pl.pallas_call(attention_kernel, out_shape=(jax.ShapeDtypeStruct((ROWS, W...  17.9 us
    all_gather x1, waiting for transfers between devices, per_device(): second_gathered = lax.all_gather(second_shard, 'dp', axis=0, tiled=True)  16.3 us
    pallas_call x1, Pallas kernels, experts(): pl.pallas_call(expert_kernel, out_shape=(jax.ShapeDtypeStruct((SLOTS, HID...  16.1 us
    ppermute x3, waiting for transfers between devices, exchange_sum(): lax.ppermute(total, 'dp', [(at, at ^ bit) for at in range(N_DP)])  13.6 us
    ppermute x3, starting transfers between devices, exchange_sum(): lax.ppermute(total, 'dp', [(at, at ^ bit) for at in range(N_DP)])  11.2 us
    all_to_all x2, starting transfers between devices, between_chips(): lax.all_to_all(pieces, 'expert', split_axis=0, concat_axis=0, tiled=True,...  11.2 us
  transfers between devices with their start and end apart: 13, of which 11 were waited for; matrix products, arithmetic and copies ran while one was open for 2% of the time, Pallas kernels for 25%

profile of v5, /device:TPU:1, one launch (start us, length us, event | category | flops | bytes accessed | tf_op | source)
XLA Modules:
  0.0 236.0 jit_solution(8682032618939288105)
XLA Ops:
  9.7 3.3 %collective-permute-start = (bf16[512,2560]{1,0:T(8,128)(2,1)S(1)}, bf16[512,2560]{1,0:T(8,128)(2,1)}, u32[]{:S(2)}, u32[]{:S(2)}) collective-permute-start(bf16[512,2560]{1,0:T(8,128)(2,1)S(1)} %copy-done), channel_id=1, source_target_pairs={{0,1},{1,0},{2,3},{3,2},{4,5},{5,4},{6,7},{7,6},{8,9},{9,8},{10,11... | collective-permute-start | bytes 7864328 | tf_op jit(solution)/shard_map/ppermute | solution.py:643
  13.1 7.3 %collective-permute-done.far_keys = bf16[512,2560]{1,0:T(8,128)(2,1)} collective-permute-done((bf16[512,2560]{1,0:T(8,128)(2,1)S(1)}, bf16[512,2560]{1,0:T(8,128)(2,1)}, u32[]{:S(2)}, u32[]{:S(2)}) %collective-permute-start) | collective-permute-done | bytes 2621472 | tf_op jit(solution)/shard_map/ppermute | solution.py:643
  21.7 17.9 %shard_map.113 = (bf16[128,2560]{1,0:T(8,128)(2,1)}, bf16[128,2560]{1,0:T(8,128)(2,1)}) custom-call(s32[1]{0:T(128)} %bitcast.parity, bf16[256,2560]{1,0:T(8,128)(2,1)} %queries.1, bf16[512,2560]{1,0:T(8,128)(2,1)} %near_keys.1, bf16[512,2560]{1,0:T(8,128)(2,1)} %collective-permute-done.far_keys, bf16[512,2560]{1,0:T(8,128)(2,1)} %near_values.1, ...), custom_call_target="tpu_custom_call" | custom-call | flops 2684354560 | bytes 13000000 | tf_op jit(solution)/shard_map/pallas_call | solution.py:106
  39.6 5.0 %all-to-all-start = ((bf16[16,8,2560]{2,1,0:T(8,128)(2,1)}), bf16[16,8,2560]{2,1,0:T(8,128)(2,1)S(1)}, u32[]{:S(2)}, u32[]{:S(2)}) async-start(bf16[16,8,2560]{2,1,0:T(8,128)(2,1)} %bitcast.19), calls=%async_computation | async-start | bytes 1310720 | tf_op jit(solution)/shard_map/all_to_all | solution.py:647
  45.9 5.6 %shard_map.115 = bf16[1792,1280]{1,0:T(8,128)(2,1)} custom-call(bf16[128,2560]{1,0:T(8,128)(2,1)} %get-tuple-element.25.latents, f32[1,2560]{1,0:T(1,128)} %reshape.35.gain, s32[128,6]{1,0:T(8,128)} %copy.12.ids), custom_call_target="tpu_custom_call" | custom-call | flops 1200000000 | bytes 6000000 | tf_op jit(solution)/shard_map/pallas_call | solution.py:159
  51.5 4.5 %all-to-all-done = bf16[16,8,2560]{2,1,0:T(8,128)(2,1)S(1)} async-done(((bf16[16,8,2560]{2,1,0:T(8,128)(2,1)}), bf16[16,8,2560]{2,1,0:T(8,128)(2,1)S(1)}, u32[]{:S(2)}, u32[]{:S(2)}) %all-to-all-start) | async-done | bytes 655392 | tf_op jit(solution)/shard_map/all_to_all | solution.py:647
  56.2 6.8 %all-to-all-start.1 = ((bf16[32,56,1280]{2,1,0:T(8,128)(2,1)}), bf16[32,56,1280]{2,1,0:T(8,128)(2,1)}, u32[]{:S(2)}, u32[]{:S(2)}) async-start(bf16[32,56,1280]{2,1,0:T(8,128)(2,1)} %bitcast.14), calls=%async_computation.1 | async-start | bytes 9175040 | tf_op jit(solution)/shard_map/all_to_all | solution.py:677
  65.5 4.6 %collective-permute-done.2 = f32[8,2560]{1,0:T(8,128)S(1)} collective-permute-done((f32[8,2560]{1,0:T(8,128)S(1)}, f32[8,2560]{1,0:T(8,128)S(1)}, u32[]{:S(2)}, u32[]{:S(2)}) %collective-permute-start.2) | collective-permute-done | bytes 81952 | tf_op jit(solution)/shard_map/ppermute | solution.py:663
  70.1 3.0 %collective-permute-start.3 = (f32[8,2560]{1,0:T(8,128)S(1)}, f32[8,2560]{1,0:T(8,128)S(1)}, u32[]{:S(2)}, u32[]{:S(2)}) collective-permute-start(f32[8,2560]{1,0:T(8,128)S(1)} %add.15), channel_id=1, source_target_pairs={{0,64},{32,96},{64,0},{96,32},{128,192},{160,224},{192,128},{224,1... | collective-permute-start | bytes 245768 | tf_op jit(solution)/shard_map/ppermute | solution.py:663
  73.2 5.9 %collective-permute-done.3 = f32[8,2560]{1,0:T(8,128)S(1)} collective-permute-done((f32[8,2560]{1,0:T(8,128)S(1)}, f32[8,2560]{1,0:T(8,128)S(1)}, u32[]{:S(2)}, u32[]{:S(2)}) %collective-permute-start.3) | collective-permute-done | bytes 81952 | tf_op jit(solution)/shard_map/ppermute | solution.py:663
  79.0 6.4 %collective-permute-start.4 = (f32[8,2560]{1,0:T(8,128)S(1)}, f32[8,2560]{1,0:T(8,128)S(1)}, u32[]{:S(2)}, u32[]{:S(2)}) collective-permute-start(f32[8,2560]{1,0:T(8,128)S(1)} %add.16), channel_id=1, source_target_pairs={{0,128},{32,160},{64,192},{96,224},{128,0},{160,32},{192,64},{224,... | collective-permute-start | bytes 245768 | tf_op jit(solution)/shard_map/ppermute | solution.py:663
  86.9 3.1 %collective-permute-done.4 = f32[8,2560]{1,0:T(8,128)S(1)} collective-permute-done((f32[8,2560]{1,0:T(8,128)S(1)}, f32[8,2560]{1,0:T(8,128)S(1)}, u32[]{:S(2)}, u32[]{:S(2)}) %collective-permute-start.4) | collective-permute-done | bytes 81952 | tf_op jit(solution)/shard_map/ppermute | solution.py:663
  90.7 3.6 %shard_map.116 = (bf16[1024,448]{1,0:T(8,128)(2,1)}, bf16[16,8,2560]{2,1,0:T(8,128)(2,1)}) custom-call(s32[128,6]{1,0:T(8,128)} %copy.13.ids, f32[128,6]{1,0:T(8,128)} %copy.14.weights, f32[8,2560]{1,0:T(8,128)} %add.17.total), custom_call_target="tpu_custom_call" | custom-call | flops 50000000 | bytes 3000000 | tf_op jit(solution)/shard_map/pallas_call | solution.py:521
  94.2 25.7 %all-to-all-done.1 = bf16[32,56,1280]{2,1,0:T(8,128)(2,1)} async-done(((bf16[32,56,1280]{2,1,0:T(8,128)(2,1)}), bf16[32,56,1280]{2,1,0:T(8,128)(2,1)}, u32[]{:S(2)}, u32[]{:S(2)}) %all-to-all-start.1) | async-done | bytes 4587552 | tf_op jit(solution)/shard_map/all_to_all | solution.py:677
  120.0 5.1 %shard_map.117.rows = bf16[896,2560]{1,0:T(8,128)(2,1)} custom-call(bf16[1792,1280]{1,0:T(8,128)(2,1)} %bitcast.7.blocks), custom_call_target="tpu_custom_call" | custom-call | flops 1000000000 | bytes 9000000 | tf_op jit(solution)/shard_map/pallas_call | solution.py:202
  125.1 6.2 %all-to-all-start.2 = ((bf16[16,8,2560]{2,1,0:T(8,128)(2,1)}), bf16[16,8,2560]{2,1,0:T(8,128)(2,1)S(1)}, u32[]{:S(2)}, u32[]{:S(2)}) async-start(bf16[16,8,2560]{2,1,0:T(8,128)(2,1)} %get-tuple-element.39), calls=%async_computation.2 | async-start | bytes 1310720 | tf_op jit(solution)/shard_map/all_to_all | solution.py:647
  131.3 16.1 %shard_map.118 = (bf16[896,832]{1,0:T(8,128)(2,1)}, bf16[1792,512]{1,0:T(8,128)(2,1)}) custom-call(bf16[896,2560]{1,0:T(8,128)(2,1)} %shard_map.117.rows, bf16[6656,768]{1,0:T(8,128)(2,1)} %all-gather.3.cloned.1.call-done.gathered), custom_call_target="tpu_custom_call" | custom-call | flops 10000000000 | bytes 20000000 | tf_op jit(solution)/shard_map/pallas_call | solution.py:379
  147.4 8.5 %all-to-all-start.4 = ((bf16[32,56,512]{2,1,0:T(8,128)(2,1)}), bf16[32,56,512]{2,1,0:T(8,128)(2,1)}, u32[]{:S(2)}, u32[]{:S(2)}) async-start(bf16[32,56,512]{2,1,0:T(8,128)(2,1)} %bitcast.18), calls=%async_computation.4 | async-start | bytes 3670016 | tf_op jit(solution)/shard_map/all_to_all | solution.py:677
  155.9 16.3 %all-gather.5.cloned.1.call-done.gathered = bf16[1664,768]{1,0:T(8,128)(2,1)} async-done(((bf16[208,768]{1,0:T(8,128)(2,1)}), bf16[1664,768]{1,0:T(8,128)(2,1)}) %all-gather.5.cloned.1.call-update) | async-done | bytes 2555920 | tf_op jit(solution)/shard_map/all_gather | solution.py:710
  172.2 6.4 %shard_map.119 = bf16[1792,768]{1,0:T(8,128)(2,1)} custom-call(bf16[896,832]{1,0:T(8,128)(2,1)} %get-tuple-element.40.hidden, bf16[1664,768]{1,0:T(8,128)(2,1)} %all-gather.5.cloned.1.call-done.gathered), custom_call_target="tpu_custom_call" | custom-call | flops 3000000000 | bytes 8000000 | tf_op jit(solution)/shard_map/pallas_call | solution.py:467
  181.5 7.4 %all-to-all-start.3 = ((bf16[32,56,768]{2,1,0:T(8,128)(2,1)}), bf16[32,56,768]{2,1,0:T(8,128)(2,1)}, u32[]{:S(2)}, u32[]{:S(2)}) async-start(bf16[32,56,768]{2,1,0:T(8,128)(2,1)} %bitcast.15), calls=%async_computation.3 | async-start | bytes 5505024 | tf_op jit(solution)/shard_map/all_to_all | solution.py:677
  193.2 3.4 %shard_map.120.first = f32[128,1024]{1,0:T(8,128)} custom-call(bf16[1024,448]{1,0:T(8,128)(2,1)} %get-tuple-element.32.shares, bf16[1792,512]{1,0:T(8,128)(2,1)} %bitcast.12.returned), custom_call_target="tpu_custom_call" | custom-call | flops 1200000000 | bytes 4000000 | tf_op jit(solution)/shard_map/pallas_call | solution.py:626
  196.6 27.7 %all-to-all-done.3 = bf16[32,56,768]{2,1,0:T(8,128)(2,1)} async-done(((bf16[32,56,768]{2,1,0:T(8,128)(2,1)}), bf16[32,56,768]{2,1,0:T(8,128)(2,1)}, u32[]{:S(2)}, u32[]{:S(2)}) %all-to-all-start.3) | async-done | bytes 2752544 | tf_op jit(solution)/shard_map/all_to_all | solution.py:677
  224.2 4.9 %shard_map.121 = bf16[128,2560]{1,0:T(8,128)(2,1)} custom-call(bf16[1024,448]{1,0:T(8,128)(2,1)} %get-tuple-element.32.shares, bf16[1792,768]{1,0:T(8,128)(2,1)} %bitcast.10.returned, f32[128,1024]{1,0:T(8,128)} %shard_map.120.first, bf16[128,2560]{1,0:T(8,128)(2,1)} %get-tuple-element.25.latents), custom_call_target="tpu_custom_call" | custom-call | flops 1200000000 | bytes 4000000 | tf_op jit(solution)/shard_map/pallas_call | solution.py:626
  (31 shorter events, 17.1 us)
Async XLA Ops:
  7.2 2.5 %copy-start = (bf16[512,2560]{1,0:T(8,128)(2,1)S(1)}, bf16[512,2560]{1,0:T(8,128)(2,1)}, u32[]{:S(2)}) copy-start(bf16[512,2560]{1,0:T(8,128)(2,1)} %near_keys.1) | copy-start | bytes 7864324
  7.2 124.1 %all-gather.3.cloned.1.call-start = ((), (), s32[]{:S(2)}) async-start(), calls=%async_computation.5 | async-start | bytes 11501568 | tf_op jit(solution)/shard_map/all_gather | solution.py:706
  9.7 10.7 %collective-permute-start = (bf16[512,2560]{1,0:T(8,128)(2,1)S(1)}, bf16[512,2560]{1,0:T(8,128)(2,1)}, u32[]{:S(2)}, u32[]{:S(2)}) collective-permute-start(bf16[512,2560]{1,0:T(8,128)(2,1)S(1)} %copy-done), channel_id=1, source_target_pairs={{0,1},{1,0},{2,3},{3,2},{4,5},{5,4},{6,7},{7,6},{8,9},{9,8},{10,11... | collective-permute-start | bytes 7864328 | tf_op jit(solution)/shard_map/ppermute | solution.py:643
  13.0 8.6 %collective-permute-start.1 = (bf16[512,2560]{1,0:T(8,128)(2,1)}, bf16[512,2560]{1,0:T(8,128)(2,1)}, u32[]{:S(2)}, u32[]{:S(2)}) collective-permute-start(bf16[512,2560]{1,0:T(8,128)(2,1)} %near_values.1), channel_id=1, source_target_pairs={{0,1},{1,0},{2,3},{3,2},{4,5},{5,4},{6,7},{7,6},{8,9},{9,8},{10,11... | collective-permute-start | bytes 7864328 | tf_op jit(solution)/shard_map/ppermute | solution.py:643
  21.7 22.9 %copy-start.2 = (f32[2560]{0:T(1024)S(1)}, f32[2560]{0:T(1024)}, u32[]{:S(2)}) copy-start(f32[2560]{0:T(1024)} %param.13) | copy-start | bytes 30724
  21.7 23.5 %copy-start.1 = (s32[128,6]{0,1:T(8,128)S(1)}, s32[128,6]{0,1:T(8,128)}, u32[]{:S(2)}) copy-start(s32[128,6]{0,1:T(8,128)} %param.17) | copy-start | bytes 9220
  39.6 16.5 %all-to-all-start = ((bf16[16,8,2560]{2,1,0:T(8,128)(2,1)}), bf16[16,8,2560]{2,1,0:T(8,128)(2,1)S(1)}, u32[]{:S(2)}, u32[]{:S(2)}) async-start(bf16[16,8,2560]{2,1,0:T(8,128)(2,1)} %bitcast.19), calls=%async_computation | async-start | bytes 1310720 | tf_op jit(solution)/shard_map/all_to_all | solution.py:647
  56.1 29.3 %copy-start.3 = (f32[128,6]{0,1:T(8,128)S(1)}, f32[128,6]{0,1:T(8,128)}, u32[]{:S(2)}) copy-start(f32[128,6]{0,1:T(8,128)} %param.18) | copy-start | bytes 9220
  56.2 63.8 %all-to-all-start.1 = ((bf16[32,56,1280]{2,1,0:T(8,128)(2,1)}), bf16[32,56,1280]{2,1,0:T(8,128)(2,1)}, u32[]{:S(2)}, u32[]{:S(2)}) async-start(bf16[32,56,1280]{2,1,0:T(8,128)(2,1)} %bitcast.14), calls=%async_computation.1 | async-start | bytes 9175040 | tf_op jit(solution)/shard_map/all_to_all | solution.py:677
  63.0 109.2 %all-gather.5.cloned.1.call-start = ((), (), s32[]{:S(2)}) async-start(), calls=%async_computation.6 | async-start | bytes 2875392 | tf_op jit(solution)/shard_map/all_gather | solution.py:710
  63.8 6.4 %collective-permute-start.2 = (f32[8,2560]{1,0:T(8,128)S(1)}, f32[8,2560]{1,0:T(8,128)S(1)}, u32[]{:S(2)}, u32[]{:S(2)}) collective-permute-start(f32[8,2560]{1,0:T(8,128)S(1)} %convert_reduce_fusion), channel_id=1, source_target_pairs={{0,32},{32,0},{64,96},{96,64},{128,160},{160,128},{192,224},{224,1... | collective-permute-start | bytes 245768 | tf_op jit(solution)/shard_map/ppermute | solution.py:663
  70.1 8.9 %collective-permute-start.3 = (f32[8,2560]{1,0:T(8,128)S(1)}, f32[8,2560]{1,0:T(8,128)S(1)}, u32[]{:S(2)}, u32[]{:S(2)}) collective-permute-start(f32[8,2560]{1,0:T(8,128)S(1)} %add.15), channel_id=1, source_target_pairs={{0,64},{32,96},{64,0},{96,32},{128,192},{160,224},{192,128},{224,1... | collective-permute-start | bytes 245768 | tf_op jit(solution)/shard_map/ppermute | solution.py:663
  79.0 11.0 %collective-permute-start.4 = (f32[8,2560]{1,0:T(8,128)S(1)}, f32[8,2560]{1,0:T(8,128)S(1)}, u32[]{:S(2)}, u32[]{:S(2)}) collective-permute-start(f32[8,2560]{1,0:T(8,128)S(1)} %add.16), channel_id=1, source_target_pairs={{0,128},{32,160},{64,192},{96,224},{128,0},{160,32},{192,64},{224,... | collective-permute-start | bytes 245768 | tf_op jit(solution)/shard_map/ppermute | solution.py:663
  125.1 22.4 %all-to-all-start.2 = ((bf16[16,8,2560]{2,1,0:T(8,128)(2,1)}), bf16[16,8,2560]{2,1,0:T(8,128)(2,1)S(1)}, u32[]{:S(2)}, u32[]{:S(2)}) async-start(bf16[16,8,2560]{2,1,0:T(8,128)(2,1)} %get-tuple-element.39), calls=%async_computation.2 | async-start | bytes 1310720 | tf_op jit(solution)/shard_map/all_to_all | solution.py:647
  147.4 34.0 %all-to-all-start.4 = ((bf16[32,56,512]{2,1,0:T(8,128)(2,1)}), bf16[32,56,512]{2,1,0:T(8,128)(2,1)}, u32[]{:S(2)}, u32[]{:S(2)}) async-start(bf16[32,56,512]{2,1,0:T(8,128)(2,1)} %bitcast.18), calls=%async_computation.4 | async-start | bytes 3670016 | tf_op jit(solution)/shard_map/all_to_all | solution.py:677
  181.5 42.8 %all-to-all-start.3 = ((bf16[32,56,768]{2,1,0:T(8,128)(2,1)}), bf16[32,56,768]{2,1,0:T(8,128)(2,1)}, u32[]{:S(2)}, u32[]{:S(2)}) async-start(bf16[32,56,768]{2,1,0:T(8,128)(2,1)} %bitcast.15), calls=%async_computation.3 | async-start | bytes 5505024 | tf_op jit(solution)/shard_map/all_to_all | solution.py:677
  188.9 2.4 %collective-permute-start.5 = (bf16[128,2560]{1,0:T(8,128)(2,1)S(1)}, bf16[128,2560]{1,0:T(8,128)(2,1)S(1)}, u32[]{:S(2)}, u32[]{:S(2)}) collective-permute-start(bf16[128,2560]{1,0:T(8,128)(2,1)S(1)} %bitcast.16), channel_id=1, source_target_pairs={{0,1},{1,0},{2,3},{3,2},{4,5},{5,4},{6,7},{7,6},{8,9},{9,8},{10,11... | collective-permute-start | bytes 1966088 | tf_op jit(solution)/shard_map/ppermute | solution.py:643
Sparse Core Ops, SparseCore 0:
  10.4 120.3 all-gather.2
  132.6 39.5 all-gather.4

commit v6 on v5

--- a/solution.py
+++ b/solution.py
@@ -612,6 +612,7 @@
 def mixed(shares, returned, *last):
     width = returned.shape[1]
     hbm = pl.BlockSpec(memory_space=pltpu.HBM)
+    early = pl.BlockSpec(memory_space=pl.ANY) if last else hbm
     out, kernel = jax.ShapeDtypeStruct((ROWS, 2 * width), F32), mix_kernel
     scratch = [
         pltpu.VMEM(shares.shape, BF16),
@@ -625,11 +626,11 @@
         scratch += [pltpu.SemaphoreType.DMA((2,))]
     return pl.pallas_call(
         kernel,
-        in_specs=[hbm] * (2 + len(last)),
+        in_specs=[early, hbm] + [early] * len(last),
         out_shape=out,
         out_specs=pl.BlockSpec(memory_space=pltpu.VMEM),
         scratch_shapes=scratch,
-        compiler_params=pltpu.CompilerParams(vmem_limit_bytes=63 * 1024 * 1024),
+        compiler_params=pltpu.CompilerParams(vmem_limit_bytes=(24 if last else 63) * 1024 * 1024),
         cost_estimate=pl.CostEstimate(
             flops=1_200_000_000, bytes_accessed=4_000_000, transcendentals=0
         ),

time: 237 us -> 239 us (level)
  transfers between devices with their start and end apart: 13 -> 13, of which waited for: 11 -> 11; matrix products, arithmetic and copies ran while one was open for 2% -> 2% of each run, Pallas kernels for 25% -> 24%
where the time goes in v6:
time: 239 us; the launch traced here: 238 us
  waiting for transfers between devices  102 us (43%)
  Pallas kernels  65.4 us (27%)
  starting transfers between devices  49.2 us (21%)
  between operations  14.2 us (6%)
  local copies, waits for them, and re-layouts  5.07 us (2%)
  other arithmetic  2.63 us (1%)
    all_to_all x3, waiting for transfers between devices, exchanged(): lax.all_to_all(blocks.reshape(EXPERTS, rows // EXPERTS, columns), 'expert...  56.2 us
    all_to_all x3, starting transfers between devices, exchanged(): lax.all_to_all(blocks.reshape(EXPERTS, rows // EXPERTS, columns), 'expert...  22.7 us
    pallas_call x1, Pallas kernels, attention(): pl.pallas_call(attention_kernel, out_shape=(jax.ShapeDtypeStruct((ROWS, W...  17.9 us
    all_gather x1, waiting for transfers between devices, per_device(): second_gathered = lax.all_gather(second_shard, 'dp', axis=0, tiled=True)  16.3 us
    pallas_call x1, Pallas kernels, experts(): pl.pallas_call(expert_kernel, out_shape=(jax.ShapeDtypeStruct((SLOTS, HID...  16.1 us
    ppermute x3, waiting for transfers between devices, exchange_sum(): lax.ppermute(total, 'dp', [(at, at ^ bit) for at in range(N_DP)])  13.6 us
    ppermute x3, starting transfers between devices, exchange_sum(): lax.ppermute(total, 'dp', [(at, at ^ bit) for at in range(N_DP)])  11.2 us
    all_to_all x2, starting transfers between devices, between_chips(): lax.all_to_all(pieces, 'expert', split_axis=0, concat_axis=0, tiled=True,...  11.2 us
  transfers between devices with their start and end apart: 13, of which 11 were waited for; matrix products, arithmetic and copies ran while one was open for 2% of the time, Pallas kernels for 24%

profile of v6, /device:TPU:1, one launch (start us, length us, event | category | flops | bytes accessed | tf_op | source)
XLA Modules:
  0.0 238.2 jit_solution(3020517049601859238)
XLA Ops:
  9.7 3.3 %collective-permute-start = (bf16[512,2560]{1,0:T(8,128)(2,1)S(1)}, bf16[512,2560]{1,0:T(8,128)(2,1)}, u32[]{:S(2)}, u32[]{:S(2)}) collective-permute-start(bf16[512,2560]{1,0:T(8,128)(2,1)S(1)} %copy-done.3), channel_id=1, source_target_pairs={{0,1},{1,0},{2,3},{3,2},{4,5},{5,4},{6,7},{7,6},{8,9},{9,8},{10,11... | collective-permute-start | bytes 7864328 | tf_op jit(solution)/shard_map/ppermute | solution.py:644
  13.1 7.3 %collective-permute-done.far_keys = bf16[512,2560]{1,0:T(8,128)(2,1)} collective-permute-done((bf16[512,2560]{1,0:T(8,128)(2,1)S(1)}, bf16[512,2560]{1,0:T(8,128)(2,1)}, u32[]{:S(2)}, u32[]{:S(2)}) %collective-permute-start) | collective-permute-done | bytes 2621472 | tf_op jit(solution)/shard_map/ppermute | solution.py:644
  21.7 17.9 %shard_map.113 = (bf16[128,2560]{1,0:T(8,128)(2,1)}, bf16[128,2560]{1,0:T(8,128)(2,1)}) custom-call(s32[1]{0:T(128)} %bitcast.parity, bf16[256,2560]{1,0:T(8,128)(2,1)} %queries.1, bf16[512,2560]{1,0:T(8,128)(2,1)} %near_keys.1, bf16[512,2560]{1,0:T(8,128)(2,1)} %collective-permute-done.far_keys, bf16[512,2560]{1,0:T(8,128)(2,1)} %near_values.1, ...), custom_call_target="tpu_custom_call" | custom-call | flops 2684354560 | bytes 13000000 | tf_op jit(solution)/shard_map/pallas_call | solution.py:106
  39.6 5.0 %all-to-all-start = ((bf16[16,8,2560]{2,1,0:T(8,128)(2,1)}), bf16[16,8,2560]{2,1,0:T(8,128)(2,1)S(1)}, u32[]{:S(2)}, u32[]{:S(2)}) async-start(bf16[16,8,2560]{2,1,0:T(8,128)(2,1)} %bitcast.19), calls=%async_computation | async-start | bytes 1310720 | tf_op jit(solution)/shard_map/all_to_all | solution.py:648
  46.0 5.6 %shard_map.115 = bf16[1792,1280]{1,0:T(8,128)(2,1)} custom-call(bf16[128,2560]{1,0:T(8,128)(2,1)} %get-tuple-element.25.latents, f32[1,2560]{1,0:T(1,128)} %reshape.35.gain, s32[128,6]{1,0:T(8,128)} %copy.12.ids), custom_call_target="tpu_custom_call" | custom-call | flops 1200000000 | bytes 6000000 | tf_op jit(solution)/shard_map/pallas_call | solution.py:159
  51.5 4.6 %all-to-all-done = bf16[16,8,2560]{2,1,0:T(8,128)(2,1)S(1)} async-done(((bf16[16,8,2560]{2,1,0:T(8,128)(2,1)}), bf16[16,8,2560]{2,1,0:T(8,128)(2,1)S(1)}, u32[]{:S(2)}, u32[]{:S(2)}) %all-to-all-start) | async-done | bytes 655392 | tf_op jit(solution)/shard_map/all_to_all | solution.py:648
  56.2 6.8 %all-to-all-start.1 = ((bf16[32,56,1280]{2,1,0:T(8,128)(2,1)}), bf16[32,56,1280]{2,1,0:T(8,128)(2,1)}, u32[]{:S(2)}, u32[]{:S(2)}) async-start(bf16[32,56,1280]{2,1,0:T(8,128)(2,1)} %bitcast.14), calls=%async_computation.1 | async-start | bytes 9175040 | tf_op jit(solution)/shard_map/all_to_all | solution.py:678
  65.5 4.6 %collective-permute-done.2 = f32[8,2560]{1,0:T(8,128)S(1)} collective-permute-done((f32[8,2560]{1,0:T(8,128)S(1)}, f32[8,2560]{1,0:T(8,128)S(1)}, u32[]{:S(2)}, u32[]{:S(2)}) %collective-permute-start.2) | collective-permute-done | bytes 81952 | tf_op jit(solution)/shard_map/ppermute | solution.py:664
  70.2 3.0 %collective-permute-start.3 = (f32[8,2560]{1,0:T(8,128)S(1)}, f32[8,2560]{1,0:T(8,128)S(1)}, u32[]{:S(2)}, u32[]{:S(2)}) collective-permute-start(f32[8,2560]{1,0:T(8,128)S(1)} %add.15), channel_id=1, source_target_pairs={{0,64},{32,96},{64,0},{96,32},{128,192},{160,224},{192,128},{224,1... | collective-permute-start | bytes 245768 | tf_op jit(solution)/shard_map/ppermute | solution.py:664
  73.2 5.9 %collective-permute-done.3 = f32[8,2560]{1,0:T(8,128)S(1)} collective-permute-done((f32[8,2560]{1,0:T(8,128)S(1)}, f32[8,2560]{1,0:T(8,128)S(1)}, u32[]{:S(2)}, u32[]{:S(2)}) %collective-permute-start.3) | collective-permute-done | bytes 81952 | tf_op jit(solution)/shard_map/ppermute | solution.py:664
  79.1 6.5 %collective-permute-start.4 = (f32[8,2560]{1,0:T(8,128)S(1)}, f32[8,2560]{1,0:T(8,128)S(1)}, u32[]{:S(2)}, u32[]{:S(2)}) collective-permute-start(f32[8,2560]{1,0:T(8,128)S(1)} %add.16), channel_id=1, source_target_pairs={{0,128},{32,160},{64,192},{96,224},{128,0},{160,32},{192,64},{224,... | collective-permute-start | bytes 245768 | tf_op jit(solution)/shard_map/ppermute | solution.py:664
  87.0 3.1 %collective-permute-done.4 = f32[8,2560]{1,0:T(8,128)S(1)} collective-permute-done((f32[8,2560]{1,0:T(8,128)S(1)}, f32[8,2560]{1,0:T(8,128)S(1)}, u32[]{:S(2)}, u32[]{:S(2)}) %collective-permute-start.4) | collective-permute-done | bytes 81952 | tf_op jit(solution)/shard_map/ppermute | solution.py:664
  90.7 3.6 %shard_map.116 = (bf16[1024,448]{1,0:T(8,128)(2,1)}, bf16[16,8,2560]{2,1,0:T(8,128)(2,1)}) custom-call(s32[128,6]{1,0:T(8,128)} %copy.13.ids, f32[128,6]{1,0:T(8,128)} %copy.14.weights, f32[8,2560]{1,0:T(8,128)} %add.17.total), custom_call_target="tpu_custom_call" | custom-call | flops 50000000 | bytes 3000000 | tf_op jit(solution)/shard_map/pallas_call | solution.py:521
  94.2 25.8 %all-to-all-done.1 = bf16[32,56,1280]{2,1,0:T(8,128)(2,1)} async-done(((bf16[32,56,1280]{2,1,0:T(8,128)(2,1)}), bf16[32,56,1280]{2,1,0:T(8,128)(2,1)}, u32[]{:S(2)}, u32[]{:S(2)}) %all-to-all-start.1) | async-done | bytes 4587552 | tf_op jit(solution)/shard_map/all_to_all | solution.py:678
  120.0 5.1 %shard_map.117.rows = bf16[896,2560]{1,0:T(8,128)(2,1)} custom-call(bf16[1792,1280]{1,0:T(8,128)(2,1)} %bitcast.7.blocks), custom_call_target="tpu_custom_call" | custom-call | flops 1000000000 | bytes 9000000 | tf_op jit(solution)/shard_map/pallas_call | solution.py:202
  125.1 6.2 %all-to-all-start.2 = ((bf16[16,8,2560]{2,1,0:T(8,128)(2,1)}), bf16[16,8,2560]{2,1,0:T(8,128)(2,1)S(1)}, u32[]{:S(2)}, u32[]{:S(2)}) async-start(bf16[16,8,2560]{2,1,0:T(8,128)(2,1)} %get-tuple-element.39), calls=%async_computation.2 | async-start | bytes 1310720 | tf_op jit(solution)/shard_map/all_to_all | solution.py:648
  131.3 16.1 %shard_map.118 = (bf16[896,832]{1,0:T(8,128)(2,1)}, bf16[1792,512]{1,0:T(8,128)(2,1)}) custom-call(bf16[896,2560]{1,0:T(8,128)(2,1)} %shard_map.117.rows, bf16[6656,768]{1,0:T(8,128)(2,1)} %all-gather.3.cloned.1.call-done.gathered), custom_call_target="tpu_custom_call" | custom-call | flops 10000000000 | bytes 20000000 | tf_op jit(solution)/shard_map/pallas_call | solution.py:379
  147.5 8.5 %all-to-all-start.4 = ((bf16[32,56,512]{2,1,0:T(8,128)(2,1)}), bf16[32,56,512]{2,1,0:T(8,128)(2,1)}, u32[]{:S(2)}, u32[]{:S(2)}) async-start(bf16[32,56,512]{2,1,0:T(8,128)(2,1)} %bitcast.18), calls=%async_computation.4 | async-start | bytes 3670016 | tf_op jit(solution)/shard_map/all_to_all | solution.py:678
  155.9 16.3 %all-gather.5.cloned.1.call-done.gathered = bf16[1664,768]{1,0:T(8,128)(2,1)} async-done(((bf16[208,768]{1,0:T(8,128)(2,1)}), bf16[1664,768]{1,0:T(8,128)(2,1)}) %all-gather.5.cloned.1.call-update) | async-done | bytes 2555920 | tf_op jit(solution)/shard_map/all_gather | solution.py:711
  172.2 6.4 %shard_map.119 = bf16[1792,768]{1,0:T(8,128)(2,1)} custom-call(bf16[896,832]{1,0:T(8,128)(2,1)} %get-tuple-element.40.hidden, bf16[1664,768]{1,0:T(8,128)(2,1)} %all-gather.5.cloned.1.call-done.gathered), custom_call_target="tpu_custom_call" | custom-call | flops 3000000000 | bytes 8000000 | tf_op jit(solution)/shard_map/pallas_call | solution.py:467
  181.5 7.4 %all-to-all-start.3 = ((bf16[32,56,768]{2,1,0:T(8,128)(2,1)}), bf16[32,56,768]{2,1,0:T(8,128)(2,1)}, u32[]{:S(2)}, u32[]{:S(2)}) async-start(bf16[32,56,768]{2,1,0:T(8,128)(2,1)} %bitcast.15), calls=%async_computation.3 | async-start | bytes 5505024 | tf_op jit(solution)/shard_map/all_to_all | solution.py:678
  193.2 3.4 %shard_map.120.first = f32[128,1024]{1,0:T(8,128)} custom-call(bf16[1024,448]{1,0:T(8,128)(2,1)} %get-tuple-element.32.shares, bf16[1792,512]{1,0:T(8,128)(2,1)} %bitcast.12.returned), custom_call_target="tpu_custom_call" | custom-call | flops 1200000000 | bytes 4000000 | tf_op jit(solution)/shard_map/pallas_call | solution.py:627
  196.7 27.6 %all-to-all-done.3 = bf16[32,56,768]{2,1,0:T(8,128)(2,1)} async-done(((bf16[32,56,768]{2,1,0:T(8,128)(2,1)}), bf16[32,56,768]{2,1,0:T(8,128)(2,1)}, u32[]{:S(2)}, u32[]{:S(2)}) %all-to-all-start.3) | async-done | bytes 2752544 | tf_op jit(solution)/shard_map/all_to_all | solution.py:678
  226.6 4.8 %shard_map.121 = bf16[128,2560]{1,0:T(8,128)(2,1)} custom-call(bf16[1024,448]{1,0:T(8,128)(2,1)S(1)} %copy-done.1, bf16[1792,768]{1,0:T(8,128)(2,1)} %bitcast.10.returned, f32[128,1024]{1,0:T(8,128)S(1)} %copy-done.2, bf16[128,2560]{1,0:T(8,128)(2,1)S(1)} %copy-done), custom_call_target="tpu_custom_call" | custom-call | flops 1200000000 | bytes 4000000 | tf_op jit(solution)/shard_map/pallas_call | solution.py:627
  (37 shorter events, 19.3 us)
Async XLA Ops:
  7.2 2.5 %copy-start.3 = (bf16[512,2560]{1,0:T(8,128)(2,1)S(1)}, bf16[512,2560]{1,0:T(8,128)(2,1)}, u32[]{:S(2)}) copy-start(bf16[512,2560]{1,0:T(8,128)(2,1)} %near_keys.1) | copy-start | bytes 7864324
  7.2 124.1 %all-gather.3.cloned.1.call-start = ((), (), s32[]{:S(2)}) async-start(), calls=%async_computation.5 | async-start | bytes 11501568 | tf_op jit(solution)/shard_map/all_gather | solution.py:707
  9.7 10.7 %collective-permute-start = (bf16[512,2560]{1,0:T(8,128)(2,1)S(1)}, bf16[512,2560]{1,0:T(8,128)(2,1)}, u32[]{:S(2)}, u32[]{:S(2)}) collective-permute-start(bf16[512,2560]{1,0:T(8,128)(2,1)S(1)} %copy-done.3), channel_id=1, source_target_pairs={{0,1},{1,0},{2,3},{3,2},{4,5},{5,4},{6,7},{7,6},{8,9},{9,8},{10,11... | collective-permute-start | bytes 7864328 | tf_op jit(solution)/shard_map/ppermute | solution.py:644
  13.0 8.6 %collective-permute-start.1 = (bf16[512,2560]{1,0:T(8,128)(2,1)}, bf16[512,2560]{1,0:T(8,128)(2,1)}, u32[]{:S(2)}, u32[]{:S(2)}) collective-permute-start(bf16[512,2560]{1,0:T(8,128)(2,1)} %near_values.1), channel_id=1, source_target_pairs={{0,1},{1,0},{2,3},{3,2},{4,5},{5,4},{6,7},{7,6},{8,9},{9,8},{10,11... | collective-permute-start | bytes 7864328 | tf_op jit(solution)/shard_map/ppermute | solution.py:644
  21.7 22.9 %copy-start.5 = (f32[2560]{0:T(1024)S(1)}, f32[2560]{0:T(1024)}, u32[]{:S(2)}) copy-start(f32[2560]{0:T(1024)} %param.13) | copy-start | bytes 30724
  21.7 23.6 %copy-start.4 = (s32[128,6]{0,1:T(8,128)S(1)}, s32[128,6]{0,1:T(8,128)}, u32[]{:S(2)}) copy-start(s32[128,6]{0,1:T(8,128)} %param.17) | copy-start | bytes 9220
  39.6 16.5 %all-to-all-start = ((bf16[16,8,2560]{2,1,0:T(8,128)(2,1)}), bf16[16,8,2560]{2,1,0:T(8,128)(2,1)S(1)}, u32[]{:S(2)}, u32[]{:S(2)}) async-start(bf16[16,8,2560]{2,1,0:T(8,128)(2,1)} %bitcast.19), calls=%async_computation | async-start | bytes 1310720 | tf_op jit(solution)/shard_map/all_to_all | solution.py:648
  56.2 29.3 %copy-start.6 = (f32[128,6]{0,1:T(8,128)S(1)}, f32[128,6]{0,1:T(8,128)}, u32[]{:S(2)}) copy-start(f32[128,6]{0,1:T(8,128)} %param.18) | copy-start | bytes 9220
  56.2 63.8 %all-to-all-start.1 = ((bf16[32,56,1280]{2,1,0:T(8,128)(2,1)}), bf16[32,56,1280]{2,1,0:T(8,128)(2,1)}, u32[]{:S(2)}, u32[]{:S(2)}) async-start(bf16[32,56,1280]{2,1,0:T(8,128)(2,1)} %bitcast.14), calls=%async_computation.1 | async-start | bytes 9175040 | tf_op jit(solution)/shard_map/all_to_all | solution.py:678
  63.0 109.2 %all-gather.5.cloned.1.call-start = ((), (), s32[]{:S(2)}) async-start(), calls=%async_computation.6 | async-start | bytes 2875392 | tf_op jit(solution)/shard_map/all_gather | solution.py:711
  63.8 6.4 %collective-permute-start.2 = (f32[8,2560]{1,0:T(8,128)S(1)}, f32[8,2560]{1,0:T(8,128)S(1)}, u32[]{:S(2)}, u32[]{:S(2)}) collective-permute-start(f32[8,2560]{1,0:T(8,128)S(1)} %convert_reduce_fusion), channel_id=1, source_target_pairs={{0,32},{32,0},{64,96},{96,64},{128,160},{160,128},{192,224},{224,1... | collective-permute-start | bytes 245768 | tf_op jit(solution)/shard_map/ppermute | solution.py:664
  70.2 8.9 %collective-permute-start.3 = (f32[8,2560]{1,0:T(8,128)S(1)}, f32[8,2560]{1,0:T(8,128)S(1)}, u32[]{:S(2)}, u32[]{:S(2)}) collective-permute-start(f32[8,2560]{1,0:T(8,128)S(1)} %add.15), channel_id=1, source_target_pairs={{0,64},{32,96},{64,0},{96,32},{128,192},{160,224},{192,128},{224,1... | collective-permute-start | bytes 245768 | tf_op jit(solution)/shard_map/ppermute | solution.py:664
  79.1 11.0 %collective-permute-start.4 = (f32[8,2560]{1,0:T(8,128)S(1)}, f32[8,2560]{1,0:T(8,128)S(1)}, u32[]{:S(2)}, u32[]{:S(2)}) collective-permute-start(f32[8,2560]{1,0:T(8,128)S(1)} %add.16), channel_id=1, source_target_pairs={{0,128},{32,160},{64,192},{96,224},{128,0},{160,32},{192,64},{224,... | collective-permute-start | bytes 245768 | tf_op jit(solution)/shard_map/ppermute | solution.py:664
  125.1 22.4 %all-to-all-start.2 = ((bf16[16,8,2560]{2,1,0:T(8,128)(2,1)}), bf16[16,8,2560]{2,1,0:T(8,128)(2,1)S(1)}, u32[]{:S(2)}, u32[]{:S(2)}) async-start(bf16[16,8,2560]{2,1,0:T(8,128)(2,1)} %get-tuple-element.39), calls=%async_computation.2 | async-start | bytes 1310720 | tf_op jit(solution)/shard_map/all_to_all | solution.py:648
  147.5 34.0 %all-to-all-start.4 = ((bf16[32,56,512]{2,1,0:T(8,128)(2,1)}), bf16[32,56,512]{2,1,0:T(8,128)(2,1)}, u32[]{:S(2)}, u32[]{:S(2)}) async-start(bf16[32,56,512]{2,1,0:T(8,128)(2,1)} %bitcast.18), calls=%async_computation.4 | async-start | bytes 3670016 | tf_op jit(solution)/shard_map/all_to_all | solution.py:678
  181.5 42.8 %all-to-all-start.3 = ((bf16[32,56,768]{2,1,0:T(8,128)(2,1)}), bf16[32,56,768]{2,1,0:T(8,128)(2,1)}, u32[]{:S(2)}, u32[]{:S(2)}) async-start(bf16[32,56,768]{2,1,0:T(8,128)(2,1)} %bitcast.15), calls=%async_computation.3 | async-start | bytes 5505024 | tf_op jit(solution)/shard_map/all_to_all | solution.py:678
  188.9 2.4 %collective-permute-start.5 = (bf16[128,2560]{1,0:T(8,128)(2,1)S(1)}, bf16[128,2560]{1,0:T(8,128)(2,1)S(1)}, u32[]{:S(2)}, u32[]{:S(2)}) collective-permute-start(bf16[128,2560]{1,0:T(8,128)(2,1)S(1)} %bitcast.16), channel_id=1, source_target_pairs={{0,1},{1,0},{2,3},{3,2},{4,5},{5,4},{6,7},{7,6},{8,9},{9,8},{10,11... | collective-permute-start | bytes 1966088 | tf_op jit(solution)/shard_map/ppermute | solution.py:644
  193.2 31.1 %copy-start = (bf16[128,2560]{1,0:T(8,128)(2,1)S(1)}, bf16[128,2560]{1,0:T(8,128)(2,1)}, u32[]{:S(2)}) copy-start(bf16[128,2560]{1,0:T(8,128)(2,1)} %get-tuple-element.25.latents) | copy-start | bytes 1966084
  224.3 1.2 copy-start.1
  225.5 1.0 copy-start.2
Sparse Core Ops, SparseCore 0:
  10.4 120.3 all-gather.2
  132.6 39.5 all-gather.4
